TPU v7x, 32 devices: a whole 2x2x4 slice. The times are simulated.
32 devices in a mesh: replica: 8 (over z, y), shard: 4 (over x, core).
Axes of the slice: x: 2, y: 2, z: 4, core: 2. Of those that a mesh axis runs over, the one named last changes fastest.
Arguments:
- features: bfloat16 [2048, 4096], P('replica', 'shard'), may hold values from -6 to 6
- weight: bfloat16 [128, 1024, 128], P('shard'), may hold values from -0.1875 to 0.1875
- rows_index: int32 [128, 8], replicated, may hold values from 0 to 31, as said below
- cotangent: bfloat16 [2048, 16384], P('replica', 'shard'), may hold values from -6 to 6
Outputs:
- activated: bfloat16 [2048, 16384], P('replica', 'shard')
- input_grad: bfloat16 [2048, 4096], P('replica', 'shard')
- weight_grad: float32 [128, 1024, 128], P('shard', 'replica')
Inputs may be any that keep to these rules, and one draw needn't show every extreme that they name: `rows_index`: each block column lists 8 different block rows.
All inputs are finite; a program needn't handle non-finite values.
Results may differ from a plain program's by a relative error of at most 0.02.
Values may be sent and summed in bfloat16 or wider, within the bound.
No kernel may reach another device: no remote copies, remote signals or barrier semaphores. Data moves between devices by JAX's collectives and lax.ppermute only.
A program may use at most 128 MiB of HBM per device.

v0:
```python
import math

import jax
import jax.numpy as jnp
from jax import lax
from jax.sharding import PartitionSpec as P


def local(features, weight, rows_index, cotangent):
    tokens_here = features.shape[0]
    side = weight.shape[2]
    columns = weight.shape[0]
    per_column = weight.shape[1] // side
    scale = 1.0 / math.sqrt(tokens_here * lax.axis_size("replica"))
    whole = lax.all_gather(features, "shard", axis=1, tiled=True)
    block_rows = whole.shape[1] // side
    blocks = whole.reshape(tokens_here, block_rows, side)
    first = lax.axis_index("shard") * columns
    local_rows = lax.dynamic_slice_in_dim(rows_index, first, columns, 0)
    selected_rows = blocks[:, local_rows]
    block_weight_tiles = weight.reshape(columns, per_column, side, side)
    preactivation = jnp.einsum(
        "defv,efvp->dep", selected_rows, block_weight_tiles, preferred_element_type=jnp.float32
    )
    sig = jax.nn.sigmoid(preactivation)
    activated = (preactivation * sig).astype(jnp.bfloat16).reshape(tokens_here, columns * side)
    slope = (
        cotangent.astype(jnp.float32).reshape(tokens_here, columns, side)
        * sig
        * (1.0 + preactivation * (1.0 - sig))
    )
    output_difference = slope.astype(jnp.bfloat16)
    backward_result = jnp.einsum(
        "iov,omgv->iomg", output_difference, block_weight_tiles, preferred_element_type=jnp.float32
    )
    positions = jnp.arange(block_rows, dtype=jnp.int32)
    onehot = (local_rows[:, :, None] == positions[None, None, :]).astype(jnp.float32)
    partial_value = jnp.einsum("tckr,ckb->tbr", backward_result, onehot).reshape(
        tokens_here, block_rows * side
    )
    input_grad = lax.psum_scatter(
        partial_value.astype(jnp.bfloat16), "shard", scatter_dimension=1, tiled=True
    )
    shard_gradient = jnp.einsum(
        "qlpf,qlx->lpfx", selected_rows, output_difference, preferred_element_type=jnp.float32
    )
    shard_gradient = shard_gradient.reshape(columns, per_column * side, side)
    weight_grad = (
        lax.psum_scatter(shard_gradient, "replica", scatter_dimension=1, tiled=True) * scale
    )
    return (activated, input_grad, weight_grad)


def solution(mesh):
    placed = (P("replica", "shard"), P("shard", None, None), P(), P("replica", "shard"))
    return jax.shard_map(
        local,
        mesh=mesh,
        in_specs=placed,
        out_specs=(P("replica", "shard"), P("replica", "shard"), P("shard", "replica", None)),
        check_vma=False,
    )
```

profile of v0, /device:TPU:0, one launch (start us, length us, event | category | flops | bytes accessed | tf_op | source)
XLA Modules:
  0.0 423.0 jit_solution(7188287947407827727)
XLA Ops:
  7.2 0.0 all-gather.2.cloned.1.call-start
  7.2 2.0 copy.20
  9.3 0.0 all-gather.2.cloned.1.call-update
  9.3 0.0 reduce-scatter.5.cloned.1.call-start
  9.3 0.8 compare_select_fusion
  10.1 0.1 copy.21
  10.2 0.1 reshape.37
  10.3 4.3 %copy.26 = f32[256,4096]{0,1:T(8,128)} copy(bf16[256,4096]{1,0:T(8,128)(2,1)} %param.7) | data formatting | bytes 6291456 | tf_op jit(solution)/shard_map/reshape | solution.py:28
  14.6 20.8 %all-gather.2.cloned.1.call-done = bf16[256,4096]{0,1:T(8,128)(2,1)} async-done(((bf16[256,1024]{0,1:T(8,128)(2,1)}), bf16[256,4096]{0,1:T(8,128)(2,1)}) %all-gather.2.cloned.1.call-update) | async-done | bytes 2097168 | tf_op jit(solution)/shard_map/all_gather | solution.py:15
  35.5 3.2 copy.22
  38.7 9.7 %gather_fusion = bf16[256,256,128]{2,1,0:T(8,128)(2,1)} fusion(bf16[256,32,128]{2,0,1:T(8,128)(2,1)S(1)} %copy.22, s32[1024]{0:T(1024)S(1)} %pad_clamp_fusion), kind=kCustom, calls=%fused_computation | custom fusion | bytes 33555456 | tf_op jit(solution)/shard_map/gather | solution.py:20
  48.4 22.6 %copy.23 = bf16[32,8,256,128]{2,3,1,0:T(8,128)(2,1)} copy(bf16[32,8,256,128]{3,2,1,0:T(8,128)(2,1)} %bitcast.61) | data formatting | bytes 33554432 | tf_op jit(solution)/shard_map/gather | solution.py:20
  71.0 13.6 %fusion.10 = (bf16[256,32,128]{0,2,1:T(8,128)(2,1)S(1)}, bf16[256,32,128]{0,2,1:T(8,128)(2,1)}) fusion(f32[256,32,128]{0,2,1:T(8,128)} %bitcast.66, bf16[256,32,8,128]{3,0,2,1:T(8,128)(2,1)} %bitcast.62, bf16[32,8,128,128]{3,2,1,0:T(8,128)(2,1)} %bitcast.63), kind=kOutput, calls=%fused_computation.16 | convolution fusion | flops 2159017984 | bytes 33554432 | tf_op jit(solution)/shard_map/defv,efvp->dep/dot_general | solution.py:22
  84.6 16.0 %fusion.2 = f32[32,8,128,128]{3,2,1,0:T(8,128)} fusion(bf16[32,8,256,128]{2,3,1,0:T(8,128)(2,1)} %copy.23, bf16[256,32,128]{0,2,1:T(8,128)(2,1)S(1)} %get-tuple-element.14), kind=kOutput, calls=%fused_computation.3 | convolution fusion | flops 2147483648 | bytes 35651584 | tf_op jit(solution)/shard_map/qlpf,qlx->lpfx/dot_general | solution.py:44
  100.6 0.0 reduce-scatter.5.cloned.1.call-update
  100.6 0.2 reduce-scatter.3.cloned.1.call-start
  100.8 11.8 %convolution_bitcast_fusion = bf16[256,32,8,128]{3,0,2,1:T(8,128)(2,1)} fusion(bf16[32,8,128,128]{3,2,1,0:T(8,128)(2,1)} %bitcast.64, bf16[256,32,128]{0,2,1:T(8,128)(2,1)S(1)} %get-tuple-element.14), kind=kOutput, calls=%fused_computation.5 | convolution fusion | flops 2147483648 | bytes 27262976 | tf_op jit(solution)/shard_map/iov,omgv->iomg/dot_general | solution.py:33
  112.7 15.8 %bitcast_convert_fusion = bf16[32,256,128]{2,0,1:T(8,128)(2,1)S(1)} fusion(bf16[256,32,8,128]{3,0,2,1:T(8,128)(2,1)} %convolution_bitcast_fusion, s32[32,8]{0,1:T(8,128)S(1)} %get-tuple-element.13), kind=kOutput, calls=%fused_computation.6 | convolution fusion | flops 536879104 | bytes 18875392 | tf_op jit(solution)/shard_map/tckr,ckb->tbr/dot_general | solution.py:38
  128.5 0.0 copy-start
  128.5 2.4 copy.49
  130.9 0.0 reduce-scatter.3.cloned.1.call-update
  130.9 0.0 copy-done
  130.9 2.9 copy.30
  133.8 249.0 %reduce-scatter.5.cloned.1.call-done = f32[32,128,128]{2,1,0:T(8,128)} async-done(((f32[32,1024,128]{2,1,0:T(8,128)}), f32[32,128,128]{2,1,0:T(8,128)}) %reduce-scatter.5.cloned.1.call-update) | async-done | bytes 2097168 | tf_op jit(solution)/shard_map/reduce_scatter | solution.py:49
  382.7 3.2 broadcast_multiply_fusion
  386.0 30.5 %reduce-scatter.3.cloned.1.call-done = bf16[256,1024]{1,0:T(8,128)(2,1)} async-done(((bf16[256,4096]{1,0:T(8,128)(2,1)}), bf16[256,1024]{1,0:T(8,128)(2,1)}) %reduce-scatter.3.cloned.1.call-update) | async-done | bytes 524304 | tf_op jit(solution)/shard_map/reduce_scatter | solution.py:41
  (1 shorter events, 0.0 us)
Async XLA Ops:
  7.2 28.3 %all-gather.2.cloned.1.call-start = ((), (), s32[]{:S(2)}) async-start(), calls=%async_computation.2 | async-start | bytes 2621440 | tf_op jit(solution)/shard_map/all_gather | solution.py:15
  9.3 373.5 %reduce-scatter.5.cloned.1.call-start = ((), (), s32[]{:S(2)}) async-start(), calls=%async_computation.4 | async-start | bytes 18874368 | tf_op jit(solution)/shard_map/reduce_scatter | solution.py:49
  100.6 315.8 %reduce-scatter.3.cloned.1.call-start = ((), (), s32[]{:S(2)}) async-start(), calls=%async_computation.3 | async-start | bytes 2621440 | tf_op jit(solution)/shard_map/reduce_scatter | solution.py:41
  128.5 2.4 copy-start
Sparse Core Ops, SparseCore 0:
  10.1 25.2 all-gather.1
  100.7 281.9 reduce-scatter.4
  386.0 30.3 reduce-scatter.2
where the time goes:
time: 424 us; the launch traced here: 423 us
  waiting for transfers between devices  300 us (71%)
  matrix products  57.3 us (14%)
  local copies, waits for them, and re-layouts  47.3 us (11%)
  between operations  13.8 us (3%)
    reduce_scatter x1, waiting for transfers between devices, local(): lax.psum_scatter(shard_gradient, 'replica', scatter_dimension=1, tiled=True)  249 us
    gather x2, local copies, waits for them, and re-layouts, local(): selected_rows = blocks[:, local_rows]  32.3 us
    reduce_scatter x1, waiting for transfers between devices, local(): lax.psum_scatter(partial_value.astype(jnp.bfloat16), 'shard', scatter_dim...  30.5 us
    all_gather x1, waiting for transfers between devices, local(): whole = lax.all_gather(features, 'shard', axis=1, tiled=True)  20.8 us
    dot_general x1, matrix products, local(): jnp.einsum('qlpf,qlx->lpfx', selected_rows, output_difference, preferred_...  16 us
    dot_general x1, matrix products, local(): jnp.einsum('tckr,ckb->tbr', backward_result, onehot)  15.8 us
    dot_general x1, matrix products, local(): jnp.einsum('defv,efvp->dep', selected_rows, block_weight_tiles, preferred...  13.6 us
    dot_general x1, matrix products, local(): jnp.einsum('iov,omgv->iomg', output_difference, block_weight_tiles, prefe...  11.8 us
  transfers between devices with their start and end apart: 3, of which 3 were waited for; matrix products, arithmetic and copies ran while one was open for 10% of the time, Pallas kernels for 0%

commit v1 on v0

v1 whole, which is shorter than its diff:
```python
import functools
import math

import jax
import jax.numpy as jnp
from jax import lax
from jax.experimental import pallas as pl
from jax.experimental.pallas import tpu as pltpu
from jax.sharding import PartitionSpec as P

F32 = jnp.float32
BF16 = jnp.bfloat16
ANY = pl.BlockSpec(memory_space=pl.ANY)
PARAMS = pltpu.CompilerParams(
    dimension_semantics=("arbitrary",), vmem_limit_bytes=48 * 1024 * 1024
)
STEP = 4


def copy_in(groups, buf, rows, tab, sems):
    copies = [pltpu.make_async_copy(rows, tab, sems.at[0])]
    top = 0
    for group in groups:
        at = 0
        for ref in group:
            height, width = ref.shape
            copies.append(
                pltpu.make_async_copy(
                    ref,
                    buf.at[pl.ds(top, height), pl.ds(at, width)],
                    sems.at[len(copies)],
                )
            )
            at += width
        top += height
    for copy in copies:
        copy.start()
    for copy in copies:
        copy.wait()


class Index:
    def __init__(self, tab, columns, per_column, fold, side):
        shard = lax.axis_index("shard")
        self.base = shard * columns
        self.flip = shard * fold
        self.tab, self.per_column, self.side = tab, per_column, side

    def block(self, col, k):
        return self.tab[(self.base + col) * self.per_column + k] ^ self.flip

    def lanes(self, col, k):
        return pl.ds(pl.multiple_of(self.block(col, k) * self.side, self.side), self.side)

    def gather(self, buf, col, ks):
        return jnp.concatenate([buf[:, self.lanes(col, k)] for k in ks], axis=1)


def staged_blocks(line):
    r = lax.axis_index("replica")
    z, y = r // 2, r % 2
    inner = (z == 1) | (z == 2)
    one, zero = jnp.int32(1), jnp.int32(0)
    order = [
        jnp.where(inner, one, zero),
        jnp.where(inner, zero, one),
        jnp.int32(2),
        jnp.int32(3),
    ]
    return [jnp.where(z >= line // 2, line - 1 - d, d) * 2 + y for d in order]


def direct_blocks(line):
    r = lax.axis_index("replica")
    z, y = r // 2, r % 2
    return [lax.rem(z + n, line) * 2 + y for n in range(line)]


def forward_column(x, w, cot):
    pre = jnp.dot(x, w, preferred_element_type=F32)
    sig = 1.0 / (1.0 + jnp.exp(-pre))
    delta = (cot.astype(F32) * sig * (1.0 + pre * (1.0 - sig))).astype(BF16)
    return pre, sig, delta


def ranges(splits, step):
    out, start = [], 0
    for n in splits:
        out.append((start // step, (start + n) // step - 1))
        start += n
    return out


def held_at(lo, hi):
    return lambda i: jnp.clip(i, lo, hi) - lo


def forward_kernel(nf, first, columns, fold, splits, *refs):
    rows, feats = refs[0], refs[1 : 1 + nf]
    w_ref, cot_ref = refs[1 + nf : 3 + nf]
    buf, tab, sems = refs[-3:]
    delta_refs = refs[-3 - len(splits) : -3]
    act_ref = refs[-4 - len(splits)]
    step, depth, side = w_ref.shape
    per_column = depth // side
    here = pl.program_id(0)

    @pl.when(here == 0)
    def _():
        copy_in([feats], buf, rows, tab, sems)

    index = Index(tab, columns, per_column, fold, side)
    done = []
    for i in range(step):
        x = index.gather(buf, first + here * step + i, range(per_column))
        lanes = slice(i * side, (i + 1) * side)
        pre, sig, delta = forward_column(x, w_ref[i], cot_ref[:, lanes])
        act_ref[:, lanes] = (pre * sig).astype(BF16)
        done.append(delta)
    row = jnp.concatenate(done, axis=1)
    for ref, (lo, hi) in zip(delta_refs, ranges(splits, step)):

        @pl.when((here >= lo) & (here <= hi))
        def _(ref=ref):
            ref[...] = row


def forward(rows, feats, weight, cotangent, fold, act, first, splits, step, after=()):
    tokens, hidden = cotangent.shape
    columns, depth, side = weight.shape
    width = sum(f.shape[1] for f in feats)
    base = first // step
    args = [rows, *feats, weight, cotangent]
    ins = [ANY] * (1 + len(feats)) + [
        pl.BlockSpec((step, depth, side), lambda i: (base + i, 0, 0)),
        pl.BlockSpec((tokens, step * side), lambda i: (0, base + i)),
    ]
    aliases = {}
    if act is not None:
        aliases = {len(args): 0}
        args.append(act)
    args += after
    ins += [ANY] * (len(args) - len(ins))
    outs = [pl.BlockSpec((tokens, step * side), lambda i: (0, base + i))]
    for lo, hi in ranges(splits, step):
        at = held_at(lo, hi)
        outs.append(pl.BlockSpec((tokens, step * side), lambda i, at=at: (0, at(i))))
    return pl.pallas_call(
        functools.partial(forward_kernel, len(feats), first, columns, fold, splits),
        grid=(sum(splits) // step,),
        in_specs=ins,
        out_specs=outs,
        scratch_shapes=[
            pltpu.VMEM((tokens, width), BF16),
            pltpu.SMEM(rows.shape, jnp.int32),
            pltpu.SemaphoreType.DMA((1 + len(feats),)),
        ],
        out_shape=[jax.ShapeDtypeStruct((tokens, hidden), BF16)]
        + [jax.ShapeDtypeStruct((tokens, n * side), BF16) for n in splits],
        input_output_aliases=aliases,
        compiler_params=PARAMS,
        name="forward",
    )(*args)


def block_grads(index, buf, ks, col, delta, scale):
    side = index.side
    x = index.gather(buf, col, ks)
    grad = lax.dot_general(
        x, delta, (((0,), (0,)), ((), ())), preferred_element_type=F32
    )
    return [
        (grad[p * side : (p + 1) * side] * scale).astype(BF16) for p in range(len(ks))
    ]


def grads_kernel(nf, first, columns, fold, scale, line, direct, *refs):
    rows, mine, other = refs[0], refs[1 : 1 + nf], refs[1 + nf : 1 + 2 * nf]
    w_ref, delta_ref, cot_ref = refs[1 + 2 * nf : 4 + 2 * nf]
    buf, tab, sems = refs[-3:]
    sends = refs[-3 - (line - 1 if direct else 1) : -3]
    own_ref = refs[-4 - len(sends)]
    step, depth, side = w_ref.shape
    per_column = depth // side
    tokens = cot_ref.shape[0]
    here = pl.program_id(0)

    @pl.when(here == 0)
    def _():
        copy_in([mine, other], buf, rows, tab, sems)

    index = Index(tab, columns, per_column, fold, side)
    ks = direct_blocks(line) if direct else staged_blocks(line)
    pair = buf.at[pl.ds(tokens, tokens), :]
    done = []
    for i in range(step):
        x = index.gather(pair, first + here * step + i, range(per_column))
        lanes = slice(i * side, (i + 1) * side)
        _, _, delta = forward_column(x, w_ref[i], cot_ref[:, lanes])
        done.append(jnp.concatenate([delta_ref[:, lanes], delta], axis=0))
    for i in range(step):
        blocks = block_grads(index, buf, ks, first + here * step + i, done[i], scale)
        own_ref[i] = blocks[0]
        for p, block in enumerate(blocks[1:]):
            if direct:
                sends[p][i] = block
            else:
                sends[0][p, i] = block


def grads(
    rows, mine, other, weight, delta, cot_other, skip, count, fold, first, line, scale, direct,
    after=(),
):
    tokens = delta.shape[0]
    columns, depth, side = weight.shape
    width = sum(f.shape[1] for f in mine)
    step = math.gcd(first, skip, count, STEP)
    base, skip = first // step, skip // step
    args = [rows, *mine, *other, weight, delta, cot_other, *after]
    ins = [ANY] * (1 + 2 * len(mine)) + [
        pl.BlockSpec((step, depth, side), lambda i: (base + i, 0, 0)),
        pl.BlockSpec((tokens, step * side), lambda i: (0, base + i)),
        pl.BlockSpec((tokens, step * side), lambda i: (0, skip + i)),
    ]
    ins += [ANY] * (len(args) - len(ins))
    one = jax.ShapeDtypeStruct((count, side, side), BF16)
    one_spec = pl.BlockSpec((step, side, side), lambda i: (i, 0, 0))
    if direct:
        sends, send_specs = [one] * (line - 1), [one_spec] * (line - 1)
    else:
        sends = [jax.ShapeDtypeStruct((line - 1, count, side, side), BF16)]
        send_specs = [pl.BlockSpec((line - 1, step, side, side), lambda i: (0, i, 0, 0))]
    return pl.pallas_call(
        functools.partial(grads_kernel, len(mine), first, columns, fold, scale, line, direct),
        grid=(count // step,),
        in_specs=ins,
        out_specs=[one_spec, *send_specs],
        scratch_shapes=[
            pltpu.VMEM((2 * tokens, width), BF16),
            pltpu.SMEM(rows.shape, jnp.int32),
            pltpu.SemaphoreType.DMA((1 + 2 * len(mine),)),
        ],
        out_shape=[one, *sends],
        compiler_params=PARAMS,
        name="grads",
    )(*args)


def dinput_kernel(nd, fold, groups, *refs):
    rows, deltas, w_ref = refs[0], refs[1 : 1 + nd], refs[1 + nd]
    buf, acc, tab, sems = refs[-4:]
    outs = refs[-4 - len(groups) : -4]
    step, depth, side = w_ref.shape
    per_column = depth // side
    here = pl.program_id(0)

    @pl.when(here == 0)
    def _():
        copy_in([deltas], buf, rows, tab, sems)
        acc[...] = jnp.zeros_like(acc)

    index = Index(tab, buf.shape[1] // side, per_column, fold, side)
    for i in range(step):
        col = here * step + i
        d = buf[:, pl.ds(pl.multiple_of(col * side, side), side)]
        g = lax.dot_general(
            d, w_ref[i], (((1,), (1,)), ((), ())), preferred_element_type=F32
        )
        for k in range(per_column):
            acc[index.block(col, k)] += g[:, k * side : (k + 1) * side]

    @pl.when(here == pl.num_programs(0) - 1)
    def _():
        for out, group in zip(outs, groups):
            blocks = out.shape[2] // side
            for n, piece in enumerate(group):
                for b in range(blocks):
                    out[n, :, b * side : (b + 1) * side] = acc[piece * blocks + b].astype(BF16)


def dinput(rows, weight, deltas, fold, groups, width, step, after=()):
    tokens = deltas[0].shape[0]
    columns, depth, side = weight.shape
    pieces = sum(len(g) for g in groups)
    shapes = [(len(g), tokens, width) for g in groups]
    return pl.pallas_call(
        functools.partial(dinput_kernel, len(deltas), fold, groups),
        grid=(columns // step,),
        in_specs=[ANY] * (1 + len(deltas))
        + [pl.BlockSpec((step, depth, side), lambda i: (i, 0, 0))]
        + [ANY] * len(after),
        out_specs=[pl.BlockSpec(s, lambda i: (0, 0, 0)) for s in shapes],
        scratch_shapes=[
            pltpu.VMEM((tokens, columns * side), BF16),
            pltpu.VMEM((pieces * width // side, tokens, side), F32),
            pltpu.SMEM(rows.shape, jnp.int32),
            pltpu.SemaphoreType.DMA((1 + len(deltas),)),
        ],
        out_shape=[jax.ShapeDtypeStruct(s, BF16) for s in shapes],
        compiler_params=PARAMS,
        name="dinput",
    )(rows, *deltas, weight, *after)


def relay_kernel(jobs, *refs):
    outs = refs[-len(jobs) :]
    for n, (a_at, b_at, count) in enumerate(jobs):
        a, b = refs[2 * n], refs[2 * n + 1]
        for i in range(count):
            outs[n][i] = (a[a_at + i].astype(F32) + b[b_at + i].astype(F32)).astype(BF16)


def relay(*jobs, after=()):
    args, ins, outs, shapes, cuts = [], [], [], [], []
    steps = 2
    for a, a_at, b, b_at, count in jobs:
        part = (a.shape[1] // steps,) + a.shape[2:]
        zeros = (0,) * (a.ndim - 2)
        for x in (a, b):
            args.append(x)
            ins.append(pl.BlockSpec(x.shape[:1] + part, lambda i, z=zeros: (0, i) + z))
        outs.append(pl.BlockSpec((count,) + part, lambda i, z=zeros: (0, i) + z))
        shapes.append(jax.ShapeDtypeStruct((count,) + a.shape[1:], BF16))
        cuts.append((a_at, b_at, count))

    def kernel(*refs):
        relay_kernel(cuts, *refs[: len(args)], *refs[len(args) + len(after) :])

    return pl.pallas_call(
        kernel,
        grid=(steps,),
        in_specs=ins + [ANY] * len(after),
        out_specs=outs,
        out_shape=shapes,
        compiler_params=PARAMS,
        name="relay",
    )(*args, *after)


def cut_kernel(splits, x_ref, *refs):
    refs = refs[-len(splits) :]
    here = pl.program_id(0)
    for ref, (lo, hi) in zip(refs, ranges(splits, 1)):

        @pl.when((here >= lo) & (here <= hi))
        def _(ref=ref):
            ref[...] = x_ref[...]


def cut(x, first, splits, width, after=()):
    height = x.shape[0]
    outs = []
    for lo, hi in ranges(splits, 1):
        at = held_at(lo, hi)
        outs.append(pl.BlockSpec((height, width), lambda i, at=at: (0, at(i))))
    return pl.pallas_call(
        functools.partial(cut_kernel, splits),
        grid=(sum(splits),),
        in_specs=[pl.BlockSpec((height, width), lambda i: (0, first + i))] + [ANY] * len(after),
        out_specs=outs,
        out_shape=[jax.ShapeDtypeStruct((height, n * width), x.dtype) for n in splits],
        compiler_params=PARAMS,
        name="cut",
    )(x, *after)


def gate_kernel(*refs):
    del refs


def gate(x, *after):
    return pl.pallas_call(
        gate_kernel,
        in_specs=[ANY] * (1 + len(after)),
        out_specs=ANY,
        out_shape=jax.ShapeDtypeStruct(x.shape, x.dtype),
        input_output_aliases={0: 0},
        name="gate",
    )(x, *after)


def local_line(features, weight, rows_index, cotangent):
    tokens, held = features.shape
    columns, depth, side = weight.shape
    per_column = depth // side
    replicas, shards = lax.axis_size("replica"), lax.axis_size("shard")
    scale = 1.0 / math.sqrt(tokens * replicas)
    rows = rows_index.reshape(-1)
    fold = held // side
    line = replicas // 2

    def permute(axis, links):
        return lambda x: lax.ppermute(x, axis, links)

    def along(steps):
        return permute("replica", [(a * 2 + p, b * 2 + p) for a, b in steps for p in range(2)])

    cores = permute("shard", [(i, i ^ 1) for i in range(shards)])
    chips = permute("shard", [(i, i ^ 2) for i in range(shards)])
    pairs = permute("replica", [(i, i ^ 1) for i in range(replicas)])
    outer_in = along([(0, 1), (3, 2)])
    middle = along([(1, 2), (2, 1)])
    outer_out = along([(1, 0), (2, 3)])
    shifts = [along([(a, (a + n) % line) for a in range(line)]) for n in range(1, line)]

    sizes = [c * columns // 32 for c in (6, 6, 6, 6, 8)]
    firsts = [sum(sizes[:n]) for n in range(len(sizes))]
    parts = [sizes[0], sizes[1] + sizes[2], sizes[3] + sizes[4]]
    places = [(0, 0), (1, 0), (1, sizes[1]), (2, 0), (2, sizes[3])]

    f0 = features
    f2 = chips(f0)
    u0 = pairs(f0)
    unit = math.gcd(*sizes)
    cots = cut(cotangent, 0, [n // unit for n in parts], unit * side)
    c0, c1, c2 = cs = [pairs(x) for x in cots]
    f1 = cores(f0)
    f3 = cores(f2)
    u1 = cores(u0)
    u2 = chips(u0)
    mine = [f0, f1, f2, f3]
    act, delta = forward(
        rows, mine, weight, cotangent, fold, None, 0, (columns,), STEP, (cots[0],)
    )
    u2 = gate(u2, delta, c0)
    u3 = cores(u2)
    other = [u0, u1, u2, u3]

    def chunk(n, direct, *after):
        part, skip = places[n]
        return grads(
            rows, mine, other, weight, delta, cs[part], skip, sizes[n], fold, firsts[n],
            line, scale, direct, after,
        )

    own0, rest0 = chunk(0, False)
    got0 = outer_in(rest0)
    near, away0, away1 = dinput(
        rows, weight, [delta], fold, ((0, 2), (1,), (3,)), held, STEP, (own0,)
    )
    sib0, sib1 = cores(away0), cores(away1)
    own1, rest1 = chunk(1, False, near)
    got1 = outer_in(rest1)
    (far0,) = relay((rest0, 1, got0, 1, 2), after=(own1,))
    across0 = middle(far0)
    own2, rest2 = chunk(2, False, far0)
    got2 = outer_in(rest2)
    far1, home0 = relay((rest1, 1, got1, 1, 2), (rest0, 0, across0, 1, 1), after=(own2,))
    across1 = middle(far1)
    back0 = outer_out(home0)
    own3, rest3 = chunk(3, False, far1)
    got3 = outer_in(rest3)
    (xsum,) = relay((near, 1, sib1, 0, 1), after=(own3,))
    xback = chips(xsum)
    own4, *sends = chunk(4, True, xsum)
    arrived = [shift(x) for shift, x in zip(shifts, sends)]
    far2, home1 = relay((rest2, 1, got2, 1, 2), (rest1, 0, across1, 1, 1), after=(own4,))
    across2 = middle(far2)
    back1 = outer_out(home1)
    far3, home2 = relay((rest3, 1, got3, 1, 2), (rest2, 0, across2, 1, 1), after=(far2,))
    across3 = middle(far3)
    back2 = outer_out(home2)
    (home3,) = relay((rest3, 0, across3, 1, 1), after=(far3,))
    back3 = outer_out(home3)

    def total(own, got, across, back):
        return own.astype(F32) + got[0].astype(F32) + across[0].astype(F32) + back[0].astype(F32)

    weight_grad = jnp.concatenate(
        [
            total(own0, got0, across0, back0),
            total(own1, got1, across1, back1),
            total(own2, got2, across2, back2),
            total(own3, got3, across3, back3),
            own4.astype(F32) + sum(x.astype(F32) for x in arrived),
        ],
        axis=0,
    )
    input_grad = (
        near[0].astype(F32) + sib0[0].astype(F32) + xback[0].astype(F32)
    ).astype(BF16)
    return act, input_grad, weight_grad


def local_any(features, weight, rows_index, cotangent):
    tokens = features.shape[0]
    columns, depth, side = weight.shape
    per_column = depth // side
    scale = 1.0 / math.sqrt(tokens * lax.axis_size("replica"))
    whole = lax.all_gather(features, "shard", axis=1, tiled=True)
    block_rows = whole.shape[1] // side
    first = lax.axis_index("shard") * columns
    local_rows = lax.dynamic_slice_in_dim(rows_index, first, columns, 0)
    rows = rows_index.reshape(-1)
    step = math.gcd(columns, STEP)
    act, delta = forward(rows, [whole], weight, cotangent, 0, None, 0, (columns,), step)
    (part,) = dinput(rows, weight, [delta], 0, ((0,),), whole.shape[1], step)
    input_grad = lax.psum_scatter(part[0], "shard", scatter_dimension=1, tiled=True)
    blocks = whole.reshape(tokens, block_rows, side)[:, local_rows]
    grads = jnp.einsum(
        "qlpf,qlx->lpfx",
        blocks,
        delta.reshape(tokens, columns, side),
        preferred_element_type=F32,
    ).reshape(columns, per_column * side, side)
    weight_grad = lax.psum_scatter(grads, "replica", scatter_dimension=1, tiled=True) * scale
    return act, input_grad, weight_grad


def solution(mesh):
    placed = (P("replica", "shard"), P("shard", None, None), P(), P("replica", "shard"))
    fits = mesh.shape["replica"] == 8 and mesh.shape["shard"] == 4
    return jax.shard_map(
        local_line if fits else local_any,
        mesh=mesh,
        in_specs=placed,
        out_specs=(P("replica", "shard"), P("replica", "shard"), P("shard", "replica", None)),
        check_vma=False,
    )
```

time: 424 us -> 168 us (0.40)
  waiting for transfers between devices: 300 us -> 52.2 us
  matrix products: 57.3 us -> 0 us
  Pallas kernels: 0 us -> 55.4 us
  starting transfers between devices: 0.3 us -> 42.2 us
  local copies, waits for them, and re-layouts: 47.3 us -> 10.4 us
  between operations: 13.8 us -> 1.02 us
    reduce_scatter x2 -> x0, waiting for transfers between devices: 279 us -> none  [the longest x1 249 us: local(): lax.psum_scatter(shard_gradient, 'replica', scatter_dimension=1, tiled=True)]
    dot_general x4 -> x0, matrix products: 57.3 us -> none  [the longest x1 16 us: local(): jnp.einsum('qlpf,qlx->lpfx', selected_rows, output_difference, preferred_...]
    pallas_call x0 -> x15, Pallas kernels: none -> 55.4 us  [the longest x5 28.2 us: grads(): pl.pallas_call(functools.partial(grads_kernel, len(mine), first, columns,...]
    ppermute x0 -> x28, waiting for transfers between devices: none -> 52.2 us  [permute(): return lambda x: lax.ppermute(x, axis, links)]
    ppermute x0 -> x28, starting transfers between devices: none -> 42.2 us  [permute(): return lambda x: lax.ppermute(x, axis, links)]
    gather x2 -> x0, local copies, waits for them, and re-layouts: 32.3 us -> none  [local(): selected_rows = blocks[:, local_rows]]
    all_gather x1 -> x0, waiting for transfers between devices: 20.8 us -> none  [local(): whole = lax.all_gather(features, 'shard', axis=1, tiled=True)]
    reshape x2 -> x1, local copies, waits for them, and re-layouts: 7.55 us -> 0.93 us  [local_line(): rows = rows_index.reshape(-1)]
  transfers between devices with their start and end apart: 3 -> 28, of which waited for: 3 -> 7; matrix products, arithmetic and copies ran while one was open for 10% -> 4% of each run, Pallas kernels for 0% -> 33%
where the time goes in v1:
time: 168 us; the launch traced here: 167 us
  Pallas kernels  55.4 us (33%)
  waiting for transfers between devices  52.2 us (31%)
  starting transfers between devices  42.2 us (25%)
  local copies, waits for them, and re-layouts  10.4 us (6%)
  other arithmetic  5.37 us (3%)
    ppermute x28, waiting for transfers between devices, permute(): return lambda x: lax.ppermute(x, axis, links)  52.2 us
    ppermute x28, starting transfers between devices, permute(): return lambda x: lax.ppermute(x, axis, links)  42.2 us
    pallas_call x5, Pallas kernels, grads(): pl.pallas_call(functools.partial(grads_kernel, len(mine), first, columns,...  28.2 us
    pallas_call x1, Pallas kernels, forward(): pl.pallas_call(functools.partial(forward_kernel, len(feats), first, colum...  12 us
    pallas_call x1, Pallas kernels, dinput(): pl.pallas_call(functools.partial(dinput_kernel, len(deltas), fold, groups...  10.7 us
    unnamed x31, local copies, waits for them, and re-layouts  9.43 us
    unnamed x4, other arithmetic  3.38 us
  transfers between devices with their start and end apart: 28, of which 7 were waited for; matrix products, arithmetic and copies ran while one was open for 4% of the time, Pallas kernels for 33%

profile of v1, /device:TPU:0, one launch (start us, length us, event | category | flops | bytes accessed | tf_op | source)
XLA Modules:
  0.0 166.5 jit_solution(17855574057628530930)
XLA Ops:
  0.6 3.0 %collective-permute-start.1 = (bf16[256,1024]{1,0:T(8,128)(2,1)}, bf16[256,1024]{1,0:T(8,128)(2,1)S(1)}, u32[]{:S(2)}, u32[]{:S(2)}) collective-permute-start(bf16[256,1024]{1,0:T(8,128)(2,1)} %refs_1_.11), channel_id=1, source_target_pairs={{0,2},{1,3},{2,0},{3,1},{4,6},{5,7},{6,4},{7,5},{8,10},{9,11},{10,... | collective-permute-start | bytes 1572872 | tf_op jit(solution)/shard_map/ppermute | solution.py:394
  3.6 1.5 collective-permute-start.3
  5.2 10.6 %collective-permute-done.1.refs_3_ = bf16[256,1024]{1,0:T(8,128)(2,1)S(1)} collective-permute-done((bf16[256,1024]{1,0:T(8,128)(2,1)}, bf16[256,1024]{1,0:T(8,128)(2,1)S(1)}, u32[]{:S(2)}, u32[]{:S(2)}) %collective-permute-start.1) | collective-permute-done | bytes 524320 | tf_op jit(solution)/shard_map/ppermute | solution.py:394
  15.8 1.5 collective-permute-done.3.refs_5_
  17.6 1.6 copy-done.6
  19.2 2.7 %cut.1 = (bf16[256,768]{1,0:T(8,128)(2,1)}, bf16[256,1536]{1,0:T(8,128)(2,1)S(1)}, bf16[256,1792]{1,0:T(8,128)(2,1)S(1)}) custom-call(bf16[256,4096]{1,0:T(8,128)(2,1)S(1)} %copy-done.6), custom_call_target="tpu_custom_call" | custom-call | tf_op jit(solution)/shard_map/cut/pallas_call | solution.py:357
  23.7 1.7 %collective-permute-start.6 = (bf16[256,768]{1,0:T(8,128)(2,1)}, bf16[256,768]{1,0:T(8,128)(2,1)S(1)}, u32[]{:S(2)}, u32[]{:S(2)}) collective-permute-start(bf16[256,768]{1,0:T(8,128)(2,1)} %get-tuple-element.29.refs_7_), channel_id=1, source_target_pairs={{0,4},{4,0},{8,12},{12,8},{16,20},{20,16},{24,28},{28,24},{1,5},{5... | collective-permute-start | bytes 1179656 | tf_op jit(solution)/shard_map/ppermute | solution.py:394
  27.2 12.0 %forward.1 = (bf16[256,4096]{1,0:T(8,128)(2,1)}, bf16[256,4096]{1,0:T(8,128)(2,1)S(1)}) custom-call(s32[1024]{0:T(1024)S(1)} %reshape.39.refs_0_, bf16[256,1024]{1,0:T(8,128)(2,1)S(1)} %copy-done.2, bf16[256,1024]{1,0:T(8,128)(2,1)S(1)} %collective-permute-done.refs_2_, bf16[256,1024]{1,0:T(8,128)(2,1)S(1)} %collective-permute-done.1.refs_3_, ...), custom_call_target="tpu_custom_call" | custom-call | tf_op jit(solution)/shard_map/forward/pallas_call | solution.py:148
  39.2 1.3 copy-done
  42.3 1.4 collective-permute-done.7.refs_8_
  45.8 5.4 %grads.5 = (bf16[6,128,128]{2,1,0:T(8,128)(2,1)S(1)}, bf16[3,6,128,128]{3,2,1,0:T(8,128)(2,1)S(1)}) custom-call(s32[1024]{0:T(1024)S(1)} %reshape.39.refs_0_, bf16[256,1024]{1,0:T(8,128)(2,1)S(1)} %copy-done.2, bf16[256,1024]{1,0:T(8,128)(2,1)S(1)} %collective-permute-done.refs_2_, bf16[256,1024]{1,0:T(8,128)(2,1)S(1)} %collective-permute-done.1.refs_3_, ...), custom_call_target="tpu_custom_call" | custom-call | tf_op jit(solution)/shard_map/grads/pallas_call | solution.py:234
  51.2 3.5 %collective-permute-start.13 = (bf16[3,6,128,128]{3,2,1,0:T(8,128)(2,1)S(1)}, bf16[3,6,128,128]{3,2,1,0:T(8,128)(2,1)S(1)}, u32[]{:S(2)}, u32[]{:S(2)}) collective-permute-start(bf16[3,6,128,128]{3,2,1,0:T(8,128)(2,1)S(1)} %get-tuple-element.39.refs_0_.refs_2_), channel_id=1, source_target_pairs={{0,8},{4,12},{24,16},{28,20},{1,9},{5,13},{25,17},{29,21},{2,10},{... | collective-permute-start | bytes 1769480 | tf_op jit(solution)/shard_map/ppermute | solution.py:394
  55.3 10.7 %dinput.1 = (bf16[2,256,1024]{2,1,0:T(8,128)(2,1)S(1)}, bf16[1,256,1024]{2,1,0:T(8,128)(2,1)S(1)}, bf16[1,256,1024]{2,1,0:T(8,128)(2,1)S(1)}) custom-call(s32[1024]{0:T(1024)S(1)} %reshape.39.refs_0_, bf16[256,4096]{1,0:T(8,128)(2,1)S(1)} %copy-done.1, bf16[32,1024,128]{2,1,0:T(8,128)(2,1)} %refs_9_.9, bf16[6,128,128]{2,1,0:T(8,128)(2,1)S(1)} %get-tuple-element.32.refs_3_), custom_call_target="tpu_custom_call" | custom-call | tf_op jit(solution)/shard_map/dinput/pallas_call | solution.py:287
  67.0 5.4 %grads.6 = (bf16[6,128,128]{2,1,0:T(8,128)(2,1)S(1)}, bf16[3,6,128,128]{3,2,1,0:T(8,128)(2,1)S(1)}) custom-call(s32[1024]{0:T(1024)S(1)} %reshape.39.refs_0_, bf16[256,1024]{1,0:T(8,128)(2,1)S(1)} %copy-done.2, bf16[256,1024]{1,0:T(8,128)(2,1)S(1)} %collective-permute-done.refs_2_, bf16[256,1024]{1,0:T(8,128)(2,1)S(1)} %collective-permute-done.1.refs_3_, ...), custom_call_target="tpu_custom_call" | custom-call | tf_op jit(solution)/shard_map/grads/pallas_call | solution.py:234
  72.4 1.3 collective-permute-start.12
  74.8 5.4 %grads.7 = (bf16[6,128,128]{2,1,0:T(8,128)(2,1)S(1)}, bf16[3,6,128,128]{3,2,1,0:T(8,128)(2,1)S(1)}) custom-call(s32[1024]{0:T(1024)S(1)} %reshape.39.refs_0_, bf16[256,1024]{1,0:T(8,128)(2,1)S(1)} %copy-done.2, bf16[256,1024]{1,0:T(8,128)(2,1)S(1)} %collective-permute-done.refs_2_, bf16[256,1024]{1,0:T(8,128)(2,1)S(1)} %collective-permute-done.1.refs_3_, ...), custom_call_target="tpu_custom_call" | custom-call | tf_op jit(solution)/shard_map/grads/pallas_call | solution.py:234
  80.2 4.1 %collective-permute-start.18 = (bf16[3,6,128,128]{3,2,1,0:T(8,128)(2,1)S(1)}, bf16[3,6,128,128]{3,2,1,0:T(8,128)(2,1)S(1)}, u32[]{:S(2)}, u32[]{:S(2)}) collective-permute-start(bf16[3,6,128,128]{3,2,1,0:T(8,128)(2,1)S(1)} %get-tuple-element.45.refs_0_.refs_2_), channel_id=1, source_target_pairs={{0,8},{4,12},{24,16},{28,20},{1,9},{5,13},{25,17},{29,21},{2,10},{... | collective-permute-start | bytes 1769480 | tf_op jit(solution)/shard_map/ppermute | solution.py:394
  84.2 3.1 %collective-permute-done.12.refs_1_ = bf16[3,6,128,128]{3,2,1,0:T(8,128)(2,1)S(1)} collective-permute-done((bf16[3,6,128,128]{3,2,1,0:T(8,128)(2,1)S(1)}, bf16[3,6,128,128]{3,2,1,0:T(8,128)(2,1)S(1)}, u32[]{:S(2)}, u32[]{:S(2)}) %collective-permute-start.12) | collective-permute-done | bytes 589856 | tf_op jit(solution)/shard_map/ppermute | solution.py:394
  88.6 5.5 %grads.8 = (bf16[6,128,128]{2,1,0:T(8,128)(2,1)S(1)}, bf16[3,6,128,128]{3,2,1,0:T(8,128)(2,1)S(1)}) custom-call(s32[1024]{0:T(1024)S(1)} %reshape.39.refs_0_, bf16[256,1024]{1,0:T(8,128)(2,1)S(1)} %copy-done.2, bf16[256,1024]{1,0:T(8,128)(2,1)S(1)} %collective-permute-done.refs_2_, bf16[256,1024]{1,0:T(8,128)(2,1)S(1)} %collective-permute-done.1.refs_3_, ...), custom_call_target="tpu_custom_call" | custom-call | tf_op jit(solution)/shard_map/grads/pallas_call | solution.py:234
  94.1 7.2 %collective-permute-start.21 = (bf16[3,6,128,128]{3,2,1,0:T(8,128)(2,1)S(1)}, bf16[3,6,128,128]{3,2,1,0:T(8,128)(2,1)S(1)}, u32[]{:S(2)}, u32[]{:S(2)}) collective-permute-start(bf16[3,6,128,128]{3,2,1,0:T(8,128)(2,1)S(1)} %get-tuple-element.49.refs_0_), channel_id=1, source_target_pairs={{0,8},{4,12},{24,16},{28,20},{1,9},{5,13},{25,17},{29,21},{2,10},{... | collective-permute-start | bytes 1769480 | tf_op jit(solution)/shard_map/ppermute | solution.py:394
  101.7 1.5 collective-permute-start.15
  103.2 1.3 collective-permute-start.16
  104.5 6.5 %grads.9 = (bf16[8,128,128]{2,1,0:T(8,128)(2,1)S(1)}, bf16[8,128,128]{2,1,0:T(8,128)(2,1)S(1)}, bf16[8,128,128]{2,1,0:T(8,128)(2,1)S(1)}, bf16[8,128,128]{2,1,0:T(8,128)(2,1)S(1)}) custom-call(s32[1024]{0:T(1024)S(1)} %reshape.39.refs_0_, bf16[256,1024]{1,0:T(8,128)(2,1)S(1)} %copy-done.2, bf16[256,1024]{1,0:T(8,128)(2,1)S(1)} %collective-permute-done.refs_2_, ...), custom_call_target="tpu_custom_call" | custom-call | tf_op jit(solution)/shard_map/grads/pallas_call | solution.py:234
  112.1 4.4 %collective-permute-start.25 = (bf16[8,128,128]{2,1,0:T(8,128)(2,1)S(1)}, bf16[8,128,128]{2,1,0:T(8,128)(2,1)S(1)}, u32[]{:S(2)}, u32[]{:S(2)}) collective-permute-start(bf16[8,128,128]{2,1,0:T(8,128)(2,1)S(1)} %get-tuple-element.52), channel_id=1, source_target_pairs={{0,8},{4,12},{8,16},{12,20},{16,24},{20,28},{24,0},{28,4},{1,9},{5... | collective-permute-start | bytes 786440 | tf_op jit(solution)/shard_map/ppermute | solution.py:394
  118.3 2.9 %collective-permute-start.27 = (bf16[8,128,128]{2,1,0:T(8,128)(2,1)S(1)}, bf16[8,128,128]{2,1,0:T(8,128)(2,1)S(1)}, u32[]{:S(2)}, u32[]{:S(2)}) collective-permute-start(bf16[8,128,128]{2,1,0:T(8,128)(2,1)S(1)} %get-tuple-element.54), channel_id=1, source_target_pairs={{0,24},{4,28},{8,0},{12,4},{16,8},{20,12},{24,16},{28,20},{1,25},{... | collective-permute-start | bytes 786440 | tf_op jit(solution)/shard_map/ppermute | solution.py:394
  121.6 1.3 collective-permute-start.19
  123.6 1.1 fusion
  124.7 27.1 %collective-permute-done.19 = bf16[1,6,128,128]{3,2,1,0:T(8,128)(2,1)S(1)} collective-permute-done((bf16[1,6,128,128]{3,2,1,0:T(8,128)(2,1)S(1)}, bf16[1,6,128,128]{3,2,1,0:T(8,128)(2,1)S(1)}, u32[]{:S(2)}, u32[]{:S(2)}) %collective-permute-start.19) | collective-permute-done | bytes 196640 | tf_op jit(solution)/shard_map/ppermute | solution.py:394
  151.8 1.3 collective-permute-start.22
  154.1 1.3 collective-permute-start.24
  155.4 6.0 %collective-permute-done.22 = bf16[1,6,128,128]{3,2,1,0:T(8,128)(2,1)S(1)} collective-permute-done((bf16[1,6,128,128]{3,2,1,0:T(8,128)(2,1)S(1)}, bf16[1,6,128,128]{3,2,1,0:T(8,128)(2,1)S(1)}, u32[]{:S(2)}, u32[]{:S(2)}) %collective-permute-start.22) | collective-permute-done | bytes 196640 | tf_op jit(solution)/shard_map/ppermute | solution.py:394
  162.3 2.4 %collective-permute-done.24 = bf16[1,6,128,128]{3,2,1,0:T(8,128)(2,1)S(1)} collective-permute-done((bf16[1,6,128,128]{3,2,1,0:T(8,128)(2,1)S(1)}, bf16[1,6,128,128]{3,2,1,0:T(8,128)(2,1)S(1)}, u32[]{:S(2)}, u32[]{:S(2)}) %collective-permute-start.24) | collective-permute-done | bytes 196640 | tf_op jit(solution)/shard_map/ppermute | solution.py:394
  (77 shorter events, 19.6 us)
Async XLA Ops:
  0.6 26.5 %copy-start.2 = (bf16[256,1024]{1,0:T(8,128)(2,1)S(1)}, bf16[256,1024]{1,0:T(8,128)(2,1)}, u32[]{:S(2)}) copy-start(bf16[256,1024]{1,0:T(8,128)(2,1)} %refs_1_.11) | copy-start | bytes 1572868
  0.6 15.1 %collective-permute-start.1 = (bf16[256,1024]{1,0:T(8,128)(2,1)}, bf16[256,1024]{1,0:T(8,128)(2,1)S(1)}, u32[]{:S(2)}, u32[]{:S(2)}) collective-permute-start(bf16[256,1024]{1,0:T(8,128)(2,1)} %refs_1_.11), channel_id=1, source_target_pairs={{0,2},{1,3},{2,0},{3,1},{4,6},{5,7},{6,4},{7,5},{8,10},{9,11},{10,... | collective-permute-start | bytes 1572872 | tf_op jit(solution)/shard_map/ppermute | solution.py:394
  3.6 13.6 %collective-permute-start.3 = (bf16[256,1024]{1,0:T(8,128)(2,1)}, bf16[256,1024]{1,0:T(8,128)(2,1)S(1)}, u32[]{:S(2)}, u32[]{:S(2)}) collective-permute-start(bf16[256,1024]{1,0:T(8,128)(2,1)} %refs_1_.11), channel_id=1, source_target_pairs={{0,4},{4,0},{8,12},{12,8},{16,20},{20,16},{24,28},{28,24},{1,5},{5... | collective-permute-start | bytes 1572872 | tf_op jit(solution)/shard_map/ppermute | solution.py:394
  5.2 22.0 %collective-permute-start = (bf16[256,1024]{1,0:T(8,128)(2,1)}, bf16[256,1024]{1,0:T(8,128)(2,1)S(1)}, u32[]{:S(2)}, u32[]{:S(2)}) collective-permute-start(bf16[256,1024]{1,0:T(8,128)(2,1)} %refs_1_.11), channel_id=1, source_target_pairs={{0,1},{1,0},{2,3},{3,2},{4,5},{5,4},{6,7},{7,6},{8,9},{9,8},{10,11... | collective-permute-start | bytes 1572872 | tf_op jit(solution)/shard_map/ppermute | solution.py:394
  15.8 11.4 %collective-permute-start.2 = (bf16[256,1024]{1,0:T(8,128)(2,1)S(1)}, bf16[256,1024]{1,0:T(8,128)(2,1)S(1)}, u32[]{:S(2)}, u32[]{:S(2)}) collective-permute-start(bf16[256,1024]{1,0:T(8,128)(2,1)S(1)} %collective-permute-done.1.refs_3_), channel_id=1, source_target_pairs={{0,1},{1,0},{2,3},{3,2},{4,5},{5,4},{6,7},{7,6},{8,9},{9,8},{10,11... | collective-permute-start | bytes 1572872 | tf_op jit(solution)/shard_map/ppermute | solution.py:394
  17.2 23.3 %collective-permute-start.5 = (bf16[256,1024]{1,0:T(8,128)(2,1)S(1)}, bf16[256,1024]{1,0:T(8,128)(2,1)S(1)}, u32[]{:S(2)}, u32[]{:S(2)}) collective-permute-start(bf16[256,1024]{1,0:T(8,128)(2,1)S(1)} %collective-permute-done.3.refs_5_), channel_id=1, source_target_pairs={{0,2},{1,3},{2,0},{3,1},{4,6},{5,7},{6,4},{7,5},{8,10},{9,11},{10,... | collective-permute-start | bytes 1572872 | tf_op jit(solution)/shard_map/ppermute | solution.py:394
  23.7 16.8 %collective-permute-start.6 = (bf16[256,768]{1,0:T(8,128)(2,1)}, bf16[256,768]{1,0:T(8,128)(2,1)S(1)}, u32[]{:S(2)}, u32[]{:S(2)}) collective-permute-start(bf16[256,768]{1,0:T(8,128)(2,1)} %get-tuple-element.29.refs_7_), channel_id=1, source_target_pairs={{0,4},{4,0},{8,12},{12,8},{16,20},{20,16},{24,28},{28,24},{1,5},{5... | collective-permute-start | bytes 1179656 | tf_op jit(solution)/shard_map/ppermute | solution.py:394
  27.1 15.3 %collective-permute-start.4 = (bf16[256,1024]{1,0:T(8,128)(2,1)S(1)}, bf16[256,1024]{1,0:T(8,128)(2,1)}, u32[]{:S(2)}, u32[]{:S(2)}) collective-permute-start(bf16[256,1024]{1,0:T(8,128)(2,1)S(1)} %collective-permute-done.3.refs_5_), channel_id=1, source_target_pairs={{0,1},{1,0},{2,3},{3,2},{4,5},{5,4},{6,7},{7,6},{8,9},{9,8},{10,11... | collective-permute-start | bytes 1572872 | tf_op jit(solution)/shard_map/ppermute | solution.py:394
  41.5 2.2 %collective-permute-start.7 = (bf16[256,1024]{1,0:T(8,128)(2,1)}, bf16[256,1024]{1,0:T(8,128)(2,1)S(1)}, u32[]{:S(2)}, u32[]{:S(2)}) collective-permute-start(bf16[256,1024]{1,0:T(8,128)(2,1)} %gate.1.refs_7_), channel_id=1, source_target_pairs={{0,1},{1,0},{2,3},{3,2},{4,5},{5,4},{6,7},{7,6},{8,9},{9,8},{10,11... | collective-permute-start | bytes 1572872 | tf_op jit(solution)/shard_map/ppermute | solution.py:394
  42.0 13.4 %copy-start.1 = (bf16[256,4096]{1,0:T(8,128)(2,1)S(1)}, bf16[256,4096]{1,0:T(8,128)(2,1)}, u32[]{:S(2)}) copy-start(bf16[256,4096]{1,0:T(8,128)(2,1)} %copy-done) | copy-start | bytes 6291460
  42.0 25.0 %collective-permute-start.11 = (bf16[256,1536]{1,0:T(8,128)(2,1)}, bf16[256,1536]{1,0:T(8,128)(2,1)S(1)}, u32[]{:S(2)}, u32[]{:S(2)}) collective-permute-start(bf16[256,1536]{1,0:T(8,128)(2,1)} %copy-done.13), channel_id=1, source_target_pairs={{0,4},{4,0},{8,12},{12,8},{16,20},{20,16},{24,28},{28,24},{1,5},{5... | collective-permute-start | bytes 2359304 | tf_op jit(solution)/shard_map/ppermute | solution.py:394
  51.2 22.5 %collective-permute-start.13 = (bf16[3,6,128,128]{3,2,1,0:T(8,128)(2,1)S(1)}, bf16[3,6,128,128]{3,2,1,0:T(8,128)(2,1)S(1)}, u32[]{:S(2)}, u32[]{:S(2)}) collective-permute-start(bf16[3,6,128,128]{3,2,1,0:T(8,128)(2,1)S(1)} %get-tuple-element.39.refs_0_.refs_2_), channel_id=1, source_target_pairs={{0,8},{4,12},{24,16},{28,20},{1,9},{5,13},{25,17},{29,21},{2,10},{... | collective-permute-start | bytes 1769480 | tf_op jit(solution)/shard_map/ppermute | solution.py:394
  54.7 33.8 %collective-permute-start.10 = (bf16[256,1792]{1,0:T(8,128)(2,1)S(1)}, bf16[256,1792]{1,0:T(8,128)(2,1)}, u32[]{:S(2)}, u32[]{:S(2)}) collective-permute-start(bf16[256,1792]{1,0:T(8,128)(2,1)S(1)} %copy-done.12), channel_id=1, source_target_pairs={{0,4},{4,0},{8,12},{12,8},{16,20},{20,16},{24,28},{28,24},{1,5},{5... | collective-permute-start | bytes 2752520 | tf_op jit(solution)/shard_map/ppermute | solution.py:394
  55.3 11.7 %copy-start.5 = (bf16[256,1024]{1,0:T(8,128)(2,1)S(1)}, bf16[256,1024]{1,0:T(8,128)(2,1)}, u32[]{:S(2)}) copy-start(bf16[256,1024]{1,0:T(8,128)(2,1)} %gate.1.refs_7_) | copy-start | bytes 1572868
  72.4 15.0 %collective-permute-start.12 = (bf16[3,6,128,128]{3,2,1,0:T(8,128)(2,1)S(1)}, bf16[3,6,128,128]{3,2,1,0:T(8,128)(2,1)S(1)}, u32[]{:S(2)}, u32[]{:S(2)}) collective-permute-start(bf16[3,6,128,128]{3,2,1,0:T(8,128)(2,1)S(1)} %get-tuple-element.38.refs_0_.refs_2_), channel_id=1, source_target_pairs={{0,8},{4,12},{24,16},{28,20},{1,9},{5,13},{25,17},{29,21},{2,10},{... | collective-permute-start | bytes 1769480 | tf_op jit(solution)/shard_map/ppermute | solution.py:394
  74.0 13.4 %collective-permute-start.14 = (bf16[2,6,128,128]{3,2,1,0:T(8,128)(2,1)S(1)}, bf16[2,6,128,128]{3,2,1,0:T(8,128)(2,1)S(1)}, u32[]{:S(2)}, u32[]{:S(2)}) collective-permute-start(bf16[2,6,128,128]{3,2,1,0:T(8,128)(2,1)S(1)} %relay.6.refs_12_), channel_id=1, source_target_pairs={{8,16},{12,20},{16,8},{20,12},{9,17},{13,21},{17,9},{21,13},{10,18... | collective-permute-start | bytes 1179656 | tf_op jit(solution)/shard_map/ppermute | solution.py:394
  74.7 26.8 %collective-permute-start.9 = (bf16[1,256,1024]{2,1,0:T(8,128)(2,1)S(1)}, bf16[1,256,1024]{2,1,0:T(8,128)(2,1)S(1)}, u32[]{:S(2)}, u32[]{:S(2)}) collective-permute-start(bf16[1,256,1024]{2,1,0:T(8,128)(2,1)S(1)} %get-tuple-element.35), channel_id=1, source_target_pairs={{0,1},{1,0},{2,3},{3,2},{4,5},{5,4},{6,7},{7,6},{8,9},{9,8},{10,11... | collective-permute-start | bytes 1572872 | tf_op jit(solution)/shard_map/ppermute | solution.py:394
  80.2 23.0 %collective-permute-start.18 = (bf16[3,6,128,128]{3,2,1,0:T(8,128)(2,1)S(1)}, bf16[3,6,128,128]{3,2,1,0:T(8,128)(2,1)S(1)}, u32[]{:S(2)}, u32[]{:S(2)}) collective-permute-start(bf16[3,6,128,128]{3,2,1,0:T(8,128)(2,1)S(1)} %get-tuple-element.45.refs_0_.refs_2_), channel_id=1, source_target_pairs={{0,8},{4,12},{24,16},{28,20},{1,9},{5,13},{25,17},{29,21},{2,10},{... | collective-permute-start | bytes 1769480 | tf_op jit(solution)/shard_map/ppermute | solution.py:394
  87.7 13.7 %copy-start.8 = (bf16[2,256,1024]{2,1,0:T(8,128)(2,1)S(1)}, bf16[2,256,1024]{2,1,0:T(8,128)(2,1)}, u32[]{:S(2)}) copy-start(bf16[2,256,1024]{2,1,0:T(8,128)(2,1)} %copy-done.7) | copy-start | bytes 3145732
  87.7 23.2 %collective-permute-start.17 = (bf16[2,6,128,128]{3,2,1,0:T(8,128)(2,1)S(1)}, bf16[2,6,128,128]{3,2,1,0:T(8,128)(2,1)S(1)}, u32[]{:S(2)}, u32[]{:S(2)}) collective-permute-start(bf16[2,6,128,128]{3,2,1,0:T(8,128)(2,1)S(1)} %get-tuple-element.42.refs_12_), channel_id=1, source_target_pairs={{8,16},{12,20},{16,8},{20,12},{9,17},{13,21},{17,9},{21,13},{10,18... | collective-permute-start | bytes 1179656 | tf_op jit(solution)/shard_map/ppermute | solution.py:394
  94.1 23.2 %collective-permute-start.21 = (bf16[3,6,128,128]{3,2,1,0:T(8,128)(2,1)S(1)}, bf16[3,6,128,128]{3,2,1,0:T(8,128)(2,1)S(1)}, u32[]{:S(2)}, u32[]{:S(2)}) collective-permute-start(bf16[3,6,128,128]{3,2,1,0:T(8,128)(2,1)S(1)} %get-tuple-element.49.refs_0_), channel_id=1, source_target_pairs={{0,8},{4,12},{24,16},{28,20},{1,9},{5,13},{25,17},{29,21},{2,10},{... | collective-permute-start | bytes 1769480 | tf_op jit(solution)/shard_map/ppermute | solution.py:394
  101.4 20.3 %collective-permute-start.8 = (bf16[1,256,1024]{2,1,0:T(8,128)(2,1)S(1)}, bf16[1,256,1024]{2,1,0:T(8,128)(2,1)S(1)}, u32[]{:S(2)}, u32[]{:S(2)}) collective-permute-start(bf16[1,256,1024]{2,1,0:T(8,128)(2,1)S(1)} %get-tuple-element.34), channel_id=1, source_target_pairs={{0,1},{1,0},{2,3},{3,2},{4,5},{5,4},{6,7},{7,6},{8,9},{9,8},{10,11... | collective-permute-start | bytes 1572872 | tf_op jit(solution)/shard_map/ppermute | solution.py:394
  101.7 21.2 %collective-permute-start.15 = (bf16[1,256,1024]{2,1,0:T(8,128)(2,1)S(1)}, bf16[1,256,1024]{2,1,0:T(8,128)(2,1)S(1)}, u32[]{:S(2)}, u32[]{:S(2)}) collective-permute-start(bf16[1,256,1024]{2,1,0:T(8,128)(2,1)S(1)} %relay.8.refs_12_), channel_id=1, source_target_pairs={{0,2},{1,3},{2,0},{3,1},{4,6},{5,7},{6,4},{7,5},{8,10},{9,11},{10,... | collective-permute-start | bytes 1572872 | tf_op jit(solution)/shard_map/ppermute | solution.py:394
  103.2 8.9 %collective-permute-start.16 = (bf16[1,6,128,128]{3,2,1,0:T(8,128)(2,1)S(1)}, bf16[1,6,128,128]{3,2,1,0:T(8,128)(2,1)S(1)}, u32[]{:S(2)}, u32[]{:S(2)}) collective-permute-start(bf16[1,6,128,128]{3,2,1,0:T(8,128)(2,1)S(1)} %get-tuple-element.44), channel_id=1, source_target_pairs={{8,0},{12,4},{16,24},{20,28},{9,1},{13,5},{17,25},{21,29},{10,2},{... | collective-permute-start | bytes 589832 | tf_op jit(solution)/shard_map/ppermute | solution.py:394
  111.4 7.0 %collective-permute-start.20 = (bf16[2,6,128,128]{3,2,1,0:T(8,128)(2,1)S(1)}, bf16[2,6,128,128]{3,2,1,0:T(8,128)(2,1)S(1)}, u32[]{:S(2)}, u32[]{:S(2)}) collective-permute-start(bf16[2,6,128,128]{3,2,1,0:T(8,128)(2,1)S(1)} %get-tuple-element.48.refs_4_), channel_id=1, source_target_pairs={{8,16},{12,20},{16,8},{20,12},{9,17},{13,21},{17,9},{21,13},{10,18... | collective-permute-start | bytes 1179656 | tf_op jit(solution)/shard_map/ppermute | solution.py:394
  112.1 53.5 %collective-permute-start.25 = (bf16[8,128,128]{2,1,0:T(8,128)(2,1)S(1)}, bf16[8,128,128]{2,1,0:T(8,128)(2,1)S(1)}, u32[]{:S(2)}, u32[]{:S(2)}) collective-permute-start(bf16[8,128,128]{2,1,0:T(8,128)(2,1)S(1)} %get-tuple-element.52), channel_id=1, source_target_pairs={{0,8},{4,12},{8,16},{12,20},{16,24},{20,28},{24,0},{28,4},{1,9},{5... | collective-permute-start | bytes 786440 | tf_op jit(solution)/shard_map/ppermute | solution.py:394
  117.3 48.3 %collective-permute-start.26 = (bf16[8,128,128]{2,1,0:T(8,128)(2,1)S(1)}, bf16[8,128,128]{2,1,0:T(8,128)(2,1)S(1)}, u32[]{:S(2)}, u32[]{:S(2)}) collective-permute-start(bf16[8,128,128]{2,1,0:T(8,128)(2,1)S(1)} %get-tuple-element.53), channel_id=1, source_target_pairs={{0,16},{4,20},{8,24},{12,28},{16,0},{20,4},{24,8},{28,12},{1,17},{... | collective-permute-start | bytes 786440 | tf_op jit(solution)/shard_map/ppermute | solution.py:394
  118.3 47.3 %collective-permute-start.27 = (bf16[8,128,128]{2,1,0:T(8,128)(2,1)S(1)}, bf16[8,128,128]{2,1,0:T(8,128)(2,1)S(1)}, u32[]{:S(2)}, u32[]{:S(2)}) collective-permute-start(bf16[8,128,128]{2,1,0:T(8,128)(2,1)S(1)} %get-tuple-element.54), channel_id=1, source_target_pairs={{0,24},{4,28},{8,0},{12,4},{16,8},{20,12},{24,16},{28,20},{1,25},{... | collective-permute-start | bytes 786440 | tf_op jit(solution)/shard_map/ppermute | solution.py:394
  121.6 30.2 %collective-permute-start.19 = (bf16[1,6,128,128]{3,2,1,0:T(8,128)(2,1)S(1)}, bf16[1,6,128,128]{3,2,1,0:T(8,128)(2,1)S(1)}, u32[]{:S(2)}, u32[]{:S(2)}) collective-permute-start(bf16[1,6,128,128]{3,2,1,0:T(8,128)(2,1)S(1)} %get-tuple-element.47), channel_id=1, source_target_pairs={{8,0},{12,4},{16,24},{20,28},{9,1},{13,5},{17,25},{21,29},{10,2},{... | collective-permute-start | bytes 589832 | tf_op jit(solution)/shard_map/ppermute | solution.py:394
  122.9 31.0 %collective-permute-start.23 = (bf16[2,6,128,128]{3,2,1,0:T(8,128)(2,1)S(1)}, bf16[2,6,128,128]{3,2,1,0:T(8,128)(2,1)S(1)}, u32[]{:S(2)}, u32[]{:S(2)}) collective-permute-start(bf16[2,6,128,128]{3,2,1,0:T(8,128)(2,1)S(1)} %get-tuple-element.51.refs_2_), channel_id=1, source_target_pairs={{8,16},{12,20},{16,8},{20,12},{9,17},{13,21},{17,9},{21,13},{10,18... | collective-permute-start | bytes 1179656 | tf_op jit(solution)/shard_map/ppermute | solution.py:394
  151.8 9.6 %collective-permute-start.22 = (bf16[1,6,128,128]{3,2,1,0:T(8,128)(2,1)S(1)}, bf16[1,6,128,128]{3,2,1,0:T(8,128)(2,1)S(1)}, u32[]{:S(2)}, u32[]{:S(2)}) collective-permute-start(bf16[1,6,128,128]{3,2,1,0:T(8,128)(2,1)S(1)} %get-tuple-element.50), channel_id=1, source_target_pairs={{8,0},{12,4},{16,24},{20,28},{9,1},{13,5},{17,25},{21,29},{10,2},{... | collective-permute-start | bytes 589832 | tf_op jit(solution)/shard_map/ppermute | solution.py:394
  154.1 10.6 %collective-permute-start.24 = (bf16[1,6,128,128]{3,2,1,0:T(8,128)(2,1)S(1)}, bf16[1,6,128,128]{3,2,1,0:T(8,128)(2,1)S(1)}, u32[]{:S(2)}, u32[]{:S(2)}) collective-permute-start(bf16[1,6,128,128]{3,2,1,0:T(8,128)(2,1)S(1)} %relay.11), channel_id=1, source_target_pairs={{8,0},{12,4},{16,24},{20,28},{9,1},{13,5},{17,25},{21,29},{10,2},{... | collective-permute-start | bytes 589832 | tf_op jit(solution)/shard_map/ppermute | solution.py:394
  (11 other events, 24.6 us)

commit v2 on v1

--- a/solution.py
+++ b/solution.py
@@ -14,6 +14,10 @@
 PARAMS = pltpu.CompilerParams(
     dimension_semantics=("arbitrary",), vmem_limit_bytes=48 * 1024 * 1024
 )
+ALL = pltpu.CompilerParams(
+    dimension_semantics=("arbitrary",), vmem_limit_bytes=60 * 1024 * 1024
+)
+FEW = pltpu.CompilerParams(vmem_limit_bytes=1024 * 1024)
 STEP = 4
 
 
@@ -70,12 +74,6 @@
     return [jnp.where(z >= line // 2, line - 1 - d, d) * 2 + y for d in order]
 
 
-def direct_blocks(line):
-    r = lax.axis_index("replica")
-    z, y = r // 2, r % 2
-    return [lax.rem(z + n, line) * 2 + y for n in range(line)]
-
-
 def forward_column(x, w, cot):
     pre = jnp.dot(x, w, preferred_element_type=F32)
     sig = 1.0 / (1.0 + jnp.exp(-pre))
@@ -95,12 +93,11 @@
     return lambda i: jnp.clip(i, lo, hi) - lo
 
 
-def forward_kernel(nf, first, columns, fold, splits, *refs):
+def forward_kernel(nf, columns, fold, copies, *refs):
     rows, feats = refs[0], refs[1 : 1 + nf]
     w_ref, cot_ref = refs[1 + nf : 3 + nf]
     buf, tab, sems = refs[-3:]
-    delta_refs = refs[-3 - len(splits) : -3]
-    act_ref = refs[-4 - len(splits)]
+    act_ref, delta_ref, *cot_copies = refs[-5 - len(copies) : -3]
     step, depth, side = w_ref.shape
     per_column = depth // side
     here = pl.program_id(0)
@@ -110,44 +107,37 @@
         copy_in([feats], buf, rows, tab, sems)
 
     index = Index(tab, columns, per_column, fold, side)
-    done = []
     for i in range(step):
-        x = index.gather(buf, first + here * step + i, range(per_column))
+        x = index.gather(buf, here * step + i, range(per_column))
         lanes = slice(i * side, (i + 1) * side)
         pre, sig, delta = forward_column(x, w_ref[i], cot_ref[:, lanes])
         act_ref[:, lanes] = (pre * sig).astype(BF16)
-        done.append(delta)
-    row = jnp.concatenate(done, axis=1)
-    for ref, (lo, hi) in zip(delta_refs, ranges(splits, step)):
+        delta_ref[:, lanes] = delta
+    for ref, (lo, hi) in zip(cot_copies, copies):
 
         @pl.when((here >= lo) & (here <= hi))
         def _(ref=ref):
-            ref[...] = row
-
-
-def forward(rows, feats, weight, cotangent, fold, act, first, splits, step, after=()):
+            ref[...] = cot_ref[...]
+
+
+def forward(rows, feats, weight, cotangent, fold, step, parts=(), after=()):
     tokens, hidden = cotangent.shape
     columns, depth, side = weight.shape
     width = sum(f.shape[1] for f in feats)
-    base = first // step
-    args = [rows, *feats, weight, cotangent]
+    args = [rows, *feats, weight, cotangent, *after]
     ins = [ANY] * (1 + len(feats)) + [
-        pl.BlockSpec((step, depth, side), lambda i: (base + i, 0, 0)),
-        pl.BlockSpec((tokens, step * side), lambda i: (0, base + i)),
+        pl.BlockSpec((step, depth, side), lambda i: (i, 0, 0)),
+        pl.BlockSpec((tokens, step * side), lambda i: (0, i)),
     ]
-    aliases = {}
-    if act is not None:
-        aliases = {len(args): 0}
-        args.append(act)
-    args += after
     ins += [ANY] * (len(args) - len(ins))
-    outs = [pl.BlockSpec((tokens, step * side), lambda i: (0, base + i))]
-    for lo, hi in ranges(splits, step):
+    outs = [pl.BlockSpec((tokens, step * side), lambda i: (0, i))] * 2
+    copies = ranges(parts, step)[1:]
+    for lo, hi in copies:
         at = held_at(lo, hi)
         outs.append(pl.BlockSpec((tokens, step * side), lambda i, at=at: (0, at(i))))
     return pl.pallas_call(
-        functools.partial(forward_kernel, len(feats), first, columns, fold, splits),
-        grid=(sum(splits) // step,),
+        functools.partial(forward_kernel, len(feats), columns, fold, copies),
+        grid=(columns // step,),
         in_specs=ins,
         out_specs=outs,
         scratch_shapes=[
@@ -155,9 +145,8 @@
             pltpu.SMEM(rows.shape, jnp.int32),
             pltpu.SemaphoreType.DMA((1 + len(feats),)),
         ],
-        out_shape=[jax.ShapeDtypeStruct((tokens, hidden), BF16)]
-        + [jax.ShapeDtypeStruct((tokens, n * side), BF16) for n in splits],
-        input_output_aliases=aliases,
+        out_shape=[jax.ShapeDtypeStruct((tokens, hidden), BF16)] * 2
+        + [jax.ShapeDtypeStruct((tokens, n * side), BF16) for n in parts[1:]],
         compiler_params=PARAMS,
         name="forward",
     )(*args)
@@ -174,12 +163,11 @@
     ]
 
 
-def grads_kernel(nf, first, columns, fold, scale, line, direct, *refs):
+def grads_kernel(nf, first, columns, fold, scale, last, *refs):
     rows, mine, other = refs[0], refs[1 : 1 + nf], refs[1 + nf : 1 + 2 * nf]
     w_ref, delta_ref, cot_ref = refs[1 + 2 * nf : 4 + 2 * nf]
     buf, tab, sems = refs[-3:]
-    sends = refs[-3 - (line - 1 if direct else 1) : -3]
-    own_ref = refs[-4 - len(sends)]
+    own_ref, rest_ref, *home = refs[-6 if last else -5 : -3]
     step, depth, side = w_ref.shape
     per_column = depth // side
     tokens = cot_ref.shape[0]
@@ -190,7 +178,7 @@
         copy_in([mine, other], buf, rows, tab, sems)
 
     index = Index(tab, columns, per_column, fold, side)
-    ks = direct_blocks(line) if direct else staged_blocks(line)
+    ks = staged_blocks(1 + rest_ref.shape[0])
     pair = buf.at[pl.ds(tokens, tokens), :]
     done = []
     for i in range(step):
@@ -202,15 +190,13 @@
         blocks = block_grads(index, buf, ks, first + here * step + i, done[i], scale)
         own_ref[i] = blocks[0]
         for p, block in enumerate(blocks[1:]):
-            if direct:
-                sends[p][i] = block
-            else:
-                sends[0][p, i] = block
+            rest_ref[p, i] = block
+        if last:
+            home[0][0, i] = blocks[1]
 
 
 def grads(
-    rows, mine, other, weight, delta, cot_other, skip, count, fold, first, line, scale, direct,
-    after=(),
+    rows, mine, other, weight, delta, cot_other, skip, count, fold, first, line, scale, after=()
 ):
     tokens = delta.shape[0]
     columns, depth, side = weight.shape
@@ -226,13 +212,15 @@
     ins += [ANY] * (len(args) - len(ins))
     one = jax.ShapeDtypeStruct((count, side, side), BF16)
     one_spec = pl.BlockSpec((step, side, side), lambda i: (i, 0, 0))
-    if direct:
-        sends, send_specs = [one] * (line - 1), [one_spec] * (line - 1)
-    else:
-        sends = [jax.ShapeDtypeStruct((line - 1, count, side, side), BF16)]
-        send_specs = [pl.BlockSpec((line - 1, step, side, side), lambda i: (0, i, 0, 0))]
+    last = first + count == columns
+    piece = lambda n: jax.ShapeDtypeStruct((n, count, side, side), BF16)
+    piece_spec = lambda n: pl.BlockSpec((n, step, side, side), lambda i: (0, i, 0, 0))
+    sends, send_specs = [piece(line - 1)], [piece_spec(line - 1)]
+    if last:
+        sends.append(piece(1))
+        send_specs.append(piece_spec(1))
     return pl.pallas_call(
-        functools.partial(grads_kernel, len(mine), first, columns, fold, scale, line, direct),
+        functools.partial(grads_kernel, len(mine), first, columns, fold, scale, last),
         grid=(count // step,),
         in_specs=ins,
         out_specs=[one_spec, *send_specs],
@@ -338,31 +326,32 @@
     )(*args, *after)
 
 
-def cut_kernel(splits, x_ref, *refs):
-    refs = refs[-len(splits) :]
-    here = pl.program_id(0)
-    for ref, (lo, hi) in zip(refs, ranges(splits, 1)):
-
-        @pl.when((here >= lo) & (here <= hi))
-        def _(ref=ref):
-            ref[...] = x_ref[...]
-
-
-def cut(x, first, splits, width, after=()):
-    height = x.shape[0]
-    outs = []
-    for lo, hi in ranges(splits, 1):
-        at = held_at(lo, hi)
-        outs.append(pl.BlockSpec((height, width), lambda i, at=at: (0, at(i))))
+def cut_kernel(x_ref, whole_ref, rows_ref, out_ref, copy_ref):
+    del rows_ref
+    out_ref[...] = x_ref[...]
+    copy_ref[...] = whole_ref[...]
+
+
+def cut(x, width, whole, rows):
     return pl.pallas_call(
-        functools.partial(cut_kernel, splits),
-        grid=(sum(splits),),
-        in_specs=[pl.BlockSpec((height, width), lambda i: (0, first + i))] + [ANY] * len(after),
-        out_specs=outs,
-        out_shape=[jax.ShapeDtypeStruct((height, n * width), x.dtype) for n in splits],
-        compiler_params=PARAMS,
+        cut_kernel,
+        grid=(1,),
+        in_specs=[
+            pl.BlockSpec((x.shape[0], width), lambda i: (0, 0)),
+            pl.BlockSpec(whole.shape, lambda i: (0, 0)),
+            ANY,
+        ],
+        out_specs=[
+            pl.BlockSpec((x.shape[0], width), lambda i: (0, 0)),
+            pl.BlockSpec(whole.shape, lambda i: (0, 0)),
+        ],
+        out_shape=[
+            jax.ShapeDtypeStruct((x.shape[0], width), x.dtype),
+            jax.ShapeDtypeStruct(whole.shape, whole.dtype),
+        ],
+        compiler_params=ALL,
         name="cut",
-    )(x, *after)
+    )(x, whole, rows)
 
 
 def gate_kernel(*refs):
@@ -376,6 +365,7 @@
         out_specs=ANY,
         out_shape=jax.ShapeDtypeStruct(x.shape, x.dtype),
         input_output_aliases={0: 0},
+        compiler_params=FEW,
         name="gate",
     )(x, *after)
 
@@ -402,70 +392,72 @@
     outer_in = along([(0, 1), (3, 2)])
     middle = along([(1, 2), (2, 1)])
     outer_out = along([(1, 0), (2, 3)])
-    shifts = [along([(a, (a + n) % line) for a in range(line)]) for n in range(1, line)]
-
-    sizes = [c * columns // 32 for c in (6, 6, 6, 6, 8)]
+    beyond = along([(1, 3), (2, 0)])
+
+    sizes = [c * columns // 32 for c in (8, 8, 6, 6, 4)]
     firsts = [sum(sizes[:n]) for n in range(len(sizes))]
-    parts = [sizes[0], sizes[1] + sizes[2], sizes[3] + sizes[4]]
-    places = [(0, 0), (1, 0), (1, sizes[1]), (2, 0), (2, sizes[3])]
+    parts = [sizes[0], sizes[1], sizes[2] + sizes[3] + sizes[4]]
+    places = [(0, 0), (1, 0), (2, 0), (2, sizes[2]), (2, sizes[2] + sizes[3])]
 
     f0 = features
     f2 = chips(f0)
-    u0 = pairs(f0)
-    unit = math.gcd(*sizes)
-    cots = cut(cotangent, 0, [n // unit for n in parts], unit * side)
-    c0, c1, c2 = cs = [pairs(x) for x in cots]
+    cot0, sent = cut(cotangent, parts[0] * side, f0, rows)
+    u0 = pairs(sent)
+    c0 = pairs(cot0)
     f1 = cores(f0)
     f3 = cores(f2)
     u1 = cores(u0)
     u2 = chips(u0)
     mine = [f0, f1, f2, f3]
-    act, delta = forward(
-        rows, mine, weight, cotangent, fold, None, 0, (columns,), STEP, (cots[0],)
-    )
+    act, delta, cot1, cot2 = forward(rows, mine, weight, cotangent, fold, STEP, parts)
+    c1, c2 = pairs(cot1), pairs(cot2)
+    cs = [c0, c1, c2]
     u2 = gate(u2, delta, c0)
     u3 = cores(u2)
     other = [u0, u1, u2, u3]
 
-    def chunk(n, direct, *after):
+    def chunk(n, *after):
         part, skip = places[n]
         return grads(
             rows, mine, other, weight, delta, cs[part], skip, sizes[n], fold, firsts[n],
-            line, scale, direct, after,
+            line, scale, after,
         )
 
-    own0, rest0 = chunk(0, False)
+    own0, rest0 = chunk(0)
     got0 = outer_in(rest0)
+    own1, rest1 = chunk(1, own0)
+    got1 = outer_in(rest1)
     near, away0, away1 = dinput(
-        rows, weight, [delta], fold, ((0, 2), (1,), (3,)), held, STEP, (own0,)
+        rows, weight, [delta], fold, ((0, 2), (1,), (3,)), held, STEP, (own1,)
     )
     sib0, sib1 = cores(away0), cores(away1)
-    own1, rest1 = chunk(1, False, near)
-    got1 = outer_in(rest1)
-    (far0,) = relay((rest0, 1, got0, 1, 2), after=(own1,))
+    (far0,) = relay((rest0, 1, got0, 1, 2), after=(near,))
     across0 = middle(far0)
-    own2, rest2 = chunk(2, False, far0)
+    own2, rest2 = chunk(2, far0)
     got2 = outer_in(rest2)
-    far1, home0 = relay((rest1, 1, got1, 1, 2), (rest0, 0, across0, 1, 1), after=(own2,))
+    (xsum,) = relay((near, 1, sib1, 0, 1), after=(own2,))
+    xback = chips(xsum)
+    far1, home0 = relay((rest1, 1, got1, 1, 2), (rest0, 0, across0, 1, 1), after=(xsum,))
     across1 = middle(far1)
     back0 = outer_out(home0)
-    own3, rest3 = chunk(3, False, far1)
+    own3, rest3 = chunk(3, far1)
     got3 = outer_in(rest3)
-    (xsum,) = relay((near, 1, sib1, 0, 1), after=(own3,))
-    xback = chips(xsum)
-    own4, *sends = chunk(4, True, xsum)
-    arrived = [shift(x) for shift, x in zip(shifts, sends)]
-    far2, home1 = relay((rest2, 1, got2, 1, 2), (rest1, 0, across1, 1, 1), after=(own4,))
+    far2, home1 = relay((rest2, 1, got2, 1, 2), (rest1, 0, across1, 1, 1), after=(own3,))
     across2 = middle(far2)
     back1 = outer_out(home1)
-    far3, home2 = relay((rest3, 1, got3, 1, 2), (rest2, 0, across2, 1, 1), after=(far2,))
+    own4, rest4, home4 = chunk(4, far2)
+    got4 = outer_in(rest4)
+    back4 = outer_out(home4)
+    far3, home2 = relay((rest3, 1, got3, 1, 2), (rest2, 0, across2, 1, 1), after=(own4,))
     across3 = middle(far3)
     back2 = outer_out(home2)
-    (home3,) = relay((rest3, 0, across3, 1, 1), after=(far3,))
+    last0, last1 = relay((rest4, 1, got4, 1, 1), (rest4, 2, got4, 2, 1), after=(far3,))
+    near4, far4 = middle(last0), beyond(last1)
+    (home3,) = relay((rest3, 0, across3, 1, 1), after=(last0,))
     back3 = outer_out(home3)
 
-    def total(own, got, across, back):
-        return own.astype(F32) + got[0].astype(F32) + across[0].astype(F32) + back[0].astype(F32)
+    def total(own, got, *more):
+        return own.astype(F32) + got[0].astype(F32) + sum(x[0].astype(F32) for x in more)
 
     weight_grad = jnp.concatenate(
         [
@@ -473,7 +465,7 @@
             total(own1, got1, across1, back1),
             total(own2, got2, across2, back2),
             total(own3, got3, across3, back3),
-            own4.astype(F32) + sum(x.astype(F32) for x in arrived),
+            total(own4, got4, near4, far4, back4),
         ],
         axis=0,
     )
@@ -494,7 +486,7 @@
     local_rows = lax.dynamic_slice_in_dim(rows_index, first, columns, 0)
     rows = rows_index.reshape(-1)
     step = math.gcd(columns, STEP)
-    act, delta = forward(rows, [whole], weight, cotangent, 0, None, 0, (columns,), step)
+    act, delta = forward(rows, [whole], weight, cotangent, 0, step)
     (part,) = dinput(rows, weight, [delta], 0, ((0,),), whole.shape[1], step)
     input_grad = lax.psum_scatter(part[0], "shard", scatter_dimension=1, tiled=True)
     blocks = whole.reshape(tokens, block_rows, side)[:, local_rows]

time: 168 us -> 137 us (0.82)
  waiting for transfers between devices: 52.2 us -> 27.2 us
  starting transfers between devices: 42.2 us -> 52.1 us
  local copies, waits for them, and re-layouts: 10.4 us -> 2.82 us
  Pallas kernels: 55.4 us -> 51.4 us
  other arithmetic: 5.37 us -> 1.6 us
    ppermute x28 -> x29, waiting for transfers between devices: 52.2 us -> 27.2 us  [permute(): return lambda x: lax.ppermute(x, axis, links)]
    ppermute x28 -> x29, starting transfers between devices: 42.2 us -> 52.1 us  [permute(): return lambda x: lax.ppermute(x, axis, links)]
    unnamed x31 -> x19, local copies, waits for them, and re-layouts: 9.43 us -> 2.14 us
    pallas_call x5, Pallas kernels: 28.2 us -> 24.1 us  [grads(): pl.pallas_call(functools.partial(grads_kernel, len(mine), first, columns,...]
    unnamed x4, other arithmetic: 3.38 us -> 0.45 us
  transfers between devices with their start and end apart: 28 -> 29, of which waited for: 7 -> 7; matrix products, arithmetic and copies ran while one was open for 4% -> 2% of each run, Pallas kernels for 33% -> 38%
where the time goes in v2:
time: 137 us; the launch traced here: 136 us
  starting transfers between devices  52.1 us (38%)
  Pallas kernels  51.4 us (38%)
  waiting for transfers between devices  27.2 us (20%)
  local copies, waits for them, and re-layouts  2.82 us (2%)
  other arithmetic  1.6 us (1%)
    ppermute x29, starting transfers between devices, permute(): return lambda x: lax.ppermute(x, axis, links)  52.1 us
    ppermute x29, waiting for transfers between devices, permute(): return lambda x: lax.ppermute(x, axis, links)  27.2 us
    pallas_call x5, Pallas kernels, grads(): pl.pallas_call(functools.partial(grads_kernel, len(mine), first, columns,...  24.1 us
    pallas_call x1, Pallas kernels, forward(): pl.pallas_call(functools.partial(forward_kernel, len(feats), columns, fol...  12.2 us
    pallas_call x1, Pallas kernels, dinput(): pl.pallas_call(functools.partial(dinput_kernel, len(deltas), fold, groups...  10.6 us
  transfers between devices with their start and end apart: 29, of which 7 were waited for; matrix products, arithmetic and copies ran while one was open for 2% of the time, Pallas kernels for 38%

profile of v2, /device:TPU:0, one launch (start us, length us, event | category | flops | bytes accessed | tf_op | source)
XLA Modules:
  0.0 136.3 jit_solution(7796775939952323993)
XLA Ops:
  0.6 3.0 %collective-permute-start.1 = (bf16[256,1024]{1,0:T(8,128)(2,1)}, bf16[256,1024]{1,0:T(8,128)(2,1)S(1)}, u32[]{:S(2)}, u32[]{:S(2)}) collective-permute-start(bf16[256,1024]{1,0:T(8,128)(2,1)} %refs_1_.11), channel_id=1, source_target_pairs={{0,2},{1,3},{2,0},{3,1},{4,6},{5,7},{6,4},{7,5},{8,10},{9,11},{10,... | collective-permute-start | bytes 1572872 | tf_op jit(solution)/shard_map/ppermute | solution.py:384
  5.1 2.2 %cut.1 = (bf16[256,1024]{1,0:T(8,128)(2,1)}, bf16[256,1024]{1,0:T(8,128)(2,1)}) custom-call(bf16[256,4096]{1,0:T(8,128)(2,1)} %x_ref.1, bf16[256,1024]{1,0:T(8,128)(2,1)} %refs_1_.11, s32[1024]{0:T(1024)} %reshape.42.refs_0_.rows_ref), custom_call_target="tpu_custom_call" | custom-call | tf_op jit(solution)/shard_map/cut/pallas_call | solution.py:336
  7.3 1.5 %collective-permute-start.3 = (bf16[256,1024]{1,0:T(8,128)(2,1)}, bf16[256,1024]{1,0:T(8,128)(2,1)S(1)}, u32[]{:S(2)}, u32[]{:S(2)}) collective-permute-start(bf16[256,1024]{1,0:T(8,128)(2,1)} %get-tuple-element.33), channel_id=1, source_target_pairs={{0,4},{4,0},{8,12},{12,8},{16,20},{20,16},{24,28},{28,24},{1,5},{5... | collective-permute-start | bytes 1572872 | tf_op jit(solution)/shard_map/ppermute | solution.py:384
  8.9 6.9 %collective-permute-done.1.refs_3_ = bf16[256,1024]{1,0:T(8,128)(2,1)S(1)} collective-permute-done((bf16[256,1024]{1,0:T(8,128)(2,1)}, bf16[256,1024]{1,0:T(8,128)(2,1)S(1)}, u32[]{:S(2)}, u32[]{:S(2)}) %collective-permute-start.1) | collective-permute-done | bytes 524320 | tf_op jit(solution)/shard_map/ppermute | solution.py:384
  15.8 1.8 %collective-permute-start.6 = (bf16[256,1024]{1,0:T(8,128)(2,1)}, bf16[256,1024]{1,0:T(8,128)(2,1)S(1)}, u32[]{:S(2)}, u32[]{:S(2)}) collective-permute-start(bf16[256,1024]{1,0:T(8,128)(2,1)} %get-tuple-element.34), channel_id=1, source_target_pairs={{0,4},{4,0},{8,12},{12,8},{16,20},{20,16},{24,28},{28,24},{1,5},{5... | collective-permute-start | bytes 1572872 | tf_op jit(solution)/shard_map/ppermute | solution.py:384
  17.6 4.8 %collective-permute-done.3.refs_5_ = bf16[256,1024]{1,0:T(8,128)(2,1)S(1)} collective-permute-done((bf16[256,1024]{1,0:T(8,128)(2,1)}, bf16[256,1024]{1,0:T(8,128)(2,1)S(1)}, u32[]{:S(2)}, u32[]{:S(2)}) %collective-permute-start.3) | collective-permute-done | bytes 524320 | tf_op jit(solution)/shard_map/ppermute | solution.py:384
  22.4 12.2 %forward.1 = (bf16[256,4096]{1,0:T(8,128)(2,1)}, bf16[256,4096]{1,0:T(8,128)(2,1)S(1)}, bf16[256,1024]{1,0:T(8,128)(2,1)S(1)}, bf16[256,2048]{1,0:T(8,128)(2,1)S(1)}) custom-call(s32[1024]{0:T(1024)S(1)} %copy-done.7, bf16[256,1024]{1,0:T(8,128)(2,1)S(1)} %copy-done.2, bf16[256,1024]{1,0:T(8,128)(2,1)S(1)} %collective-permute-done.refs_2_, ...), custom_call_target="tpu_custom_call" | custom-call | tf_op jit(solution)/shard_map/forward/pallas_call | solution.py:138
  35.2 1.5 %collective-permute-start.8 = (bf16[256,1024]{1,0:T(8,128)(2,1)S(1)}, bf16[256,1024]{1,0:T(8,128)(2,1)S(1)}, u32[]{:S(2)}, u32[]{:S(2)}) collective-permute-start(bf16[256,1024]{1,0:T(8,128)(2,1)S(1)} %get-tuple-element.35), channel_id=1, source_target_pairs={{0,4},{4,0},{8,12},{12,8},{16,20},{20,16},{24,28},{28,24},{1,5},{5... | collective-permute-start | bytes 1572872 | tf_op jit(solution)/shard_map/ppermute | solution.py:384
  36.8 5.3 %grads.5 = (bf16[8,128,128]{2,1,0:T(8,128)(2,1)S(1)}, bf16[3,8,128,128]{3,2,1,0:T(8,128)(2,1)S(1)}) custom-call(s32[1024]{0:T(1024)S(1)} %copy-done.7, bf16[256,1024]{1,0:T(8,128)(2,1)S(1)} %copy-done.2, bf16[256,1024]{1,0:T(8,128)(2,1)S(1)} %collective-permute-done.refs_2_, bf16[256,1024]{1,0:T(8,128)(2,1)S(1)} %collective-permute-done.1.refs_3_, ...), custom_call_target="tpu_custom_call" | custom-call | tf_op jit(solution)/shard_map/grads/pallas_call | solution.py:222
  42.1 3.6 %collective-permute-start.12 = (bf16[3,8,128,128]{3,2,1,0:T(8,128)(2,1)S(1)}, bf16[3,8,128,128]{3,2,1,0:T(8,128)(2,1)S(1)}, u32[]{:S(2)}, u32[]{:S(2)}) collective-permute-start(bf16[3,8,128,128]{3,2,1,0:T(8,128)(2,1)S(1)} %get-tuple-element.42.refs_0_.refs_2_), channel_id=1, source_target_pairs={{0,8},{4,12},{24,16},{28,20},{1,9},{5,13},{25,17},{29,21},{2,10},{... | collective-permute-start | bytes 2359304 | tf_op jit(solution)/shard_map/ppermute | solution.py:384
  45.7 1.6 %collective-permute-start.11 = (bf16[256,2048]{1,0:T(8,128)(2,1)S(1)}, bf16[256,2048]{1,0:T(8,128)(2,1)}, u32[]{:S(2)}, u32[]{:S(2)}) collective-permute-start(bf16[256,2048]{1,0:T(8,128)(2,1)S(1)} %get-tuple-element.41), channel_id=1, source_target_pairs={{0,4},{4,0},{8,12},{12,8},{16,20},{20,16},{24,28},{28,24},{1,5},{5... | collective-permute-start | bytes 3145736 | tf_op jit(solution)/shard_map/ppermute | solution.py:384
  47.2 2.6 %collective-permute-done.8.refs_11_ = bf16[256,1024]{1,0:T(8,128)(2,1)S(1)} collective-permute-done((bf16[256,1024]{1,0:T(8,128)(2,1)S(1)}, bf16[256,1024]{1,0:T(8,128)(2,1)S(1)}, u32[]{:S(2)}, u32[]{:S(2)}) %collective-permute-start.8) | collective-permute-done | bytes 524320 | tf_op jit(solution)/shard_map/ppermute | solution.py:384
  49.8 5.4 %grads.6 = (bf16[8,128,128]{2,1,0:T(8,128)(2,1)S(1)}, bf16[3,8,128,128]{3,2,1,0:T(8,128)(2,1)S(1)}) custom-call(s32[1024]{0:T(1024)S(1)} %copy-done.7, bf16[256,1024]{1,0:T(8,128)(2,1)S(1)} %copy-done.2, bf16[256,1024]{1,0:T(8,128)(2,1)S(1)} %collective-permute-done.refs_2_, bf16[256,1024]{1,0:T(8,128)(2,1)S(1)} %collective-permute-done.1.refs_3_, ...), custom_call_target="tpu_custom_call" | custom-call | tf_op jit(solution)/shard_map/grads/pallas_call | solution.py:222
  55.3 3.7 %collective-permute-start.15 = (bf16[3,8,128,128]{3,2,1,0:T(8,128)(2,1)S(1)}, bf16[3,8,128,128]{3,2,1,0:T(8,128)(2,1)S(1)}, u32[]{:S(2)}, u32[]{:S(2)}) collective-permute-start(bf16[3,8,128,128]{3,2,1,0:T(8,128)(2,1)S(1)} %get-tuple-element.44.refs_0_.refs_2_), channel_id=1, source_target_pairs={{0,8},{4,12},{24,16},{28,20},{1,9},{5,13},{25,17},{29,21},{2,10},{... | collective-permute-start | bytes 2359304 | tf_op jit(solution)/shard_map/ppermute | solution.py:384
  59.0 10.6 %dinput.1 = (bf16[2,256,1024]{2,1,0:T(8,128)(2,1)S(1)}, bf16[1,256,1024]{2,1,0:T(8,128)(2,1)S(1)}, bf16[1,256,1024]{2,1,0:T(8,128)(2,1)S(1)}) custom-call(s32[1024]{0:T(1024)S(1)} %copy-done.7, bf16[256,4096]{1,0:T(8,128)(2,1)S(1)} %copy-done.1, bf16[32,1024,128]{2,1,0:T(8,128)(2,1)} %refs_9_.9, bf16[8,128,128]{2,1,0:T(8,128)(2,1)S(1)} %get-tuple-element.37.refs_3_), custom_call_target="tpu_custom_call" | custom-call | tf_op jit(solution)/shard_map/dinput/pallas_call | solution.py:275
  71.7 4.8 %grads.7 = (bf16[6,128,128]{2,1,0:T(8,128)(2,1)S(1)}, bf16[3,6,128,128]{3,2,1,0:T(8,128)(2,1)S(1)}) custom-call(s32[1024]{0:T(1024)S(1)} %copy-done.7, bf16[256,1024]{1,0:T(8,128)(2,1)S(1)} %copy-done.2, bf16[256,1024]{1,0:T(8,128)(2,1)S(1)} %collective-permute-done.refs_2_, bf16[256,1024]{1,0:T(8,128)(2,1)S(1)} %collective-permute-done.1.refs_3_, ...), custom_call_target="tpu_custom_call" | custom-call | tf_op jit(solution)/shard_map/grads/pallas_call | solution.py:222
  76.6 3.5 %collective-permute-start.18 = (bf16[3,6,128,128]{3,2,1,0:T(8,128)(2,1)S(1)}, bf16[3,6,128,128]{3,2,1,0:T(8,128)(2,1)S(1)}, u32[]{:S(2)}, u32[]{:S(2)}) collective-permute-start(bf16[3,6,128,128]{3,2,1,0:T(8,128)(2,1)S(1)} %get-tuple-element.47.refs_0_.refs_2_), channel_id=1, source_target_pairs={{0,8},{4,12},{24,16},{28,20},{1,9},{5,13},{25,17},{29,21},{2,10},{... | collective-permute-start | bytes 1769480 | tf_op jit(solution)/shard_map/ppermute | solution.py:384
  81.7 2.1 %collective-permute-start.13 = (bf16[1,256,1024]{2,1,0:T(8,128)(2,1)S(1)}, bf16[1,256,1024]{2,1,0:T(8,128)(2,1)S(1)}, u32[]{:S(2)}, u32[]{:S(2)}) collective-permute-start(bf16[1,256,1024]{2,1,0:T(8,128)(2,1)S(1)} %relay.8.refs_4_), channel_id=1, source_target_pairs={{0,2},{1,3},{2,0},{3,1},{4,6},{5,7},{6,4},{7,5},{8,10},{9,11},{10,... | collective-permute-start | bytes 1572872 | tf_op jit(solution)/shard_map/ppermute | solution.py:384
  83.7 4.8 %grads.8 = (bf16[6,128,128]{2,1,0:T(8,128)(2,1)S(1)}, bf16[3,6,128,128]{3,2,1,0:T(8,128)(2,1)S(1)}) custom-call(s32[1024]{0:T(1024)S(1)} %copy-done.7, bf16[256,1024]{1,0:T(8,128)(2,1)S(1)} %copy-done.2, bf16[256,1024]{1,0:T(8,128)(2,1)S(1)} %collective-permute-done.refs_2_, bf16[256,1024]{1,0:T(8,128)(2,1)S(1)} %collective-permute-done.1.refs_3_, ...), custom_call_target="tpu_custom_call" | custom-call | tf_op jit(solution)/shard_map/grads/pallas_call | solution.py:222
  88.6 9.9 %collective-permute-start.21 = (bf16[3,6,128,128]{3,2,1,0:T(8,128)(2,1)S(1)}, bf16[3,6,128,128]{3,2,1,0:T(8,128)(2,1)S(1)}, u32[]{:S(2)}, u32[]{:S(2)}) collective-permute-start(bf16[3,6,128,128]{3,2,1,0:T(8,128)(2,1)S(1)} %get-tuple-element.51.refs_0_), channel_id=1, source_target_pairs={{0,8},{4,12},{24,16},{28,20},{1,9},{5,13},{25,17},{29,21},{2,10},{... | collective-permute-start | bytes 1769480 | tf_op jit(solution)/shard_map/ppermute | solution.py:384
  99.7 1.3 collective-permute-start.16
  102.1 1.5 %collective-permute-start.19 = (bf16[1,8,128,128]{3,2,1,0:T(8,128)(2,1)S(1)}, bf16[1,8,128,128]{3,2,1,0:T(8,128)(2,1)S(1)}, u32[]{:S(2)}, u32[]{:S(2)}) collective-permute-start(bf16[1,8,128,128]{3,2,1,0:T(8,128)(2,1)S(1)} %get-tuple-element.49), channel_id=1, source_target_pairs={{8,0},{12,4},{16,24},{20,28},{9,1},{13,5},{17,25},{21,29},{10,2},{... | collective-permute-start | bytes 786440 | tf_op jit(solution)/shard_map/ppermute | solution.py:384
  103.5 3.7 %grads.9 = (bf16[4,128,128]{2,1,0:T(8,128)(2,1)S(1)}, bf16[3,4,128,128]{3,2,1,0:T(8,128)(2,1)S(1)}, bf16[1,4,128,128]{3,2,1,0:T(8,128)(2,1)S(1)}) custom-call(s32[1024]{0:T(1024)S(1)} %copy-done.7, bf16[256,1024]{1,0:T(8,128)(2,1)S(1)} %copy-done.2, bf16[256,1024]{1,0:T(8,128)(2,1)S(1)} %collective-permute-done.refs_2_, ...), custom_call_target="tpu_custom_call" | custom-call | tf_op jit(solution)/shard_map/grads/pallas_call | solution.py:222
  107.2 7.8 %collective-permute-start.24 = (bf16[3,4,128,128]{3,2,1,0:T(8,128)(2,1)S(1)}, bf16[3,4,128,128]{3,2,1,0:T(8,128)(2,1)S(1)}, u32[]{:S(2)}, u32[]{:S(2)}) collective-permute-start(bf16[3,4,128,128]{3,2,1,0:T(8,128)(2,1)S(1)} %get-tuple-element.55.refs_0_.refs_2_), channel_id=1, source_target_pairs={{0,8},{4,12},{24,16},{28,20},{1,9},{5,13},{25,17},{29,21},{2,10},{... | collective-permute-start | bytes 1179656 | tf_op jit(solution)/shard_map/ppermute | solution.py:384
  116.3 1.3 collective-permute-start.28
  117.6 1.3 collective-permute-start.22
  119.1 3.0 %collective-permute-done.24.refs_1_.refs_3_ = bf16[3,4,128,128]{3,2,1,0:T(8,128)(2,1)S(1)} collective-permute-done((bf16[3,4,128,128]{3,2,1,0:T(8,128)(2,1)S(1)}, bf16[3,4,128,128]{3,2,1,0:T(8,128)(2,1)S(1)}, u32[]{:S(2)}, u32[]{:S(2)}) %collective-permute-start.24) | collective-permute-done | bytes 393248 | tf_op jit(solution)/shard_map/ppermute | solution.py:384
  122.3 1.3 collective-permute-start.27
  124.5 1.3 collective-permute-start.25
  125.8 1.7 %collective-permute-done.22 = bf16[1,6,128,128]{3,2,1,0:T(8,128)(2,1)S(1)} collective-permute-done((bf16[1,6,128,128]{3,2,1,0:T(8,128)(2,1)S(1)}, bf16[1,6,128,128]{3,2,1,0:T(8,128)(2,1)S(1)}, u32[]{:S(2)}, u32[]{:S(2)}) %collective-permute-start.22) | collective-permute-done | bytes 196640 | tf_op jit(solution)/shard_map/ppermute | solution.py:384
  127.6 7.2 %collective-permute-done.25 = bf16[1,6,128,128]{3,2,1,0:T(8,128)(2,1)S(1)} collective-permute-done((bf16[1,6,128,128]{3,2,1,0:T(8,128)(2,1)S(1)}, bf16[1,6,128,128]{3,2,1,0:T(8,128)(2,1)S(1)}, u32[]{:S(2)}, u32[]{:S(2)}) %collective-permute-start.25) | collective-permute-done | bytes 196640 | tf_op jit(solution)/shard_map/ppermute | solution.py:384
  135.0 1.3 copy-done.8
  (68 shorter events, 10.6 us)
Async XLA Ops:
  0.6 15.1 %collective-permute-start.1 = (bf16[256,1024]{1,0:T(8,128)(2,1)}, bf16[256,1024]{1,0:T(8,128)(2,1)S(1)}, u32[]{:S(2)}, u32[]{:S(2)}) collective-permute-start(bf16[256,1024]{1,0:T(8,128)(2,1)} %refs_1_.11), channel_id=1, source_target_pairs={{0,2},{1,3},{2,0},{3,1},{4,6},{5,7},{6,4},{7,5},{8,10},{9,11},{10,... | collective-permute-start | bytes 1572872 | tf_op jit(solution)/shard_map/ppermute | solution.py:384
  5.1 17.3 %copy-start.7 = (s32[1024]{0:T(1024)S(1)}, s32[1024]{0:T(1024)}, u32[]{:S(2)}) copy-start(s32[1024]{0:T(1024)} %reshape.42.refs_0_.rows_ref) | copy-start | bytes 12292
  7.3 15.1 %collective-permute-start.3 = (bf16[256,1024]{1,0:T(8,128)(2,1)}, bf16[256,1024]{1,0:T(8,128)(2,1)S(1)}, u32[]{:S(2)}, u32[]{:S(2)}) collective-permute-start(bf16[256,1024]{1,0:T(8,128)(2,1)} %get-tuple-element.33), channel_id=1, source_target_pairs={{0,4},{4,0},{8,12},{12,8},{16,20},{20,16},{24,28},{28,24},{1,5},{5... | collective-permute-start | bytes 1572872 | tf_op jit(solution)/shard_map/ppermute | solution.py:384
  8.9 13.5 %collective-permute-start = (bf16[256,1024]{1,0:T(8,128)(2,1)S(1)}, bf16[256,1024]{1,0:T(8,128)(2,1)S(1)}, u32[]{:S(2)}, u32[]{:S(2)}) collective-permute-start(bf16[256,1024]{1,0:T(8,128)(2,1)S(1)} %copy-done.2), channel_id=1, source_target_pairs={{0,1},{1,0},{2,3},{3,2},{4,5},{5,4},{6,7},{7,6},{8,9},{9,8},{10,11... | collective-permute-start | bytes 1572872 | tf_op jit(solution)/shard_map/ppermute | solution.py:384
  15.8 6.6 %collective-permute-start.2 = (bf16[256,1024]{1,0:T(8,128)(2,1)S(1)}, bf16[256,1024]{1,0:T(8,128)(2,1)S(1)}, u32[]{:S(2)}, u32[]{:S(2)}) collective-permute-start(bf16[256,1024]{1,0:T(8,128)(2,1)S(1)} %collective-permute-done.1.refs_3_), channel_id=1, source_target_pairs={{0,1},{1,0},{2,3},{3,2},{4,5},{5,4},{6,7},{7,6},{8,9},{9,8},{10,11... | collective-permute-start | bytes 1572872 | tf_op jit(solution)/shard_map/ppermute | solution.py:384
  15.8 18.8 %collective-permute-start.6 = (bf16[256,1024]{1,0:T(8,128)(2,1)}, bf16[256,1024]{1,0:T(8,128)(2,1)S(1)}, u32[]{:S(2)}, u32[]{:S(2)}) collective-permute-start(bf16[256,1024]{1,0:T(8,128)(2,1)} %get-tuple-element.34), channel_id=1, source_target_pairs={{0,4},{4,0},{8,12},{12,8},{16,20},{20,16},{24,28},{28,24},{1,5},{5... | collective-permute-start | bytes 1572872 | tf_op jit(solution)/shard_map/ppermute | solution.py:384
  22.4 12.2 %collective-permute-start.5 = (bf16[256,1024]{1,0:T(8,128)(2,1)S(1)}, bf16[256,1024]{1,0:T(8,128)(2,1)S(1)}, u32[]{:S(2)}, u32[]{:S(2)}) collective-permute-start(bf16[256,1024]{1,0:T(8,128)(2,1)S(1)} %collective-permute-done.3.refs_5_), channel_id=1, source_target_pairs={{0,2},{1,3},{2,0},{3,1},{4,6},{5,7},{6,4},{7,5},{8,10},{9,11},{10,... | collective-permute-start | bytes 1572872 | tf_op jit(solution)/shard_map/ppermute | solution.py:384
  22.4 14.4 %collective-permute-start.4 = (bf16[256,1024]{1,0:T(8,128)(2,1)S(1)}, bf16[256,1024]{1,0:T(8,128)(2,1)S(1)}, u32[]{:S(2)}, u32[]{:S(2)}) collective-permute-start(bf16[256,1024]{1,0:T(8,128)(2,1)S(1)} %collective-permute-done.3.refs_5_), channel_id=1, source_target_pairs={{0,1},{1,0},{2,3},{3,2},{4,5},{5,4},{6,7},{7,6},{8,9},{9,8},{10,11... | collective-permute-start | bytes 1572872 | tf_op jit(solution)/shard_map/ppermute | solution.py:384
  34.7 2.1 %collective-permute-start.7 = (bf16[256,1024]{1,0:T(8,128)(2,1)S(1)}, bf16[256,1024]{1,0:T(8,128)(2,1)S(1)}, u32[]{:S(2)}, u32[]{:S(2)}) collective-permute-start(bf16[256,1024]{1,0:T(8,128)(2,1)S(1)} %gate.1.refs_7_), channel_id=1, source_target_pairs={{0,1},{1,0},{2,3},{3,2},{4,5},{5,4},{6,7},{7,6},{8,9},{9,8},{10,11... | collective-permute-start | bytes 1572872 | tf_op jit(solution)/shard_map/ppermute | solution.py:384
  35.2 14.6 %collective-permute-start.8 = (bf16[256,1024]{1,0:T(8,128)(2,1)S(1)}, bf16[256,1024]{1,0:T(8,128)(2,1)S(1)}, u32[]{:S(2)}, u32[]{:S(2)}) collective-permute-start(bf16[256,1024]{1,0:T(8,128)(2,1)S(1)} %get-tuple-element.35), channel_id=1, source_target_pairs={{0,4},{4,0},{8,12},{12,8},{16,20},{20,16},{24,28},{28,24},{1,5},{5... | collective-permute-start | bytes 1572872 | tf_op jit(solution)/shard_map/ppermute | solution.py:384
  42.1 13.2 %copy-start.3 = (bf16[8,128,128]{2,1,0:T(8,128)(2,1)}, bf16[8,128,128]{2,1,0:T(8,128)(2,1)S(1)}, u32[]{:S(2)}) copy-start(bf16[8,128,128]{2,1,0:T(8,128)(2,1)S(1)} %get-tuple-element.36.refs_12_) | copy-start | bytes 786436
  42.1 27.6 %collective-permute-start.12 = (bf16[3,8,128,128]{3,2,1,0:T(8,128)(2,1)S(1)}, bf16[3,8,128,128]{3,2,1,0:T(8,128)(2,1)S(1)}, u32[]{:S(2)}, u32[]{:S(2)}) collective-permute-start(bf16[3,8,128,128]{3,2,1,0:T(8,128)(2,1)S(1)} %get-tuple-element.42.refs_0_.refs_2_), channel_id=1, source_target_pairs={{0,8},{4,12},{24,16},{28,20},{1,9},{5,13},{25,17},{29,21},{2,10},{... | collective-permute-start | bytes 2359304 | tf_op jit(solution)/shard_map/ppermute | solution.py:384
  45.7 26.1 %collective-permute-start.11 = (bf16[256,2048]{1,0:T(8,128)(2,1)S(1)}, bf16[256,2048]{1,0:T(8,128)(2,1)}, u32[]{:S(2)}, u32[]{:S(2)}) collective-permute-start(bf16[256,2048]{1,0:T(8,128)(2,1)S(1)} %get-tuple-element.41), channel_id=1, source_target_pairs={{0,4},{4,0},{8,12},{12,8},{16,20},{20,16},{24,28},{28,24},{1,5},{5... | collective-permute-start | bytes 3145736 | tf_op jit(solution)/shard_map/ppermute | solution.py:384
  55.3 14.4 %copy-start.5 = (bf16[8,128,128]{2,1,0:T(8,128)(2,1)}, bf16[8,128,128]{2,1,0:T(8,128)(2,1)S(1)}, u32[]{:S(2)}) copy-start(bf16[8,128,128]{2,1,0:T(8,128)(2,1)S(1)} %get-tuple-element.37.refs_3_) | copy-start | bytes 786436
  55.3 25.1 %collective-permute-start.15 = (bf16[3,8,128,128]{3,2,1,0:T(8,128)(2,1)S(1)}, bf16[3,8,128,128]{3,2,1,0:T(8,128)(2,1)S(1)}, u32[]{:S(2)}, u32[]{:S(2)}) collective-permute-start(bf16[3,8,128,128]{3,2,1,0:T(8,128)(2,1)S(1)} %get-tuple-element.44.refs_0_.refs_2_), channel_id=1, source_target_pairs={{0,8},{4,12},{24,16},{28,20},{1,9},{5,13},{25,17},{29,21},{2,10},{... | collective-permute-start | bytes 2359304 | tf_op jit(solution)/shard_map/ppermute | solution.py:384
  69.7 10.4 %collective-permute-start.10 = (bf16[1,256,1024]{2,1,0:T(8,128)(2,1)S(1)}, bf16[1,256,1024]{2,1,0:T(8,128)(2,1)S(1)}, u32[]{:S(2)}, u32[]{:S(2)}) collective-permute-start(bf16[1,256,1024]{2,1,0:T(8,128)(2,1)S(1)} %get-tuple-element.40), channel_id=1, source_target_pairs={{0,1},{1,0},{2,3},{3,2},{4,5},{5,4},{6,7},{7,6},{8,9},{9,8},{10,11... | collective-permute-start | bytes 1572872 | tf_op jit(solution)/shard_map/ppermute | solution.py:384
  70.1 10.3 %collective-permute-start.14 = (bf16[2,8,128,128]{3,2,1,0:T(8,128)(2,1)S(1)}, bf16[2,8,128,128]{3,2,1,0:T(8,128)(2,1)S(1)}, u32[]{:S(2)}, u32[]{:S(2)}) collective-permute-start(bf16[2,8,128,128]{3,2,1,0:T(8,128)(2,1)S(1)} %relay.7.refs_12_), channel_id=1, source_target_pairs={{8,16},{12,20},{16,8},{20,12},{9,17},{13,21},{17,9},{21,13},{10,18... | collective-permute-start | bytes 1572872 | tf_op jit(solution)/shard_map/ppermute | solution.py:384
  76.6 22.0 %collective-permute-start.18 = (bf16[3,6,128,128]{3,2,1,0:T(8,128)(2,1)S(1)}, bf16[3,6,128,128]{3,2,1,0:T(8,128)(2,1)S(1)}, u32[]{:S(2)}, u32[]{:S(2)}) collective-permute-start(bf16[3,6,128,128]{3,2,1,0:T(8,128)(2,1)S(1)} %get-tuple-element.47.refs_0_.refs_2_), channel_id=1, source_target_pairs={{0,8},{4,12},{24,16},{28,20},{1,9},{5,13},{25,17},{29,21},{2,10},{... | collective-permute-start | bytes 1769480 | tf_op jit(solution)/shard_map/ppermute | solution.py:384
  80.9 17.7 %collective-permute-start.17 = (bf16[2,8,128,128]{3,2,1,0:T(8,128)(2,1)S(1)}, bf16[2,8,128,128]{3,2,1,0:T(8,128)(2,1)S(1)}, u32[]{:S(2)}, u32[]{:S(2)}) collective-permute-start(bf16[2,8,128,128]{3,2,1,0:T(8,128)(2,1)S(1)} %get-tuple-element.46.refs_12_), channel_id=1, source_target_pairs={{8,16},{12,20},{16,8},{20,12},{9,17},{13,21},{17,9},{21,13},{10,18... | collective-permute-start | bytes 1572872 | tf_op jit(solution)/shard_map/ppermute | solution.py:384
  81.6 19.4 %collective-permute-start.9 = (bf16[1,256,1024]{2,1,0:T(8,128)(2,1)S(1)}, bf16[1,256,1024]{2,1,0:T(8,128)(2,1)S(1)}, u32[]{:S(2)}, u32[]{:S(2)}) collective-permute-start(bf16[1,256,1024]{2,1,0:T(8,128)(2,1)S(1)} %get-tuple-element.39), channel_id=1, source_target_pairs={{0,1},{1,0},{2,3},{3,2},{4,5},{5,4},{6,7},{7,6},{8,9},{9,8},{10,11... | collective-permute-start | bytes 1572872 | tf_op jit(solution)/shard_map/ppermute | solution.py:384
  81.7 19.3 %collective-permute-start.13 = (bf16[1,256,1024]{2,1,0:T(8,128)(2,1)S(1)}, bf16[1,256,1024]{2,1,0:T(8,128)(2,1)S(1)}, u32[]{:S(2)}, u32[]{:S(2)}) collective-permute-start(bf16[1,256,1024]{2,1,0:T(8,128)(2,1)S(1)} %relay.8.refs_4_), channel_id=1, source_target_pairs={{0,2},{1,3},{2,0},{3,1},{4,6},{5,7},{6,4},{7,5},{8,10},{9,11},{10,... | collective-permute-start | bytes 1572872 | tf_op jit(solution)/shard_map/ppermute | solution.py:384
  88.6 26.5 %collective-permute-start.21 = (bf16[3,6,128,128]{3,2,1,0:T(8,128)(2,1)S(1)}, bf16[3,6,128,128]{3,2,1,0:T(8,128)(2,1)S(1)}, u32[]{:S(2)}, u32[]{:S(2)}) collective-permute-start(bf16[3,6,128,128]{3,2,1,0:T(8,128)(2,1)S(1)} %get-tuple-element.51.refs_0_), channel_id=1, source_target_pairs={{0,8},{4,12},{24,16},{28,20},{1,9},{5,13},{25,17},{29,21},{2,10},{... | collective-permute-start | bytes 1769480 | tf_op jit(solution)/shard_map/ppermute | solution.py:384
  99.0 16.1 %collective-permute-start.20 = (bf16[2,6,128,128]{3,2,1,0:T(8,128)(2,1)S(1)}, bf16[2,6,128,128]{3,2,1,0:T(8,128)(2,1)S(1)}, u32[]{:S(2)}, u32[]{:S(2)}) collective-permute-start(bf16[2,6,128,128]{3,2,1,0:T(8,128)(2,1)S(1)} %get-tuple-element.50.refs_12_), channel_id=1, source_target_pairs={{8,16},{12,20},{16,8},{20,12},{9,17},{13,21},{17,9},{21,13},{10,18... | collective-permute-start | bytes 1179656 | tf_op jit(solution)/shard_map/ppermute | solution.py:384
  99.7 16.5 %collective-permute-start.16 = (bf16[1,8,128,128]{3,2,1,0:T(8,128)(2,1)S(1)}, bf16[1,8,128,128]{3,2,1,0:T(8,128)(2,1)S(1)}, u32[]{:S(2)}, u32[]{:S(2)}) collective-permute-start(bf16[1,8,128,128]{3,2,1,0:T(8,128)(2,1)S(1)} %get-tuple-element.45), channel_id=1, source_target_pairs={{8,0},{12,4},{16,24},{20,28},{9,1},{13,5},{17,25},{21,29},{10,2},{... | collective-permute-start | bytes 786440 | tf_op jit(solution)/shard_map/ppermute | solution.py:384
  102.1 16.9 %collective-permute-start.19 = (bf16[1,8,128,128]{3,2,1,0:T(8,128)(2,1)S(1)}, bf16[1,8,128,128]{3,2,1,0:T(8,128)(2,1)S(1)}, u32[]{:S(2)}, u32[]{:S(2)}) collective-permute-start(bf16[1,8,128,128]{3,2,1,0:T(8,128)(2,1)S(1)} %get-tuple-element.49), channel_id=1, source_target_pairs={{8,0},{12,4},{16,24},{20,28},{9,1},{13,5},{17,25},{21,29},{10,2},{... | collective-permute-start | bytes 786440 | tf_op jit(solution)/shard_map/ppermute | solution.py:384
  107.2 14.9 %collective-permute-start.24 = (bf16[3,4,128,128]{3,2,1,0:T(8,128)(2,1)S(1)}, bf16[3,4,128,128]{3,2,1,0:T(8,128)(2,1)S(1)}, u32[]{:S(2)}, u32[]{:S(2)}) collective-permute-start(bf16[3,4,128,128]{3,2,1,0:T(8,128)(2,1)S(1)} %get-tuple-element.55.refs_0_.refs_2_), channel_id=1, source_target_pairs={{0,8},{4,12},{24,16},{28,20},{1,9},{5,13},{25,17},{29,21},{2,10},{... | collective-permute-start | bytes 1179656 | tf_op jit(solution)/shard_map/ppermute | solution.py:384
  115.5 8.8 %collective-permute-start.23 = (bf16[2,6,128,128]{3,2,1,0:T(8,128)(2,1)S(1)}, bf16[2,6,128,128]{3,2,1,0:T(8,128)(2,1)S(1)}, u32[]{:S(2)}, u32[]{:S(2)}) collective-permute-start(bf16[2,6,128,128]{3,2,1,0:T(8,128)(2,1)S(1)} %get-tuple-element.54.refs_4_), channel_id=1, source_target_pairs={{8,16},{12,20},{16,8},{20,12},{9,17},{13,21},{17,9},{21,13},{10,18... | collective-permute-start | bytes 1179656 | tf_op jit(solution)/shard_map/ppermute | solution.py:384
  116.3 18.6 %collective-permute-start.28 = (bf16[1,4,128,128]{3,2,1,0:T(8,128)(2,1)S(1)}, bf16[1,4,128,128]{3,2,1,0:T(8,128)(2,1)S(1)}, u32[]{:S(2)}, u32[]{:S(2)}) collective-permute-start(bf16[1,4,128,128]{3,2,1,0:T(8,128)(2,1)S(1)} %get-tuple-element.58), channel_id=1, source_target_pairs={{8,0},{12,4},{16,24},{20,28},{9,1},{13,5},{17,25},{21,29},{10,2},{... | collective-permute-start | bytes 393224 | tf_op jit(solution)/shard_map/ppermute | solution.py:384
  117.6 9.9 %collective-permute-start.22 = (bf16[1,6,128,128]{3,2,1,0:T(8,128)(2,1)S(1)}, bf16[1,6,128,128]{3,2,1,0:T(8,128)(2,1)S(1)}, u32[]{:S(2)}, u32[]{:S(2)}) collective-permute-start(bf16[1,6,128,128]{3,2,1,0:T(8,128)(2,1)S(1)} %get-tuple-element.53), channel_id=1, source_target_pairs={{8,0},{12,4},{16,24},{20,28},{9,1},{13,5},{17,25},{21,29},{10,2},{... | collective-permute-start | bytes 589832 | tf_op jit(solution)/shard_map/ppermute | solution.py:384
  122.3 12.6 %collective-permute-start.27 = (bf16[1,4,128,128]{3,2,1,0:T(8,128)(2,1)S(1)}, bf16[1,4,128,128]{3,2,1,0:T(8,128)(2,1)S(1)}, u32[]{:S(2)}, u32[]{:S(2)}) collective-permute-start(bf16[1,4,128,128]{3,2,1,0:T(8,128)(2,1)S(1)} %get-tuple-element.57), channel_id=1, source_target_pairs={{8,24},{12,28},{16,0},{20,4},{9,25},{13,29},{17,1},{21,5},{10,26},... | collective-permute-start | bytes 393224 | tf_op jit(solution)/shard_map/ppermute | solution.py:384
  123.6 11.3 %collective-permute-start.26 = (bf16[1,4,128,128]{3,2,1,0:T(8,128)(2,1)S(1)}, bf16[1,4,128,128]{3,2,1,0:T(8,128)(2,1)S(1)}, u32[]{:S(2)}, u32[]{:S(2)}) collective-permute-start(bf16[1,4,128,128]{3,2,1,0:T(8,128)(2,1)S(1)} %get-tuple-element.56.refs_2_), channel_id=1, source_target_pairs={{8,16},{12,20},{16,8},{20,12},{9,17},{13,21},{17,9},{21,13},{10,18... | collective-permute-start | bytes 393224 | tf_op jit(solution)/shard_map/ppermute | solution.py:384
  124.5 10.3 %collective-permute-start.25 = (bf16[1,6,128,128]{3,2,1,0:T(8,128)(2,1)S(1)}, bf16[1,6,128,128]{3,2,1,0:T(8,128)(2,1)S(1)}, u32[]{:S(2)}, u32[]{:S(2)}) collective-permute-start(bf16[1,6,128,128]{3,2,1,0:T(8,128)(2,1)S(1)} %relay.13), channel_id=1, source_target_pairs={{8,0},{12,4},{16,24},{20,28},{9,1},{13,5},{17,25},{21,29},{10,2},{... | collective-permute-start | bytes 589832 | tf_op jit(solution)/shard_map/ppermute | solution.py:384
  (6 other events, 41.6 us)

commit v3 on v2

--- a/solution.py
+++ b/solution.py
@@ -12,7 +12,7 @@
 BF16 = jnp.bfloat16
 ANY = pl.BlockSpec(memory_space=pl.ANY)
 PARAMS = pltpu.CompilerParams(
-    dimension_semantics=("arbitrary",), vmem_limit_bytes=48 * 1024 * 1024
+    dimension_semantics=("arbitrary",), vmem_limit_bytes=36 * 1024 * 1024
 )
 ALL = pltpu.CompilerParams(
     dimension_semantics=("arbitrary",), vmem_limit_bytes=60 * 1024 * 1024
@@ -93,11 +93,11 @@
     return lambda i: jnp.clip(i, lo, hi) - lo
 
 
-def forward_kernel(nf, columns, fold, copies, *refs):
+def forward_kernel(nf, first, columns, fold, copies, ahead, *refs):
     rows, feats = refs[0], refs[1 : 1 + nf]
-    w_ref, cot_ref = refs[1 + nf : 3 + nf]
+    w_ref, cot_ref, cot_ahead_ref = refs[1 + nf : 4 + nf]
     buf, tab, sems = refs[-3:]
-    act_ref, delta_ref, *cot_copies = refs[-5 - len(copies) : -3]
+    act_ref, delta_ref, *cot_copies = refs[-5 - len(copies) - ahead : -3]
     step, depth, side = w_ref.shape
     per_column = depth // side
     here = pl.program_id(0)
@@ -108,7 +108,7 @@
 
     index = Index(tab, columns, per_column, fold, side)
     for i in range(step):
-        x = index.gather(buf, here * step + i, range(per_column))
+        x = index.gather(buf, first + here * step + i, range(per_column))
         lanes = slice(i * side, (i + 1) * side)
         pre, sig, delta = forward_column(x, w_ref[i], cot_ref[:, lanes])
         act_ref[:, lanes] = (pre * sig).astype(BF16)
@@ -119,25 +119,43 @@
         def _(ref=ref):
             ref[...] = cot_ref[...]
 
-
-def forward(rows, feats, weight, cotangent, fold, step, parts=(), after=()):
+    if ahead:
+        cot_copies[-1][...] = cot_ahead_ref[...]
+
+
+def forward(rows, feats, weight, cotangent, fold, act, first, parts, copied, ahead, step, after=()):
     tokens, hidden = cotangent.shape
     columns, depth, side = weight.shape
     width = sum(f.shape[1] for f in feats)
-    args = [rows, *feats, weight, cotangent, *after]
+    count = sum(parts)
+    base = first // step
+    jump = base + count // step if ahead else base
+    args = [rows, *feats, weight, cotangent, cotangent]
+    wide = lambda at: pl.BlockSpec((tokens, step * side), lambda i: (0, at + i))
     ins = [ANY] * (1 + len(feats)) + [
-        pl.BlockSpec((step, depth, side), lambda i: (i, 0, 0)),
-        pl.BlockSpec((tokens, step * side), lambda i: (0, i)),
+        pl.BlockSpec((step, depth, side), lambda i: (base + i, 0, 0)),
+        wide(base),
+        wide(jump),
     ]
+    aliases = {}
+    if act is not None:
+        aliases = {len(args): 0}
+        args.append(act)
+    args += after
     ins += [ANY] * (len(args) - len(ins))
-    outs = [pl.BlockSpec((tokens, step * side), lambda i: (0, i))] * 2
-    copies = ranges(parts, step)[1:]
+    outs = [wide(base), wide(0)]
+    spans = ranges(parts, step)
+    copies = [spans[n] for n in copied]
     for lo, hi in copies:
         at = held_at(lo, hi)
         outs.append(pl.BlockSpec((tokens, step * side), lambda i, at=at: (0, at(i))))
-    return pl.pallas_call(
-        functools.partial(forward_kernel, len(feats), columns, fold, copies),
-        grid=(columns // step,),
+    sizes = [parts[n] for n in copied]
+    if ahead:
+        outs.append(wide(0))
+        sizes.append(count)
+    return pl.pallas_call(
+        functools.partial(forward_kernel, len(feats), first, columns, fold, copies, ahead),
+        grid=(count // step,),
         in_specs=ins,
         out_specs=outs,
         scratch_shapes=[
@@ -145,8 +163,12 @@
             pltpu.SMEM(rows.shape, jnp.int32),
             pltpu.SemaphoreType.DMA((1 + len(feats),)),
         ],
-        out_shape=[jax.ShapeDtypeStruct((tokens, hidden), BF16)] * 2
-        + [jax.ShapeDtypeStruct((tokens, n * side), BF16) for n in parts[1:]],
+        out_shape=[
+            jax.ShapeDtypeStruct((tokens, hidden), BF16),
+            jax.ShapeDtypeStruct((tokens, count * side), BF16),
+        ]
+        + [jax.ShapeDtypeStruct((tokens, n * side), BF16) for n in sizes],
+        input_output_aliases=aliases,
         compiler_params=PARAMS,
         name="forward",
     )(*args)
@@ -163,11 +185,11 @@
     ]
 
 
-def grads_kernel(nf, first, columns, fold, scale, last, *refs):
+def grads_kernel(nf, first, columns, fold, scale, *refs):
     rows, mine, other = refs[0], refs[1 : 1 + nf], refs[1 + nf : 1 + 2 * nf]
     w_ref, delta_ref, cot_ref = refs[1 + 2 * nf : 4 + 2 * nf]
     buf, tab, sems = refs[-3:]
-    own_ref, rest_ref, *home = refs[-6 if last else -5 : -3]
+    own_ref, rest_ref = refs[-5:-3]
     step, depth, side = w_ref.shape
     per_column = depth // side
     tokens = cot_ref.shape[0]
@@ -191,45 +213,41 @@
         own_ref[i] = blocks[0]
         for p, block in enumerate(blocks[1:]):
             rest_ref[p, i] = block
-        if last:
-            home[0][0, i] = blocks[1]
 
 
 def grads(
-    rows, mine, other, weight, delta, cot_other, skip, count, fold, first, line, scale, after=()
+    rows, mine, other, weight, delta, at, cot_other, skip, count, fold, first, line, scale,
+    after=(),
 ):
     tokens = delta.shape[0]
     columns, depth, side = weight.shape
     width = sum(f.shape[1] for f in mine)
-    step = math.gcd(first, skip, count, STEP)
-    base, skip = first // step, skip // step
+    step = math.gcd(first, at, skip, count, STEP)
+    base, at, skip = first // step, at // step, skip // step
     args = [rows, *mine, *other, weight, delta, cot_other, *after]
     ins = [ANY] * (1 + 2 * len(mine)) + [
         pl.BlockSpec((step, depth, side), lambda i: (base + i, 0, 0)),
-        pl.BlockSpec((tokens, step * side), lambda i: (0, base + i)),
+        pl.BlockSpec((tokens, step * side), lambda i: (0, at + i)),
         pl.BlockSpec((tokens, step * side), lambda i: (0, skip + i)),
     ]
     ins += [ANY] * (len(args) - len(ins))
-    one = jax.ShapeDtypeStruct((count, side, side), BF16)
-    one_spec = pl.BlockSpec((step, side, side), lambda i: (i, 0, 0))
-    last = first + count == columns
-    piece = lambda n: jax.ShapeDtypeStruct((n, count, side, side), BF16)
-    piece_spec = lambda n: pl.BlockSpec((n, step, side, side), lambda i: (0, i, 0, 0))
-    sends, send_specs = [piece(line - 1)], [piece_spec(line - 1)]
-    if last:
-        sends.append(piece(1))
-        send_specs.append(piece_spec(1))
-    return pl.pallas_call(
-        functools.partial(grads_kernel, len(mine), first, columns, fold, scale, last),
+    return pl.pallas_call(
+        functools.partial(grads_kernel, len(mine), first, columns, fold, scale),
         grid=(count // step,),
         in_specs=ins,
-        out_specs=[one_spec, *send_specs],
+        out_specs=[
+            pl.BlockSpec((step, side, side), lambda i: (i, 0, 0)),
+            pl.BlockSpec((line - 1, step, side, side), lambda i: (0, i, 0, 0)),
+        ],
         scratch_shapes=[
             pltpu.VMEM((2 * tokens, width), BF16),
             pltpu.SMEM(rows.shape, jnp.int32),
             pltpu.SemaphoreType.DMA((1 + 2 * len(mine),)),
         ],
-        out_shape=[one, *sends],
+        out_shape=[
+            jax.ShapeDtypeStruct((count, side, side), BF16),
+            jax.ShapeDtypeStruct((line - 1, count, side, side), BF16),
+        ],
         compiler_params=PARAMS,
         name="grads",
     )(*args)
@@ -293,65 +311,112 @@
 
 def relay_kernel(jobs, *refs):
     outs = refs[-len(jobs) :]
-    for n, (a_at, b_at, count) in enumerate(jobs):
-        a, b = refs[2 * n], refs[2 * n + 1]
-        for i in range(count):
-            outs[n][i] = (a[a_at + i].astype(F32) + b[b_at + i].astype(F32)).astype(BF16)
+    refs = list(refs)
+    for out, parts in zip(outs, jobs):
+        at = 0
+        for a_at, b_at, count in parts:
+            a = refs.pop(0)
+            b = None if b_at is None else refs.pop(0)
+            wide = a.shape[1]
+            for i in range(count):
+                value = a[a_at + i]
+                if b is not None:
+                    value = (value.astype(F32) + b[b_at + i].astype(F32)).astype(BF16)
+                out[i, at : at + wide] = value
+            at += wide
 
 
 def relay(*jobs, after=()):
-    args, ins, outs, shapes, cuts = [], [], [], [], []
-    steps = 2
-    for a, a_at, b, b_at, count in jobs:
-        part = (a.shape[1] // steps,) + a.shape[2:]
-        zeros = (0,) * (a.ndim - 2)
-        for x in (a, b):
-            args.append(x)
-            ins.append(pl.BlockSpec(x.shape[:1] + part, lambda i, z=zeros: (0, i) + z))
-        outs.append(pl.BlockSpec((count,) + part, lambda i, z=zeros: (0, i) + z))
-        shapes.append(jax.ShapeDtypeStruct((count,) + a.shape[1:], BF16))
-        cuts.append((a_at, b_at, count))
+    args, shapes, cuts = [], [], []
+    for parts in jobs:
+        cuts.append([])
+        wide = 0
+        for a, a_at, b, b_at, count in parts:
+            args += [a] if b is None else [a, b]
+            cuts[-1].append((a_at, None if b is None else b_at, count))
+            wide += a.shape[1]
+        shapes.append((count, wide) + a.shape[2:])
+    used = len(args)
 
     def kernel(*refs):
-        relay_kernel(cuts, *refs[: len(args)], *refs[len(args) + len(after) :])
-
+        relay_kernel(cuts, *refs[:used], *refs[used + len(after) :])
+
+    whole = lambda shape: pl.BlockSpec(shape, lambda i: (0,) * len(shape))
     return pl.pallas_call(
         kernel,
-        grid=(steps,),
-        in_specs=ins + [ANY] * len(after),
-        out_specs=outs,
-        out_shape=shapes,
+        grid=(1,),
+        in_specs=[whole(x.shape) for x in args] + [ANY] * len(after),
+        out_specs=[whole(x) for x in shapes],
+        out_shape=[jax.ShapeDtypeStruct(x, BF16) for x in shapes],
         compiler_params=PARAMS,
         name="relay",
     )(*args, *after)
 
 
-def cut_kernel(x_ref, whole_ref, rows_ref, out_ref, copy_ref):
-    del rows_ref
+def cut_kernel(x_ref, out_ref):
     out_ref[...] = x_ref[...]
-    copy_ref[...] = whole_ref[...]
-
-
-def cut(x, width, whole, rows):
+
+
+def cut(x, width):
+    spec = pl.BlockSpec((x.shape[0], width), lambda i: (0, 0))
     return pl.pallas_call(
         cut_kernel,
         grid=(1,),
-        in_specs=[
-            pl.BlockSpec((x.shape[0], width), lambda i: (0, 0)),
-            pl.BlockSpec(whole.shape, lambda i: (0, 0)),
-            ANY,
-        ],
-        out_specs=[
-            pl.BlockSpec((x.shape[0], width), lambda i: (0, 0)),
-            pl.BlockSpec(whole.shape, lambda i: (0, 0)),
-        ],
-        out_shape=[
-            jax.ShapeDtypeStruct((x.shape[0], width), x.dtype),
-            jax.ShapeDtypeStruct(whole.shape, whole.dtype),
-        ],
+        in_specs=[spec],
+        out_specs=spec,
+        out_shape=jax.ShapeDtypeStruct((x.shape[0], width), x.dtype),
         compiler_params=ALL,
         name="cut",
-    )(x, whole, rows)
+    )(x)
+
+
+def total_kernel(chunks, *refs):
+    out_ref = refs[-1]
+    refs = list(refs)
+    at = 0
+    for count, starts in chunks:
+        value = 0.0
+        for start in starts:
+            ref = refs.pop(0)
+            part = ref[0, start : start + count] if len(ref.shape) == 4 else ref[...]
+            value = value + part.astype(F32)
+        out_ref[at : at + count] = value
+        at += count
+
+
+def total(whole, first, columns, chunks, after=()):
+    chunks = [[t if isinstance(t, tuple) else (t, 0) for t in terms] for terms in chunks]
+    sizes = [(terms[0][0].shape[0], [start for _, start in terms]) for terms in chunks]
+    count = sum(n for n, _ in sizes)
+    side = chunks[0][0][0].shape[1]
+    base = first // count
+    args = [t for terms in chunks for t, _ in terms]
+    ins = [
+        pl.BlockSpec((1,) + t.shape[1:], lambda i: (0, 0, 0, 0))
+        if t.ndim == 4
+        else pl.BlockSpec(t.shape, lambda i: (0, 0, 0))
+        for t in args
+    ]
+    used = len(args)
+    aliases = {}
+    if whole is not None:
+        aliases = {len(args): 0}
+        args.append(whole)
+    args += after
+
+    def kernel(*refs):
+        total_kernel(sizes, *refs[:used], refs[-1])
+
+    return pl.pallas_call(
+        kernel,
+        grid=(1,),
+        in_specs=ins + [ANY] * (len(args) - len(ins)),
+        out_specs=pl.BlockSpec((count, side, side), lambda i: (base, 0, 0)),
+        out_shape=jax.ShapeDtypeStruct((columns, side, side), F32),
+        input_output_aliases=aliases,
+        compiler_params=PARAMS,
+        name="total",
+    )(*args)
 
 
 def gate_kernel(*refs):
@@ -397,77 +462,91 @@
     sizes = [c * columns // 32 for c in (8, 8, 6, 6, 4)]
     firsts = [sum(sizes[:n]) for n in range(len(sizes))]
     parts = [sizes[0], sizes[1], sizes[2] + sizes[3] + sizes[4]]
-    places = [(0, 0), (1, 0), (2, 0), (2, sizes[2]), (2, sizes[2] + sizes[3])]
 
     f0 = features
     f2 = chips(f0)
-    cot0, sent = cut(cotangent, parts[0] * side, f0, rows)
-    u0 = pairs(sent)
+    u0 = pairs(f0)
+    cot0 = cut(cotangent, parts[0] * side)
+    f2 = gate(f2, cot0, rows)
     c0 = pairs(cot0)
     f1 = cores(f0)
     f3 = cores(f2)
     u1 = cores(u0)
     u2 = chips(u0)
     mine = [f0, f1, f2, f3]
-    act, delta, cot1, cot2 = forward(rows, mine, weight, cotangent, fold, STEP, parts)
+    act, delta0, cot1, cot2 = forward(
+        rows, mine, weight, cotangent, fold, None, 0, parts[:2], (1,), True, STEP
+    )
     c1, c2 = pairs(cot1), pairs(cot2)
-    cs = [c0, c1, c2]
-    u2 = gate(u2, delta, c0)
+    u2 = gate(u2, delta0, c0)
     u3 = cores(u2)
     other = [u0, u1, u2, u3]
 
-    def chunk(n, *after):
-        part, skip = places[n]
+    def chunk(n, delta, cot, *after):
+        half = firsts[n] - firsts[2] if n >= 2 else firsts[n]
         return grads(
-            rows, mine, other, weight, delta, cs[part], skip, sizes[n], fold, firsts[n],
-            line, scale, after,
+            rows, mine, other, weight, delta, half, cot, half if n >= 2 else 0, sizes[n], fold,
+            firsts[n], line, scale, after,
         )
 
-    own0, rest0 = chunk(0)
+    own0, rest0 = chunk(0, delta0, c0)
     got0 = outer_in(rest0)
-    own1, rest1 = chunk(1, own0)
+    act, delta1 = forward(
+        rows, mine, weight, cotangent, fold, act, firsts[2], parts[2:], (), False, STEP, (own0,)
+    )
+    own1, rest1 = chunk(1, delta0, c1, delta1)
     got1 = outer_in(rest1)
     near, away0, away1 = dinput(
-        rows, weight, [delta], fold, ((0, 2), (1,), (3,)), held, STEP, (own1,)
+        rows, weight, [delta0, delta1], fold, ((0, 2), (1,), (3,)), held, STEP, (own1,)
     )
     sib0, sib1 = cores(away0), cores(away1)
-    (far0,) = relay((rest0, 1, got0, 1, 2), after=(near,))
+    (far0,) = relay([(rest0, 1, got0, 1, 2)], after=(near,))
     across0 = middle(far0)
-    own2, rest2 = chunk(2, far0)
+    own2, rest2 = chunk(2, delta1, c2, far0)
     got2 = outer_in(rest2)
-    (xsum,) = relay((near, 1, sib1, 0, 1), after=(own2,))
+    (far1,) = relay([(rest1, 1, got1, 1, 2)], after=(own2,))
+    across1 = middle(far1)
+    own3, rest3 = chunk(3, delta1, c2, far1, across0)
+    got3 = outer_in(rest3)
+    (xsum,) = relay([(near, 1, sib1, 0, 1)], after=(own3, sib0))
     xback = chips(xsum)
-    far1, home0 = relay((rest1, 1, got1, 1, 2), (rest0, 0, across0, 1, 1), after=(xsum,))
-    across1 = middle(far1)
+    far2, home0 = relay(
+        [(rest2, 1, got2, 1, 2)],
+        [(rest0, 0, across0, 1, 1), (rest1, 0, across1, 1, 1)],
+        after=(xsum,),
+    )
+    across2 = middle(far2)
     back0 = outer_out(home0)
-    own3, rest3 = chunk(3, far1)
-    got3 = outer_in(rest3)
-    far2, home1 = relay((rest2, 1, got2, 1, 2), (rest1, 0, across1, 1, 1), after=(own3,))
-    across2 = middle(far2)
+    own4, rest4 = chunk(4, delta1, c2, far2)
+    got4 = outer_in(rest4)
+    third0, third1, home1 = relay(
+        [(rest3, 1, got3, 1, 1)],
+        [(rest3, 2, got3, 2, 1)],
+        [(rest2, 0, across2, 1, 1), (rest3, 0, None, 0, 1), (rest4, 0, None, 0, 1)],
+        after=(own4, xback),
+    )
+    near3, far3 = middle(third0), beyond(third1)
     back1 = outer_out(home1)
-    own4, rest4, home4 = chunk(4, far2)
-    got4 = outer_in(rest4)
-    back4 = outer_out(home4)
-    far3, home2 = relay((rest3, 1, got3, 1, 2), (rest2, 0, across2, 1, 1), after=(own4,))
-    across3 = middle(far3)
-    back2 = outer_out(home2)
-    last0, last1 = relay((rest4, 1, got4, 1, 1), (rest4, 2, got4, 2, 1), after=(far3,))
+    last0, last1 = relay(
+        [(rest4, 1, got4, 1, 1)], [(rest4, 2, got4, 2, 1)], after=(third0, back0)
+    )
     near4, far4 = middle(last0), beyond(last1)
-    (home3,) = relay((rest3, 0, across3, 1, 1), after=(last0,))
-    back3 = outer_out(home3)
-
-    def total(own, got, *more):
-        return own.astype(F32) + got[0].astype(F32) + sum(x[0].astype(F32) for x in more)
-
-    weight_grad = jnp.concatenate(
+    grad = total(
+        None,
+        firsts[0],
+        columns,
+        [[own0, got0, across0, back0], [own1, got1, across1, (back0, sizes[0])]],
+        (last0,),
+    )
+    weight_grad = total(
+        grad,
+        firsts[2],
+        columns,
         [
-            total(own0, got0, across0, back0),
-            total(own1, got1, across1, back1),
-            total(own2, got2, across2, back2),
-            total(own3, got3, across3, back3),
-            total(own4, got4, near4, far4, back4),
+            [own2, got2, across2, back1],
+            [own3, got3, near3, far3, (back1, sizes[2])],
+            [own4, got4, near4, far4, (back1, sizes[2] + sizes[3])],
         ],
-        axis=0,
     )
     input_grad = (
         near[0].astype(F32) + sib0[0].astype(F32) + xback[0].astype(F32)
@@ -486,7 +565,9 @@
     local_rows = lax.dynamic_slice_in_dim(rows_index, first, columns, 0)
     rows = rows_index.reshape(-1)
     step = math.gcd(columns, STEP)
-    act, delta = forward(rows, [whole], weight, cotangent, 0, step)
+    act, delta = forward(
+        rows, [whole], weight, cotangent, 0, None, 0, (columns,), (), False, step
+    )
     (part,) = dinput(rows, weight, [delta], 0, ((0,),), whole.shape[1], step)
     input_grad = lax.psum_scatter(part[0], "shard", scatter_dimension=1, tiled=True)
     blocks = whole.reshape(tokens, block_rows, side)[:, local_rows]

time: 137 us -> 132 us (0.964)
  starting transfers between devices: 52.1 us -> 44 us
  local copies, waits for them, and re-layouts: 2.82 us -> 7.98 us
  Pallas kernels: 51.4 us -> 47 us
  waiting for transfers between devices: 27.2 us -> 29.7 us
    ppermute x29 -> x27, starting transfers between devices: 52.1 us -> 44 us  [permute(): return lambda x: lax.ppermute(x, axis, links)]
    unnamed x19 -> x41, local copies, waits for them, and re-layouts: 2.14 us -> 7.89 us
    pallas_call x5, Pallas kernels: 24.1 us -> 21.2 us  [grads(): pl.pallas_call(functools.partial(grads_kernel, len(mine), first, columns,...]
    ppermute x29 -> x27, waiting for transfers between devices: 27.2 us -> 29.7 us  [permute(): return lambda x: lax.ppermute(x, axis, links)]
    pallas_call x1, Pallas kernels: 10.6 us -> 8.85 us  [dinput(): pl.pallas_call(functools.partial(dinput_kernel, len(deltas), fold, groups...]
    pallas_call x9 -> x11, Pallas kernels: 16.7 us -> 17 us  [the longest x2 11.7 us: forward(): pl.pallas_call(functools.partial(forward_kernel, len(feats), first, colum...]
  transfers between devices with their start and end apart: 29 -> 27, of which waited for: 7 -> 8; matrix products, arithmetic and copies ran while one was open for 2% -> 1% of each run, Pallas kernels for 38% -> 35%
where the time goes in v3:
time: 132 us; the launch traced here: 131 us
  Pallas kernels  47 us (36%)
  starting transfers between devices  44 us (33%)
  waiting for transfers between devices  29.7 us (22%)
  local copies, waits for them, and re-layouts  7.98 us (6%)
    ppermute x27, starting transfers between devices, permute(): return lambda x: lax.ppermute(x, axis, links)  44 us
    ppermute x27, waiting for transfers between devices, permute(): return lambda x: lax.ppermute(x, axis, links)  29.7 us
    pallas_call x5, Pallas kernels, grads(): pl.pallas_call(functools.partial(grads_kernel, len(mine), first, columns,...  21.2 us
    pallas_call x2, Pallas kernels, forward(): pl.pallas_call(functools.partial(forward_kernel, len(feats), first, colum...  11.7 us
    pallas_call x1, Pallas kernels, dinput(): pl.pallas_call(functools.partial(dinput_kernel, len(deltas), fold, groups...  8.85 us
    unnamed x41, local copies, waits for them, and re-layouts  7.89 us
  transfers between devices with their start and end apart: 27, of which 8 were waited for; matrix products, arithmetic and copies ran while one was open for 1% of the time, Pallas kernels for 35%

profile of v3, /device:TPU:0, one launch (start us, length us, event | category | flops | bytes accessed | tf_op | source)
XLA Modules:
  0.0 130.9 jit_solution(9902893062755935498)
XLA Ops:
  0.6 3.0 %collective-permute-start.1 = (bf16[256,1024]{1,0:T(8,128)(2,1)}, bf16[256,1024]{1,0:T(8,128)(2,1)S(1)}, u32[]{:S(2)}, u32[]{:S(2)}) collective-permute-start(bf16[256,1024]{1,0:T(8,128)(2,1)} %refs_1_.13), channel_id=1, source_target_pairs={{0,2},{1,3},{2,0},{3,1},{4,6},{5,7},{6,4},{7,5},{8,10},{9,11},{10,... | collective-permute-start | bytes 1572872 | tf_op jit(solution)/shard_map/ppermute | solution.py:449
  3.6 1.5 %collective-permute-start.3 = (bf16[256,1024]{1,0:T(8,128)(2,1)}, bf16[256,1024]{1,0:T(8,128)(2,1)}, u32[]{:S(2)}, u32[]{:S(2)}) collective-permute-start(bf16[256,1024]{1,0:T(8,128)(2,1)} %refs_1_.13), channel_id=1, source_target_pairs={{0,4},{4,0},{8,12},{12,8},{16,20},{20,16},{24,28},{28,24},{1,5},{5... | collective-permute-start | bytes 1572872 | tf_op jit(solution)/shard_map/ppermute | solution.py:449
  6.1 2.0 %cut.1.refs_1_ = bf16[256,1024]{1,0:T(8,128)(2,1)} custom-call(bf16[256,4096]{1,0:T(8,128)(2,1)} %refs_7_.3), custom_call_target="tpu_custom_call" | custom-call | tf_op jit(solution)/shard_map/cut/pallas_call | solution.py:362
  8.1 7.7 %collective-permute-done.1.refs_0_ = bf16[256,1024]{1,0:T(8,128)(2,1)S(1)} collective-permute-done((bf16[256,1024]{1,0:T(8,128)(2,1)}, bf16[256,1024]{1,0:T(8,128)(2,1)S(1)}, u32[]{:S(2)}, u32[]{:S(2)}) %collective-permute-start.1) | collective-permute-done | bytes 524320 | tf_op jit(solution)/shard_map/ppermute | solution.py:449
  16.8 1.8 %collective-permute-start.6 = (bf16[256,1024]{1,0:T(8,128)(2,1)}, bf16[256,1024]{1,0:T(8,128)(2,1)S(1)}, u32[]{:S(2)}, u32[]{:S(2)}) collective-permute-start(bf16[256,1024]{1,0:T(8,128)(2,1)} %cut.1.refs_1_), channel_id=1, source_target_pairs={{0,4},{4,0},{8,12},{12,8},{16,20},{20,16},{24,28},{28,24},{1,5},{5... | collective-permute-start | bytes 1572872 | tf_op jit(solution)/shard_map/ppermute | solution.py:449
  18.6 1.5 %collective-permute-start.5 = (bf16[256,1024]{1,0:T(8,128)(2,1)}, bf16[256,1024]{1,0:T(8,128)(2,1)S(1)}, u32[]{:S(2)}, u32[]{:S(2)}) collective-permute-start(bf16[256,1024]{1,0:T(8,128)(2,1)} %collective-permute-done.3.refs_5_), channel_id=1, source_target_pairs={{0,2},{1,3},{2,0},{3,1},{4,6},{5,7},{6,4},{7,5},{8,10},{9,11},{10,... | collective-permute-start | bytes 1572872 | tf_op jit(solution)/shard_map/ppermute | solution.py:449
  20.1 3.4 %copy-done = bf16[32,1024,128]{2,1,0:T(8,128)(2,1)S(1)} copy-done((bf16[32,1024,128]{2,1,0:T(8,128)(2,1)S(1)}, bf16[32,1024,128]{2,1,0:T(8,128)(2,1)}, u32[]{:S(2)}) %copy-start) | copy-done | bytes 8388632
  23.5 6.0 %forward.2 = (bf16[256,4096]{1,0:T(8,128)(2,1)}, bf16[256,2048]{1,0:T(8,128)(2,1)S(1)}, bf16[256,1024]{1,0:T(8,128)(2,1)S(1)}, bf16[256,2048]{1,0:T(8,128)(2,1)S(1)}) custom-call(s32[1024]{0:T(1024)S(1)} %reshape.15.refs_2_.refs_0_, bf16[256,1024]{1,0:T(8,128)(2,1)S(1)} %copy-done.3, bf16[256,1024]{1,0:T(8,128)(2,1)S(1)} %collective-permute-done.refs_2_, ...), custom_call_target="tpu_custom_call" | custom-call | tf_op jit(solution)/shard_map/forward/pallas_call | solution.py:156
  29.5 1.9 %collective-permute-done.6.refs_2_.refs_11_ = bf16[256,1024]{1,0:T(8,128)(2,1)S(1)} collective-permute-done((bf16[256,1024]{1,0:T(8,128)(2,1)}, bf16[256,1024]{1,0:T(8,128)(2,1)S(1)}, u32[]{:S(2)}, u32[]{:S(2)}) %collective-permute-start.6) | collective-permute-done | bytes 524320 | tf_op jit(solution)/shard_map/ppermute | solution.py:449
  31.4 1.5 %collective-permute-done.5.refs_0_ = bf16[256,1024]{1,0:T(8,128)(2,1)S(1)} collective-permute-done((bf16[256,1024]{1,0:T(8,128)(2,1)}, bf16[256,1024]{1,0:T(8,128)(2,1)S(1)}, u32[]{:S(2)}, u32[]{:S(2)}) %collective-permute-start.5) | collective-permute-done | bytes 524320 | tf_op jit(solution)/shard_map/ppermute | solution.py:449
  33.2 1.7 %collective-permute-start.11 = (bf16[256,2048]{1,0:T(8,128)(2,1)S(1)}, bf16[256,2048]{1,0:T(8,128)(2,1)S(1)}, u32[]{:S(2)}, u32[]{:S(2)}) collective-permute-start(bf16[256,2048]{1,0:T(8,128)(2,1)S(1)} %get-tuple-element.39), channel_id=1, source_target_pairs={{0,4},{4,0},{8,12},{12,8},{16,20},{20,16},{24,28},{28,24},{1,5},{5... | collective-permute-start | bytes 3145736 | tf_op jit(solution)/shard_map/ppermute | solution.py:449
  34.9 4.8 %grads.5 = (bf16[8,128,128]{2,1,0:T(8,128)(2,1)S(1)}, bf16[3,8,128,128]{3,2,1,0:T(8,128)(2,1)S(1)}) custom-call(s32[1024]{0:T(1024)S(1)} %reshape.15.refs_2_.refs_0_, bf16[256,1024]{1,0:T(8,128)(2,1)S(1)} %copy-done.3, bf16[256,1024]{1,0:T(8,128)(2,1)S(1)} %collective-permute-done.refs_2_, bf16[256,1024]{1,0:T(8,128)(2,1)S(1)} %gate.2.refs_3_, ...), custom_call_target="tpu_custom_call" | custom-call | tf_op jit(solution)/shard_map/grads/pallas_call | solution.py:234
  39.7 3.5 %collective-permute-start.13 = (bf16[3,8,128,128]{3,2,1,0:T(8,128)(2,1)S(1)}, bf16[3,8,128,128]{3,2,1,0:T(8,128)(2,1)S(1)}, u32[]{:S(2)}, u32[]{:S(2)}) collective-permute-start(bf16[3,8,128,128]{3,2,1,0:T(8,128)(2,1)S(1)} %get-tuple-element.41.refs_0_.refs_2_), channel_id=1, source_target_pairs={{0,8},{4,12},{24,16},{28,20},{1,9},{5,13},{25,17},{29,21},{2,10},{... | collective-permute-start | bytes 2359304 | tf_op jit(solution)/shard_map/ppermute | solution.py:449
  43.2 5.7 %forward.3 = (bf16[256,4096]{1,0:T(8,128)(2,1)}, bf16[256,2048]{1,0:T(8,128)(2,1)S(1)}) custom-call(s32[1024]{0:T(1024)S(1)} %reshape.15.refs_2_.refs_0_, bf16[256,1024]{1,0:T(8,128)(2,1)S(1)} %copy-done.3, bf16[256,1024]{1,0:T(8,128)(2,1)S(1)} %collective-permute-done.refs_2_, bf16[256,1024]{1,0:T(8,128)(2,1)S(1)} %gate.2.refs_3_, ...), custom_call_target="tpu_custom_call", output_to_operand_aliasing={{0}: (8, {})} | custom-call | tf_op jit(solution)/shard_map/forward/pallas_call | solution.py:156
  49.0 4.8 %grads.6 = (bf16[8,128,128]{2,1,0:T(8,128)(2,1)S(1)}, bf16[3,8,128,128]{3,2,1,0:T(8,128)(2,1)S(1)}) custom-call(s32[1024]{0:T(1024)S(1)} %reshape.15.refs_2_.refs_0_, bf16[256,1024]{1,0:T(8,128)(2,1)S(1)} %copy-done.3, bf16[256,1024]{1,0:T(8,128)(2,1)S(1)} %collective-permute-done.refs_2_, bf16[256,1024]{1,0:T(8,128)(2,1)S(1)} %gate.2.refs_3_, ...), custom_call_target="tpu_custom_call" | custom-call | tf_op jit(solution)/shard_map/grads/pallas_call | solution.py:234
  53.8 2.1 %collective-permute-start.12 = (bf16[3,8,128,128]{3,2,1,0:T(8,128)(2,1)S(1)}, bf16[3,8,128,128]{3,2,1,0:T(8,128)(2,1)S(1)}, u32[]{:S(2)}, u32[]{:S(2)}) collective-permute-start(bf16[3,8,128,128]{3,2,1,0:T(8,128)(2,1)S(1)} %get-tuple-element.40.refs_0_.refs_4_), channel_id=1, source_target_pairs={{0,8},{4,12},{24,16},{28,20},{1,9},{5,13},{25,17},{29,21},{2,10},{... | collective-permute-start | bytes 2359304 | tf_op jit(solution)/shard_map/ppermute | solution.py:449
  55.9 8.8 %dinput.1 = (bf16[2,256,1024]{2,1,0:T(8,128)(2,1)S(1)}, bf16[1,256,1024]{2,1,0:T(8,128)(2,1)}, bf16[1,256,1024]{2,1,0:T(8,128)(2,1)S(1)}) custom-call(s32[1024]{0:T(1024)S(1)} %reshape.15.refs_2_.refs_0_, bf16[256,2048]{1,0:T(8,128)(2,1)S(1)} %get-tuple-element.30.refs_1_.refs_10_, bf16[256,2048]{1,0:T(8,128)(2,1)S(1)} %get-tuple-element.33.refs_12_.refs_2_.refs_10_, ...), custom_call_target="tpu_custom_call" | custom-call | tf_op jit(solution)/shard_map/dinput/pallas_call | solution.py:293
  66.2 3.5 %collective-permute-done.11.refs_11_ = bf16[256,2048]{1,0:T(8,128)(2,1)S(1)} collective-permute-done((bf16[256,2048]{1,0:T(8,128)(2,1)S(1)}, bf16[256,2048]{1,0:T(8,128)(2,1)S(1)}, u32[]{:S(2)}, u32[]{:S(2)}) %collective-permute-start.11) | collective-permute-done | bytes 1048608 | tf_op jit(solution)/shard_map/ppermute | solution.py:449
  69.7 4.3 %grads.7 = (bf16[6,128,128]{2,1,0:T(8,128)(2,1)S(1)}, bf16[3,6,128,128]{3,2,1,0:T(8,128)(2,1)S(1)}) custom-call(s32[1024]{0:T(1024)S(1)} %reshape.15.refs_2_.refs_0_, bf16[256,1024]{1,0:T(8,128)(2,1)S(1)} %copy-done.3, bf16[256,1024]{1,0:T(8,128)(2,1)S(1)} %collective-permute-done.refs_2_, bf16[256,1024]{1,0:T(8,128)(2,1)S(1)} %gate.2.refs_3_, ...), custom_call_target="tpu_custom_call" | custom-call | tf_op jit(solution)/shard_map/grads/pallas_call | solution.py:234
  74.0 3.5 %collective-permute-start.16 = (bf16[3,6,128,128]{3,2,1,0:T(8,128)(2,1)S(1)}, bf16[3,6,128,128]{3,2,1,0:T(8,128)(2,1)S(1)}, u32[]{:S(2)}, u32[]{:S(2)}) collective-permute-start(bf16[3,6,128,128]{3,2,1,0:T(8,128)(2,1)S(1)} %get-tuple-element.44.refs_0_.refs_4_), channel_id=1, source_target_pairs={{0,8},{4,12},{24,16},{28,20},{1,9},{5,13},{25,17},{29,21},{2,10},{... | collective-permute-start | bytes 1769480 | tf_op jit(solution)/shard_map/ppermute | solution.py:449
  78.4 4.3 %grads.8 = (bf16[6,128,128]{2,1,0:T(8,128)(2,1)S(1)}, bf16[3,6,128,128]{3,2,1,0:T(8,128)(2,1)S(1)}) custom-call(s32[1024]{0:T(1024)S(1)} %reshape.15.refs_2_.refs_0_, bf16[256,1024]{1,0:T(8,128)(2,1)S(1)} %copy-done.3, bf16[256,1024]{1,0:T(8,128)(2,1)S(1)} %collective-permute-done.refs_2_, bf16[256,1024]{1,0:T(8,128)(2,1)S(1)} %gate.2.refs_3_, ...), custom_call_target="tpu_custom_call" | custom-call | tf_op jit(solution)/shard_map/grads/pallas_call | solution.py:234
  82.8 6.9 %collective-permute-start.19 = (bf16[3,6,128,128]{3,2,1,0:T(8,128)(2,1)S(1)}, bf16[3,6,128,128]{3,2,1,0:T(8,128)(2,1)S(1)}, u32[]{:S(2)}, u32[]{:S(2)}) collective-permute-start(bf16[3,6,128,128]{3,2,1,0:T(8,128)(2,1)S(1)} %get-tuple-element.46.refs_0_.refs_2_.refs_6_), channel_id=1, source_target_pairs={{0,8},{4,12},{24,16},{28,20},{1,9},{5,13},{25,17},{29,21},{2,10},{... | collective-permute-start | bytes 1769480 | tf_op jit(solution)/shard_map/ppermute | solution.py:449
  90.7 1.5 %collective-permute-start.15 = (bf16[1,256,1024]{2,1,0:T(8,128)(2,1)S(1)}, bf16[1,256,1024]{2,1,0:T(8,128)(2,1)S(1)}, u32[]{:S(2)}, u32[]{:S(2)}) collective-permute-start(bf16[1,256,1024]{2,1,0:T(8,128)(2,1)S(1)} %relay.8.refs_6_), channel_id=1, source_target_pairs={{0,2},{1,3},{2,0},{3,1},{4,6},{5,7},{6,4},{7,5},{8,10},{9,11},{10,... | collective-permute-start | bytes 1572872 | tf_op jit(solution)/shard_map/ppermute | solution.py:449
  94.9 1.4 %collective-permute-start.24 = (bf16[1,16,128,128]{3,2,1,0:T(8,128)(2,1)S(1)}, bf16[1,16,128,128]{3,2,1,0:T(8,128)(2,1)S(1)}, u32[]{:S(2)}, u32[]{:S(2)}) collective-permute-start(bf16[1,16,128,128]{3,2,1,0:T(8,128)(2,1)S(1)} %get-tuple-element.52), channel_id=1, source_target_pairs={{8,0},{12,4},{16,24},{20,28},{9,1},{13,5},{17,25},{21,29},{10,2},{... | collective-permute-start | bytes 1572872 | tf_op jit(solution)/shard_map/ppermute | solution.py:449
  96.4 3.0 %grads.9 = (bf16[4,128,128]{2,1,0:T(8,128)(2,1)S(1)}, bf16[3,4,128,128]{3,2,1,0:T(8,128)(2,1)S(1)}) custom-call(s32[1024]{0:T(1024)S(1)} %reshape.15.refs_2_.refs_0_, bf16[256,1024]{1,0:T(8,128)(2,1)S(1)} %copy-done.3, bf16[256,1024]{1,0:T(8,128)(2,1)S(1)} %collective-permute-done.refs_2_, bf16[256,1024]{1,0:T(8,128)(2,1)S(1)} %gate.2.refs_3_, ...), custom_call_target="tpu_custom_call" | custom-call | tf_op jit(solution)/shard_map/grads/pallas_call | solution.py:234
  99.4 7.0 %collective-permute-start.23 = (bf16[3,4,128,128]{3,2,1,0:T(8,128)(2,1)S(1)}, bf16[3,4,128,128]{3,2,1,0:T(8,128)(2,1)S(1)}, u32[]{:S(2)}, u32[]{:S(2)}) collective-permute-start(bf16[3,4,128,128]{3,2,1,0:T(8,128)(2,1)S(1)} %get-tuple-element.47.refs_7_.refs_0_.refs_2_), channel_id=1, source_target_pairs={{0,8},{4,12},{24,16},{28,20},{1,9},{5,13},{25,17},{29,21},{2,10},{... | collective-permute-start | bytes 1179656 | tf_op jit(solution)/shard_map/ppermute | solution.py:449
  106.6 1.4 %collective-permute-start.20 = (bf16[1,16,128,128]{3,2,1,0:T(8,128)(2,1)S(1)}, bf16[1,16,128,128]{3,2,1,0:T(8,128)(2,1)S(1)}, u32[]{:S(2)}, u32[]{:S(2)}) collective-permute-start(bf16[1,16,128,128]{3,2,1,0:T(8,128)(2,1)S(1)} %get-tuple-element.49), channel_id=1, source_target_pairs={{8,0},{12,4},{16,24},{20,28},{9,1},{13,5},{17,25},{21,29},{10,2},{... | collective-permute-start | bytes 1572872 | tf_op jit(solution)/shard_map/ppermute | solution.py:449
  108.7 1.4 %collective-permute-start.22 = (bf16[1,6,128,128]{3,2,1,0:T(8,128)(2,1)S(1)}, bf16[1,6,128,128]{3,2,1,0:T(8,128)(2,1)S(1)}, u32[]{:S(2)}, u32[]{:S(2)}) collective-permute-start(bf16[1,6,128,128]{3,2,1,0:T(8,128)(2,1)S(1)} %get-tuple-element.51), channel_id=1, source_target_pairs={{8,24},{12,28},{16,0},{20,4},{9,25},{13,29},{17,1},{21,5},{10,26},... | collective-permute-start | bytes 589832 | tf_op jit(solution)/shard_map/ppermute | solution.py:449
  110.2 2.7 %collective-permute-done.23.refs_1_.refs_3_.refs_10_ = bf16[3,4,128,128]{3,2,1,0:T(8,128)(2,1)S(1)} collective-permute-done((bf16[3,4,128,128]{3,2,1,0:T(8,128)(2,1)S(1)}, bf16[3,4,128,128]{3,2,1,0:T(8,128)(2,1)S(1)}, u32[]{:S(2)}, u32[]{:S(2)}) %collective-permute-start.23) | collective-permute-done | bytes 393248 | tf_op jit(solution)/shard_map/ppermute | solution.py:449
  114.6 1.3 collective-permute-start.26
  118.2 8.0 %collective-permute-done.26.refs_12_ = bf16[1,4,128,128]{3,2,1,0:T(8,128)(2,1)S(1)} collective-permute-done((bf16[1,4,128,128]{3,2,1,0:T(8,128)(2,1)S(1)}, bf16[1,4,128,128]{3,2,1,0:T(8,128)(2,1)S(1)}, u32[]{:S(2)}, u32[]{:S(2)}) %collective-permute-start.26) | collective-permute-done | bytes 131104 | tf_op jit(solution)/shard_map/ppermute | solution.py:449
  126.2 3.4 %collective-permute-done.20.refs_3_.refs_8_.refs_13_ = bf16[1,16,128,128]{3,2,1,0:T(8,128)(2,1)S(1)} collective-permute-done((bf16[1,16,128,128]{3,2,1,0:T(8,128)(2,1)S(1)}, bf16[1,16,128,128]{3,2,1,0:T(8,128)(2,1)S(1)}, u32[]{:S(2)}, u32[]{:S(2)}) %collective-permute-start.20) | collective-permute-done | bytes 524320 | tf_op jit(solution)/shard_map/ppermute | solution.py:449
  (84 shorter events, 14.4 us)
Async XLA Ops:
  0.6 15.1 %collective-permute-start.1 = (bf16[256,1024]{1,0:T(8,128)(2,1)}, bf16[256,1024]{1,0:T(8,128)(2,1)S(1)}, u32[]{:S(2)}, u32[]{:S(2)}) collective-permute-start(bf16[256,1024]{1,0:T(8,128)(2,1)} %refs_1_.13), channel_id=1, source_target_pairs={{0,2},{1,3},{2,0},{3,1},{4,6},{5,7},{6,4},{7,5},{8,10},{9,11},{10,... | collective-permute-start | bytes 1572872 | tf_op jit(solution)/shard_map/ppermute | solution.py:449
  3.6 15.0 %collective-permute-start.3 = (bf16[256,1024]{1,0:T(8,128)(2,1)}, bf16[256,1024]{1,0:T(8,128)(2,1)}, u32[]{:S(2)}, u32[]{:S(2)}) collective-permute-start(bf16[256,1024]{1,0:T(8,128)(2,1)} %refs_1_.13), channel_id=1, source_target_pairs={{0,4},{4,0},{8,12},{12,8},{16,20},{20,16},{24,28},{28,24},{1,5},{5... | collective-permute-start | bytes 1572872 | tf_op jit(solution)/shard_map/ppermute | solution.py:449
  5.2 14.9 %collective-permute-start = (bf16[256,1024]{1,0:T(8,128)(2,1)}, bf16[256,1024]{1,0:T(8,128)(2,1)S(1)}, u32[]{:S(2)}, u32[]{:S(2)}) collective-permute-start(bf16[256,1024]{1,0:T(8,128)(2,1)} %refs_1_.13), channel_id=1, source_target_pairs={{0,1},{1,0},{2,3},{3,2},{4,5},{5,4},{6,7},{7,6},{8,9},{9,8},{10,11... | collective-permute-start | bytes 1572872 | tf_op jit(solution)/shard_map/ppermute | solution.py:449
  16.8 3.3 %collective-permute-start.2 = (bf16[256,1024]{1,0:T(8,128)(2,1)S(1)}, bf16[256,1024]{1,0:T(8,128)(2,1)S(1)}, u32[]{:S(2)}, u32[]{:S(2)}) collective-permute-start(bf16[256,1024]{1,0:T(8,128)(2,1)S(1)} %gate.2.refs_3_), channel_id=1, source_target_pairs={{0,1},{1,0},{2,3},{3,2},{4,5},{5,4},{6,7},{7,6},{8,9},{9,8},{10,11... | collective-permute-start | bytes 1572872 | tf_op jit(solution)/shard_map/ppermute | solution.py:449
  16.8 14.6 %collective-permute-start.6 = (bf16[256,1024]{1,0:T(8,128)(2,1)}, bf16[256,1024]{1,0:T(8,128)(2,1)S(1)}, u32[]{:S(2)}, u32[]{:S(2)}) collective-permute-start(bf16[256,1024]{1,0:T(8,128)(2,1)} %cut.1.refs_1_), channel_id=1, source_target_pairs={{0,4},{4,0},{8,12},{12,8},{16,20},{20,16},{24,28},{28,24},{1,5},{5... | collective-permute-start | bytes 1572872 | tf_op jit(solution)/shard_map/ppermute | solution.py:449
  18.6 14.3 %collective-permute-start.5 = (bf16[256,1024]{1,0:T(8,128)(2,1)}, bf16[256,1024]{1,0:T(8,128)(2,1)S(1)}, u32[]{:S(2)}, u32[]{:S(2)}) collective-permute-start(bf16[256,1024]{1,0:T(8,128)(2,1)} %collective-permute-done.3.refs_5_), channel_id=1, source_target_pairs={{0,2},{1,3},{2,0},{3,1},{4,6},{5,7},{6,4},{7,5},{8,10},{9,11},{10,... | collective-permute-start | bytes 1572872 | tf_op jit(solution)/shard_map/ppermute | solution.py:449
  20.1 14.8 %collective-permute-start.4 = (bf16[256,1024]{1,0:T(8,128)(2,1)}, bf16[256,1024]{1,0:T(8,128)(2,1)S(1)}, u32[]{:S(2)}, u32[]{:S(2)}) collective-permute-start(bf16[256,1024]{1,0:T(8,128)(2,1)} %collective-permute-done.3.refs_5_), channel_id=1, source_target_pairs={{0,1},{1,0},{2,3},{3,2},{4,5},{5,4},{6,7},{7,6},{8,9},{9,8},{10,11... | collective-permute-start | bytes 1572872 | tf_op jit(solution)/shard_map/ppermute | solution.py:449
  23.5 54.9 %copy-start.4 = (bf16[256,1024]{1,0:T(8,128)(2,1)}, bf16[256,1024]{1,0:T(8,128)(2,1)S(1)}, u32[]{:S(2)}) copy-start(bf16[256,1024]{1,0:T(8,128)(2,1)S(1)} %collective-permute-done.2.refs_4_) | copy-start | bytes 1572868
  32.9 45.5 %copy-start.6 = (bf16[256,1024]{1,0:T(8,128)(2,1)}, bf16[256,1024]{1,0:T(8,128)(2,1)S(1)}, u32[]{:S(2)}) copy-start(bf16[256,1024]{1,0:T(8,128)(2,1)S(1)} %gate.3.refs_7_) | copy-start | bytes 1572868
  32.9 2.0 %collective-permute-start.7 = (bf16[256,1024]{1,0:T(8,128)(2,1)S(1)}, bf16[256,1024]{1,0:T(8,128)(2,1)S(1)}, u32[]{:S(2)}, u32[]{:S(2)}) collective-permute-start(bf16[256,1024]{1,0:T(8,128)(2,1)S(1)} %gate.3.refs_7_), channel_id=1, source_target_pairs={{0,1},{1,0},{2,3},{3,2},{4,5},{5,4},{6,7},{7,6},{8,9},{9,8},{10,11... | collective-permute-start | bytes 1572872 | tf_op jit(solution)/shard_map/ppermute | solution.py:449
  32.9 16.1 %collective-permute-start.8 = (bf16[256,1024]{1,0:T(8,128)(2,1)S(1)}, bf16[256,1024]{1,0:T(8,128)(2,1)S(1)}, u32[]{:S(2)}, u32[]{:S(2)}) collective-permute-start(bf16[256,1024]{1,0:T(8,128)(2,1)S(1)} %get-tuple-element.34), channel_id=1, source_target_pairs={{0,4},{4,0},{8,12},{12,8},{16,20},{20,16},{24,28},{28,24},{1,5},{5... | collective-permute-start | bytes 1572872 | tf_op jit(solution)/shard_map/ppermute | solution.py:449
  33.2 36.5 %collective-permute-start.11 = (bf16[256,2048]{1,0:T(8,128)(2,1)S(1)}, bf16[256,2048]{1,0:T(8,128)(2,1)S(1)}, u32[]{:S(2)}, u32[]{:S(2)}) collective-permute-start(bf16[256,2048]{1,0:T(8,128)(2,1)S(1)} %get-tuple-element.39), channel_id=1, source_target_pairs={{0,4},{4,0},{8,12},{12,8},{16,20},{20,16},{24,28},{28,24},{1,5},{5... | collective-permute-start | bytes 3145736 | tf_op jit(solution)/shard_map/ppermute | solution.py:449
  34.9 14.1 %copy-start.8 = (bf16[256,1024]{1,0:T(8,128)(2,1)}, bf16[256,1024]{1,0:T(8,128)(2,1)S(1)}, u32[]{:S(2)}) copy-start(bf16[256,1024]{1,0:T(8,128)(2,1)S(1)} %collective-permute-done.4.refs_6_) | copy-start | bytes 1572868
  39.7 25.1 %copy-start.10 = (bf16[3,8,128,128]{3,2,1,0:T(8,128)(2,1)}, bf16[3,8,128,128]{3,2,1,0:T(8,128)(2,1)S(1)}, u32[]{:S(2)}) copy-start(bf16[3,8,128,128]{3,2,1,0:T(8,128)(2,1)S(1)} %get-tuple-element.41.refs_0_.refs_2_) | copy-start | bytes 2359300
  39.7 25.1 %collective-permute-start.13 = (bf16[3,8,128,128]{3,2,1,0:T(8,128)(2,1)S(1)}, bf16[3,8,128,128]{3,2,1,0:T(8,128)(2,1)S(1)}, u32[]{:S(2)}, u32[]{:S(2)}) collective-permute-start(bf16[3,8,128,128]{3,2,1,0:T(8,128)(2,1)S(1)} %get-tuple-element.41.refs_0_.refs_2_), channel_id=1, source_target_pairs={{0,8},{4,12},{24,16},{28,20},{1,9},{5,13},{25,17},{29,21},{2,10},{... | collective-permute-start | bytes 2359304 | tf_op jit(solution)/shard_map/ppermute | solution.py:449
  53.8 23.8 %collective-permute-start.12 = (bf16[3,8,128,128]{3,2,1,0:T(8,128)(2,1)S(1)}, bf16[3,8,128,128]{3,2,1,0:T(8,128)(2,1)S(1)}, u32[]{:S(2)}, u32[]{:S(2)}) collective-permute-start(bf16[3,8,128,128]{3,2,1,0:T(8,128)(2,1)S(1)} %get-tuple-element.40.refs_0_.refs_4_), channel_id=1, source_target_pairs={{0,8},{4,12},{24,16},{28,20},{1,9},{5,13},{25,17},{29,21},{2,10},{... | collective-permute-start | bytes 2359304 | tf_op jit(solution)/shard_map/ppermute | solution.py:449
  64.9 13.5 %collective-permute-start.14 = (bf16[2,8,128,128]{3,2,1,0:T(8,128)(2,1)S(1)}, bf16[2,8,128,128]{3,2,1,0:T(8,128)(2,1)S(1)}, u32[]{:S(2)}, u32[]{:S(2)}) collective-permute-start(bf16[2,8,128,128]{3,2,1,0:T(8,128)(2,1)S(1)} %relay.6.refs_12_), channel_id=1, source_target_pairs={{8,16},{12,20},{16,8},{20,12},{9,17},{13,21},{17,9},{21,13},{10,18... | collective-permute-start | bytes 1572872 | tf_op jit(solution)/shard_map/ppermute | solution.py:449
  65.6 24.1 %collective-permute-start.10 = (bf16[1,256,1024]{2,1,0:T(8,128)(2,1)S(1)}, bf16[1,256,1024]{2,1,0:T(8,128)(2,1)S(1)}, u32[]{:S(2)}, u32[]{:S(2)}) collective-permute-start(bf16[1,256,1024]{2,1,0:T(8,128)(2,1)S(1)} %get-tuple-element.38), channel_id=1, source_target_pairs={{0,1},{1,0},{2,3},{3,2},{4,5},{5,4},{6,7},{7,6},{8,9},{9,8},{10,11... | collective-permute-start | bytes 1572872 | tf_op jit(solution)/shard_map/ppermute | solution.py:449
  65.7 24.0 %collective-permute-start.9 = (bf16[1,256,1024]{2,1,0:T(8,128)(2,1)}, bf16[1,256,1024]{2,1,0:T(8,128)(2,1)S(1)}, u32[]{:S(2)}, u32[]{:S(2)}) collective-permute-start(bf16[1,256,1024]{2,1,0:T(8,128)(2,1)} %get-tuple-element.37), channel_id=1, source_target_pairs={{0,1},{1,0},{2,3},{3,2},{4,5},{5,4},{6,7},{7,6},{8,9},{9,8},{10,11... | collective-permute-start | bytes 1572872 | tf_op jit(solution)/shard_map/ppermute | solution.py:449
  74.0 19.0 %copy-start.12 = (bf16[3,6,128,128]{3,2,1,0:T(8,128)(2,1)}, bf16[3,6,128,128]{3,2,1,0:T(8,128)(2,1)S(1)}, u32[]{:S(2)}) copy-start(bf16[3,6,128,128]{3,2,1,0:T(8,128)(2,1)S(1)} %get-tuple-element.44.refs_0_.refs_4_) | copy-start | bytes 1769476
  74.0 18.9 %collective-permute-start.16 = (bf16[3,6,128,128]{3,2,1,0:T(8,128)(2,1)S(1)}, bf16[3,6,128,128]{3,2,1,0:T(8,128)(2,1)S(1)}, u32[]{:S(2)}, u32[]{:S(2)}) collective-permute-start(bf16[3,6,128,128]{3,2,1,0:T(8,128)(2,1)S(1)} %get-tuple-element.44.refs_0_.refs_4_), channel_id=1, source_target_pairs={{0,8},{4,12},{24,16},{28,20},{1,9},{5,13},{25,17},{29,21},{2,10},{... | collective-permute-start | bytes 1769480 | tf_op jit(solution)/shard_map/ppermute | solution.py:449
  77.7 14.5 %collective-permute-start.17 = (bf16[2,8,128,128]{3,2,1,0:T(8,128)(2,1)S(1)}, bf16[2,8,128,128]{3,2,1,0:T(8,128)(2,1)S(1)}, u32[]{:S(2)}, u32[]{:S(2)}) collective-permute-start(bf16[2,8,128,128]{3,2,1,0:T(8,128)(2,1)S(1)} %relay.7.refs_12_), channel_id=1, source_target_pairs={{8,16},{12,20},{16,8},{20,12},{9,17},{13,21},{17,9},{21,13},{10,18... | collective-permute-start | bytes 1572872 | tf_op jit(solution)/shard_map/ppermute | solution.py:449
  82.8 23.7 %collective-permute-start.19 = (bf16[3,6,128,128]{3,2,1,0:T(8,128)(2,1)S(1)}, bf16[3,6,128,128]{3,2,1,0:T(8,128)(2,1)S(1)}, u32[]{:S(2)}, u32[]{:S(2)}) collective-permute-start(bf16[3,6,128,128]{3,2,1,0:T(8,128)(2,1)S(1)} %get-tuple-element.46.refs_0_.refs_2_.refs_6_), channel_id=1, source_target_pairs={{0,8},{4,12},{24,16},{28,20},{1,9},{5,13},{25,17},{29,21},{2,10},{... | collective-permute-start | bytes 1769480 | tf_op jit(solution)/shard_map/ppermute | solution.py:449
  90.7 15.8 %collective-permute-start.15 = (bf16[1,256,1024]{2,1,0:T(8,128)(2,1)S(1)}, bf16[1,256,1024]{2,1,0:T(8,128)(2,1)S(1)}, u32[]{:S(2)}, u32[]{:S(2)}) collective-permute-start(bf16[1,256,1024]{2,1,0:T(8,128)(2,1)S(1)} %relay.8.refs_6_), channel_id=1, source_target_pairs={{0,2},{1,3},{2,0},{3,1},{4,6},{5,7},{6,4},{7,5},{8,10},{9,11},{10,... | collective-permute-start | bytes 1572872 | tf_op jit(solution)/shard_map/ppermute | solution.py:449
  94.2 12.2 %collective-permute-start.18 = (bf16[2,6,128,128]{3,2,1,0:T(8,128)(2,1)S(1)}, bf16[2,6,128,128]{3,2,1,0:T(8,128)(2,1)S(1)}, u32[]{:S(2)}, u32[]{:S(2)}) collective-permute-start(bf16[2,6,128,128]{3,2,1,0:T(8,128)(2,1)S(1)} %get-tuple-element.45.refs_12_), channel_id=1, source_target_pairs={{8,16},{12,20},{16,8},{20,12},{9,17},{13,21},{17,9},{21,13},{10,18... | collective-permute-start | bytes 1179656 | tf_op jit(solution)/shard_map/ppermute | solution.py:449
  94.9 19.0 %collective-permute-start.24 = (bf16[1,16,128,128]{3,2,1,0:T(8,128)(2,1)S(1)}, bf16[1,16,128,128]{3,2,1,0:T(8,128)(2,1)S(1)}, u32[]{:S(2)}, u32[]{:S(2)}) collective-permute-start(bf16[1,16,128,128]{3,2,1,0:T(8,128)(2,1)S(1)} %get-tuple-element.52), channel_id=1, source_target_pairs={{8,0},{12,4},{16,24},{20,28},{9,1},{13,5},{17,25},{21,29},{10,2},{... | collective-permute-start | bytes 1572872 | tf_op jit(solution)/shard_map/ppermute | solution.py:449
  99.4 13.5 %collective-permute-start.23 = (bf16[3,4,128,128]{3,2,1,0:T(8,128)(2,1)S(1)}, bf16[3,4,128,128]{3,2,1,0:T(8,128)(2,1)S(1)}, u32[]{:S(2)}, u32[]{:S(2)}) collective-permute-start(bf16[3,4,128,128]{3,2,1,0:T(8,128)(2,1)S(1)} %get-tuple-element.47.refs_7_.refs_0_.refs_2_), channel_id=1, source_target_pairs={{0,8},{4,12},{24,16},{28,20},{1,9},{5,13},{25,17},{29,21},{2,10},{... | collective-permute-start | bytes 1179656 | tf_op jit(solution)/shard_map/ppermute | solution.py:449
  106.6 23.0 %collective-permute-start.20 = (bf16[1,16,128,128]{3,2,1,0:T(8,128)(2,1)S(1)}, bf16[1,16,128,128]{3,2,1,0:T(8,128)(2,1)S(1)}, u32[]{:S(2)}, u32[]{:S(2)}) collective-permute-start(bf16[1,16,128,128]{3,2,1,0:T(8,128)(2,1)S(1)} %get-tuple-element.49), channel_id=1, source_target_pairs={{8,0},{12,4},{16,24},{20,28},{9,1},{13,5},{17,25},{21,29},{10,2},{... | collective-permute-start | bytes 1572872 | tf_op jit(solution)/shard_map/ppermute | solution.py:449
  108.0 18.2 %collective-permute-start.21 = (bf16[1,6,128,128]{3,2,1,0:T(8,128)(2,1)S(1)}, bf16[1,6,128,128]{3,2,1,0:T(8,128)(2,1)S(1)}, u32[]{:S(2)}, u32[]{:S(2)}) collective-permute-start(bf16[1,6,128,128]{3,2,1,0:T(8,128)(2,1)S(1)} %get-tuple-element.50.refs_4_), channel_id=1, source_target_pairs={{8,16},{12,20},{16,8},{20,12},{9,17},{13,21},{17,9},{21,13},{10,18... | collective-permute-start | bytes 589832 | tf_op jit(solution)/shard_map/ppermute | solution.py:449
  108.7 17.5 %collective-permute-start.22 = (bf16[1,6,128,128]{3,2,1,0:T(8,128)(2,1)S(1)}, bf16[1,6,128,128]{3,2,1,0:T(8,128)(2,1)S(1)}, u32[]{:S(2)}, u32[]{:S(2)}) collective-permute-start(bf16[1,6,128,128]{3,2,1,0:T(8,128)(2,1)S(1)} %get-tuple-element.51), channel_id=1, source_target_pairs={{8,24},{12,28},{16,0},{20,4},{9,25},{13,29},{17,1},{21,5},{10,26},... | collective-permute-start | bytes 589832 | tf_op jit(solution)/shard_map/ppermute | solution.py:449
  113.9 4.3 %collective-permute-start.25 = (bf16[1,4,128,128]{3,2,1,0:T(8,128)(2,1)S(1)}, bf16[1,4,128,128]{3,2,1,0:T(8,128)(2,1)S(1)}, u32[]{:S(2)}, u32[]{:S(2)}) collective-permute-start(bf16[1,4,128,128]{3,2,1,0:T(8,128)(2,1)S(1)} %get-tuple-element.53.refs_8_), channel_id=1, source_target_pairs={{8,16},{12,20},{16,8},{20,12},{9,17},{13,21},{17,9},{21,13},{10,18... | collective-permute-start | bytes 393224 | tf_op jit(solution)/shard_map/ppermute | solution.py:449
  114.6 11.6 %collective-permute-start.26 = (bf16[1,4,128,128]{3,2,1,0:T(8,128)(2,1)S(1)}, bf16[1,4,128,128]{3,2,1,0:T(8,128)(2,1)S(1)}, u32[]{:S(2)}, u32[]{:S(2)}) collective-permute-start(bf16[1,4,128,128]{3,2,1,0:T(8,128)(2,1)S(1)} %get-tuple-element.54), channel_id=1, source_target_pairs={{8,24},{12,28},{16,0},{20,4},{9,25},{13,29},{17,1},{21,5},{10,26},... | collective-permute-start | bytes 393224 | tf_op jit(solution)/shard_map/ppermute | solution.py:449
  (15 other events, 102.2 us)

commit v4 on v3

--- a/solution.py
+++ b/solution.py
@@ -12,7 +12,7 @@
 BF16 = jnp.bfloat16
 ANY = pl.BlockSpec(memory_space=pl.ANY)
 PARAMS = pltpu.CompilerParams(
-    dimension_semantics=("arbitrary",), vmem_limit_bytes=36 * 1024 * 1024
+    dimension_semantics=("arbitrary",), vmem_limit_bytes=28 * 1024 * 1024
 )
 ALL = pltpu.CompilerParams(
     dimension_semantics=("arbitrary",), vmem_limit_bytes=60 * 1024 * 1024

time: 132 us -> 130 us (0.985)
  local copies, waits for them, and re-layouts: 7.98 us -> 5.31 us
    unnamed x41 -> x11, local copies, waits for them, and re-layouts: 7.89 us -> 5.22 us
  transfers between devices with their start and end apart: 27 -> 27, of which waited for: 8 -> 8; matrix products, arithmetic and copies ran while one was open for 1% -> 2% of each run, Pallas kernels for 35% -> 35%
where the time goes in v4:
time: 130 us; the launch traced here: 129 us
  Pallas kernels  46.2 us (36%)
  starting transfers between devices  44.5 us (34%)
  waiting for transfers between devices  30.9 us (24%)
  local copies, waits for them, and re-layouts  5.31 us (4%)
    ppermute x27, starting transfers between devices, permute(): return lambda x: lax.ppermute(x, axis, links)  44.5 us
    ppermute x27, waiting for transfers between devices, permute(): return lambda x: lax.ppermute(x, axis, links)  30.9 us
    pallas_call x5, Pallas kernels, grads(): pl.pallas_call(functools.partial(grads_kernel, len(mine), first, columns,...  21.1 us
    pallas_call x2, Pallas kernels, forward(): pl.pallas_call(functools.partial(forward_kernel, len(feats), first, colum...  11.8 us
    pallas_call x1, Pallas kernels, dinput(): pl.pallas_call(functools.partial(dinput_kernel, len(deltas), fold, groups...  8.02 us
    unnamed x11, local copies, waits for them, and re-layouts  5.22 us
  transfers between devices with their start and end apart: 27, of which 8 were waited for; matrix products, arithmetic and copies ran while one was open for 2% of the time, Pallas kernels for 35%

profile of v4, /device:TPU:0, one launch (start us, length us, event | category | flops | bytes accessed | tf_op | source)
XLA Modules:
  0.0 129.0 jit_solution(13872859976722540750)
XLA Ops:
  0.6 3.0 %collective-permute-start.1 = (bf16[256,1024]{1,0:T(8,128)(2,1)}, bf16[256,1024]{1,0:T(8,128)(2,1)S(1)}, u32[]{:S(2)}, u32[]{:S(2)}) collective-permute-start(bf16[256,1024]{1,0:T(8,128)(2,1)} %refs_1_.13), channel_id=1, source_target_pairs={{0,2},{1,3},{2,0},{3,1},{4,6},{5,7},{6,4},{7,5},{8,10},{9,11},{10,... | collective-permute-start | bytes 1572872 | tf_op jit(solution)/shard_map/ppermute | solution.py:449
  3.6 1.5 %collective-permute-start.3 = (bf16[256,1024]{1,0:T(8,128)(2,1)}, bf16[256,1024]{1,0:T(8,128)(2,1)}, u32[]{:S(2)}, u32[]{:S(2)}) collective-permute-start(bf16[256,1024]{1,0:T(8,128)(2,1)} %refs_1_.13), channel_id=1, source_target_pairs={{0,4},{4,0},{8,12},{12,8},{16,20},{20,16},{24,28},{28,24},{1,5},{5... | collective-permute-start | bytes 1572872 | tf_op jit(solution)/shard_map/ppermute | solution.py:449
  6.1 2.0 %cut.1.refs_1_ = bf16[256,1024]{1,0:T(8,128)(2,1)} custom-call(bf16[256,4096]{1,0:T(8,128)(2,1)} %refs_7_.3), custom_call_target="tpu_custom_call" | custom-call | tf_op jit(solution)/shard_map/cut/pallas_call | solution.py:362
  8.1 7.7 %collective-permute-done.1.refs_0_ = bf16[256,1024]{1,0:T(8,128)(2,1)S(1)} collective-permute-done((bf16[256,1024]{1,0:T(8,128)(2,1)}, bf16[256,1024]{1,0:T(8,128)(2,1)S(1)}, u32[]{:S(2)}, u32[]{:S(2)}) %collective-permute-start.1) | collective-permute-done | bytes 524320 | tf_op jit(solution)/shard_map/ppermute | solution.py:449
  16.8 1.8 %collective-permute-start.6 = (bf16[256,1024]{1,0:T(8,128)(2,1)}, bf16[256,1024]{1,0:T(8,128)(2,1)S(1)}, u32[]{:S(2)}, u32[]{:S(2)}) collective-permute-start(bf16[256,1024]{1,0:T(8,128)(2,1)} %cut.1.refs_1_), channel_id=1, source_target_pairs={{0,4},{4,0},{8,12},{12,8},{16,20},{20,16},{24,28},{28,24},{1,5},{5... | collective-permute-start | bytes 1572872 | tf_op jit(solution)/shard_map/ppermute | solution.py:449
  18.6 1.5 %collective-permute-start.5 = (bf16[256,1024]{1,0:T(8,128)(2,1)}, bf16[256,1024]{1,0:T(8,128)(2,1)S(1)}, u32[]{:S(2)}, u32[]{:S(2)}) collective-permute-start(bf16[256,1024]{1,0:T(8,128)(2,1)} %collective-permute-done.3.refs_5_), channel_id=1, source_target_pairs={{0,2},{1,3},{2,0},{3,1},{4,6},{5,7},{6,4},{7,5},{8,10},{9,11},{10,... | collective-permute-start | bytes 1572872 | tf_op jit(solution)/shard_map/ppermute | solution.py:449
  20.1 3.4 %copy-done = bf16[32,1024,128]{2,1,0:T(8,128)(2,1)S(1)} copy-done((bf16[32,1024,128]{2,1,0:T(8,128)(2,1)S(1)}, bf16[32,1024,128]{2,1,0:T(8,128)(2,1)}, u32[]{:S(2)}) %copy-start) | copy-done | bytes 8388632
  23.5 6.0 %forward.2 = (bf16[256,4096]{1,0:T(8,128)(2,1)}, bf16[256,2048]{1,0:T(8,128)(2,1)S(1)}, bf16[256,1024]{1,0:T(8,128)(2,1)S(1)}, bf16[256,2048]{1,0:T(8,128)(2,1)S(1)}) custom-call(s32[1024]{0:T(1024)S(1)} %reshape.15.refs_2_.refs_0_, bf16[256,1024]{1,0:T(8,128)(2,1)S(1)} %copy-done.3, bf16[256,1024]{1,0:T(8,128)(2,1)S(1)} %collective-permute-done.refs_2_, ...), custom_call_target="tpu_custom_call" | custom-call | tf_op jit(solution)/shard_map/forward/pallas_call | solution.py:156
  29.5 1.9 %collective-permute-done.6.refs_2_.refs_11_ = bf16[256,1024]{1,0:T(8,128)(2,1)S(1)} collective-permute-done((bf16[256,1024]{1,0:T(8,128)(2,1)}, bf16[256,1024]{1,0:T(8,128)(2,1)S(1)}, u32[]{:S(2)}, u32[]{:S(2)}) %collective-permute-start.6) | collective-permute-done | bytes 524320 | tf_op jit(solution)/shard_map/ppermute | solution.py:449
  31.4 1.5 %collective-permute-done.5.refs_0_ = bf16[256,1024]{1,0:T(8,128)(2,1)S(1)} collective-permute-done((bf16[256,1024]{1,0:T(8,128)(2,1)}, bf16[256,1024]{1,0:T(8,128)(2,1)S(1)}, u32[]{:S(2)}, u32[]{:S(2)}) %collective-permute-start.5) | collective-permute-done | bytes 524320 | tf_op jit(solution)/shard_map/ppermute | solution.py:449
  33.2 1.7 %collective-permute-start.11 = (bf16[256,2048]{1,0:T(8,128)(2,1)S(1)}, bf16[256,2048]{1,0:T(8,128)(2,1)S(1)}, u32[]{:S(2)}, u32[]{:S(2)}) collective-permute-start(bf16[256,2048]{1,0:T(8,128)(2,1)S(1)} %get-tuple-element.39), channel_id=1, source_target_pairs={{0,4},{4,0},{8,12},{12,8},{16,20},{20,16},{24,28},{28,24},{1,5},{5... | collective-permute-start | bytes 3145736 | tf_op jit(solution)/shard_map/ppermute | solution.py:449
  34.9 4.7 %grads.5 = (bf16[8,128,128]{2,1,0:T(8,128)(2,1)S(1)}, bf16[3,8,128,128]{3,2,1,0:T(8,128)(2,1)S(1)}) custom-call(s32[1024]{0:T(1024)S(1)} %reshape.15.refs_2_.refs_0_, bf16[256,1024]{1,0:T(8,128)(2,1)S(1)} %copy-done.3, bf16[256,1024]{1,0:T(8,128)(2,1)S(1)} %collective-permute-done.refs_2_, bf16[256,1024]{1,0:T(8,128)(2,1)S(1)} %gate.2.refs_3_, ...), custom_call_target="tpu_custom_call" | custom-call | tf_op jit(solution)/shard_map/grads/pallas_call | solution.py:234
  39.7 3.5 %collective-permute-start.13 = (bf16[3,8,128,128]{3,2,1,0:T(8,128)(2,1)S(1)}, bf16[3,8,128,128]{3,2,1,0:T(8,128)(2,1)S(1)}, u32[]{:S(2)}, u32[]{:S(2)}) collective-permute-start(bf16[3,8,128,128]{3,2,1,0:T(8,128)(2,1)S(1)} %get-tuple-element.41.refs_0_.refs_2_), channel_id=1, source_target_pairs={{0,8},{4,12},{24,16},{28,20},{1,9},{5,13},{25,17},{29,21},{2,10},{... | collective-permute-start | bytes 2359304 | tf_op jit(solution)/shard_map/ppermute | solution.py:449
  43.2 5.7 %forward.3 = (bf16[256,4096]{1,0:T(8,128)(2,1)}, bf16[256,2048]{1,0:T(8,128)(2,1)S(1)}) custom-call(s32[1024]{0:T(1024)S(1)} %reshape.15.refs_2_.refs_0_, bf16[256,1024]{1,0:T(8,128)(2,1)S(1)} %copy-done.3, bf16[256,1024]{1,0:T(8,128)(2,1)S(1)} %collective-permute-done.refs_2_, bf16[256,1024]{1,0:T(8,128)(2,1)S(1)} %gate.2.refs_3_, ...), custom_call_target="tpu_custom_call", output_to_operand_aliasing={{0}: (8, {})} | custom-call | tf_op jit(solution)/shard_map/forward/pallas_call | solution.py:156
  48.9 4.8 %grads.6 = (bf16[8,128,128]{2,1,0:T(8,128)(2,1)S(1)}, bf16[3,8,128,128]{3,2,1,0:T(8,128)(2,1)S(1)}) custom-call(s32[1024]{0:T(1024)S(1)} %reshape.15.refs_2_.refs_0_, bf16[256,1024]{1,0:T(8,128)(2,1)S(1)} %copy-done.3, bf16[256,1024]{1,0:T(8,128)(2,1)S(1)} %collective-permute-done.refs_2_, bf16[256,1024]{1,0:T(8,128)(2,1)S(1)} %gate.2.refs_3_, ...), custom_call_target="tpu_custom_call" | custom-call | tf_op jit(solution)/shard_map/grads/pallas_call | solution.py:234
  53.7 2.1 %collective-permute-start.12 = (bf16[3,8,128,128]{3,2,1,0:T(8,128)(2,1)S(1)}, bf16[3,8,128,128]{3,2,1,0:T(8,128)(2,1)S(1)}, u32[]{:S(2)}, u32[]{:S(2)}) collective-permute-start(bf16[3,8,128,128]{3,2,1,0:T(8,128)(2,1)S(1)} %get-tuple-element.40.refs_0_.refs_4_), channel_id=1, source_target_pairs={{0,8},{4,12},{24,16},{28,20},{1,9},{5,13},{25,17},{29,21},{2,10},{... | collective-permute-start | bytes 2359304 | tf_op jit(solution)/shard_map/ppermute | solution.py:449
  55.9 8.0 %dinput.1 = (bf16[2,256,1024]{2,1,0:T(8,128)(2,1)S(1)}, bf16[1,256,1024]{2,1,0:T(8,128)(2,1)S(1)}, bf16[1,256,1024]{2,1,0:T(8,128)(2,1)S(1)}) custom-call(s32[1024]{0:T(1024)S(1)} %reshape.15.refs_2_.refs_0_, bf16[256,2048]{1,0:T(8,128)(2,1)S(1)} %get-tuple-element.30.refs_1_.refs_10_, bf16[256,2048]{1,0:T(8,128)(2,1)S(1)} %get-tuple-element.33.refs_12_.refs_2_.refs_10_, ...), custom_call_target="tpu_custom_call" | custom-call | tf_op jit(solution)/shard_map/dinput/pallas_call | solution.py:293
  65.3 4.3 %collective-permute-done.11.refs_11_ = bf16[256,2048]{1,0:T(8,128)(2,1)S(1)} collective-permute-done((bf16[256,2048]{1,0:T(8,128)(2,1)S(1)}, bf16[256,2048]{1,0:T(8,128)(2,1)S(1)}, u32[]{:S(2)}, u32[]{:S(2)}) %collective-permute-start.11) | collective-permute-done | bytes 1048608 | tf_op jit(solution)/shard_map/ppermute | solution.py:449
  69.7 4.3 %grads.7 = (bf16[6,128,128]{2,1,0:T(8,128)(2,1)S(1)}, bf16[3,6,128,128]{3,2,1,0:T(8,128)(2,1)S(1)}) custom-call(s32[1024]{0:T(1024)S(1)} %reshape.15.refs_2_.refs_0_, bf16[256,1024]{1,0:T(8,128)(2,1)S(1)} %copy-done.3, bf16[256,1024]{1,0:T(8,128)(2,1)S(1)} %collective-permute-done.refs_2_, bf16[256,1024]{1,0:T(8,128)(2,1)S(1)} %gate.2.refs_3_, ...), custom_call_target="tpu_custom_call" | custom-call | tf_op jit(solution)/shard_map/grads/pallas_call | solution.py:234
  74.0 3.5 %collective-permute-start.16 = (bf16[3,6,128,128]{3,2,1,0:T(8,128)(2,1)S(1)}, bf16[3,6,128,128]{3,2,1,0:T(8,128)(2,1)S(1)}, u32[]{:S(2)}, u32[]{:S(2)}) collective-permute-start(bf16[3,6,128,128]{3,2,1,0:T(8,128)(2,1)S(1)} %get-tuple-element.44.refs_0_.refs_4_), channel_id=1, source_target_pairs={{0,8},{4,12},{24,16},{28,20},{1,9},{5,13},{25,17},{29,21},{2,10},{... | collective-permute-start | bytes 1769480 | tf_op jit(solution)/shard_map/ppermute | solution.py:449
  78.4 4.3 %grads.8 = (bf16[6,128,128]{2,1,0:T(8,128)(2,1)S(1)}, bf16[3,6,128,128]{3,2,1,0:T(8,128)(2,1)S(1)}) custom-call(s32[1024]{0:T(1024)S(1)} %reshape.15.refs_2_.refs_0_, bf16[256,1024]{1,0:T(8,128)(2,1)S(1)} %copy-done.3, bf16[256,1024]{1,0:T(8,128)(2,1)S(1)} %collective-permute-done.refs_2_, bf16[256,1024]{1,0:T(8,128)(2,1)S(1)} %gate.2.refs_3_, ...), custom_call_target="tpu_custom_call" | custom-call | tf_op jit(solution)/shard_map/grads/pallas_call | solution.py:234
  82.7 6.8 %collective-permute-start.19 = (bf16[3,6,128,128]{3,2,1,0:T(8,128)(2,1)S(1)}, bf16[3,6,128,128]{3,2,1,0:T(8,128)(2,1)S(1)}, u32[]{:S(2)}, u32[]{:S(2)}) collective-permute-start(bf16[3,6,128,128]{3,2,1,0:T(8,128)(2,1)S(1)} %get-tuple-element.46.refs_0_.refs_2_.refs_6_), channel_id=1, source_target_pairs={{0,8},{4,12},{24,16},{28,20},{1,9},{5,13},{25,17},{29,21},{2,10},{... | collective-permute-start | bytes 1769480 | tf_op jit(solution)/shard_map/ppermute | solution.py:449
  89.7 1.6 %collective-permute-start.15 = (bf16[1,256,1024]{2,1,0:T(8,128)(2,1)S(1)}, bf16[1,256,1024]{2,1,0:T(8,128)(2,1)S(1)}, u32[]{:S(2)}, u32[]{:S(2)}) collective-permute-start(bf16[1,256,1024]{2,1,0:T(8,128)(2,1)S(1)} %relay.8.refs_6_), channel_id=1, source_target_pairs={{0,2},{1,3},{2,0},{3,1},{4,6},{5,7},{6,4},{7,5},{8,10},{9,11},{10,... | collective-permute-start | bytes 1572872 | tf_op jit(solution)/shard_map/ppermute | solution.py:449
  92.1 1.3 %collective-permute-start.24 = (bf16[1,16,128,128]{3,2,1,0:T(8,128)(2,1)S(1)}, bf16[1,16,128,128]{3,2,1,0:T(8,128)(2,1)S(1)}, u32[]{:S(2)}, u32[]{:S(2)}) collective-permute-start(bf16[1,16,128,128]{3,2,1,0:T(8,128)(2,1)S(1)} %get-tuple-element.52), channel_id=1, source_target_pairs={{8,0},{12,4},{16,24},{20,28},{9,1},{13,5},{17,25},{21,29},{10,2},{... | collective-permute-start | bytes 1572872 | tf_op jit(solution)/shard_map/ppermute | solution.py:449
  93.4 3.0 %grads.9 = (bf16[4,128,128]{2,1,0:T(8,128)(2,1)S(1)}, bf16[3,4,128,128]{3,2,1,0:T(8,128)(2,1)S(1)}) custom-call(s32[1024]{0:T(1024)S(1)} %reshape.15.refs_2_.refs_0_, bf16[256,1024]{1,0:T(8,128)(2,1)S(1)} %copy-done.3, bf16[256,1024]{1,0:T(8,128)(2,1)S(1)} %collective-permute-done.refs_2_, bf16[256,1024]{1,0:T(8,128)(2,1)S(1)} %gate.2.refs_3_, ...), custom_call_target="tpu_custom_call" | custom-call | tf_op jit(solution)/shard_map/grads/pallas_call | solution.py:234
  96.4 8.0 %collective-permute-start.23 = (bf16[3,4,128,128]{3,2,1,0:T(8,128)(2,1)S(1)}, bf16[3,4,128,128]{3,2,1,0:T(8,128)(2,1)S(1)}, u32[]{:S(2)}, u32[]{:S(2)}) collective-permute-start(bf16[3,4,128,128]{3,2,1,0:T(8,128)(2,1)S(1)} %get-tuple-element.47.refs_7_.refs_0_.refs_2_), channel_id=1, source_target_pairs={{0,8},{4,12},{24,16},{28,20},{1,9},{5,13},{25,17},{29,21},{2,10},{... | collective-permute-start | bytes 1179656 | tf_op jit(solution)/shard_map/ppermute | solution.py:449
  104.6 1.3 %collective-permute-start.20 = (bf16[1,16,128,128]{3,2,1,0:T(8,128)(2,1)S(1)}, bf16[1,16,128,128]{3,2,1,0:T(8,128)(2,1)S(1)}, u32[]{:S(2)}, u32[]{:S(2)}) collective-permute-start(bf16[1,16,128,128]{3,2,1,0:T(8,128)(2,1)S(1)} %get-tuple-element.49), channel_id=1, source_target_pairs={{8,0},{12,4},{16,24},{20,28},{9,1},{13,5},{17,25},{21,29},{10,2},{... | collective-permute-start | bytes 1572872 | tf_op jit(solution)/shard_map/ppermute | solution.py:449
  106.6 1.3 %collective-permute-start.22 = (bf16[1,6,128,128]{3,2,1,0:T(8,128)(2,1)S(1)}, bf16[1,6,128,128]{3,2,1,0:T(8,128)(2,1)S(1)}, u32[]{:S(2)}, u32[]{:S(2)}) collective-permute-start(bf16[1,6,128,128]{3,2,1,0:T(8,128)(2,1)S(1)} %get-tuple-element.51), channel_id=1, source_target_pairs={{8,24},{12,28},{16,0},{20,4},{9,25},{13,29},{17,1},{21,5},{10,26},... | collective-permute-start | bytes 589832 | tf_op jit(solution)/shard_map/ppermute | solution.py:449
  107.9 3.1 %collective-permute-done.23.refs_1_.refs_3_.refs_10_ = bf16[3,4,128,128]{3,2,1,0:T(8,128)(2,1)S(1)} collective-permute-done((bf16[3,4,128,128]{3,2,1,0:T(8,128)(2,1)S(1)}, bf16[3,4,128,128]{3,2,1,0:T(8,128)(2,1)S(1)}, u32[]{:S(2)}, u32[]{:S(2)}) %collective-permute-start.23) | collective-permute-done | bytes 393248 | tf_op jit(solution)/shard_map/ppermute | solution.py:449
  112.9 1.3 %collective-permute-start.26 = (bf16[1,4,128,128]{3,2,1,0:T(8,128)(2,1)S(1)}, bf16[1,4,128,128]{3,2,1,0:T(8,128)(2,1)S(1)}, u32[]{:S(2)}, u32[]{:S(2)}) collective-permute-start(bf16[1,4,128,128]{3,2,1,0:T(8,128)(2,1)S(1)} %get-tuple-element.54), channel_id=1, source_target_pairs={{8,24},{12,28},{16,0},{20,4},{9,25},{13,29},{17,1},{21,5},{10,26},... | collective-permute-start | bytes 393224 | tf_op jit(solution)/shard_map/ppermute | solution.py:449
  116.5 7.7 %collective-permute-done.26.refs_12_ = bf16[1,4,128,128]{3,2,1,0:T(8,128)(2,1)S(1)} collective-permute-done((bf16[1,4,128,128]{3,2,1,0:T(8,128)(2,1)S(1)}, bf16[1,4,128,128]{3,2,1,0:T(8,128)(2,1)S(1)}, u32[]{:S(2)}, u32[]{:S(2)}) %collective-permute-start.26) | collective-permute-done | bytes 131104 | tf_op jit(solution)/shard_map/ppermute | solution.py:449
  124.2 3.6 %collective-permute-done.20.refs_3_.refs_8_.refs_13_ = bf16[1,16,128,128]{3,2,1,0:T(8,128)(2,1)S(1)} collective-permute-done((bf16[1,16,128,128]{3,2,1,0:T(8,128)(2,1)S(1)}, bf16[1,16,128,128]{3,2,1,0:T(8,128)(2,1)S(1)}, u32[]{:S(2)}, u32[]{:S(2)}) %collective-permute-start.20) | collective-permute-done | bytes 524320 | tf_op jit(solution)/shard_map/ppermute | solution.py:449
  (54 shorter events, 11.8 us)
Async XLA Ops:
  0.6 15.1 %collective-permute-start.1 = (bf16[256,1024]{1,0:T(8,128)(2,1)}, bf16[256,1024]{1,0:T(8,128)(2,1)S(1)}, u32[]{:S(2)}, u32[]{:S(2)}) collective-permute-start(bf16[256,1024]{1,0:T(8,128)(2,1)} %refs_1_.13), channel_id=1, source_target_pairs={{0,2},{1,3},{2,0},{3,1},{4,6},{5,7},{6,4},{7,5},{8,10},{9,11},{10,... | collective-permute-start | bytes 1572872 | tf_op jit(solution)/shard_map/ppermute | solution.py:449
  3.6 15.0 %collective-permute-start.3 = (bf16[256,1024]{1,0:T(8,128)(2,1)}, bf16[256,1024]{1,0:T(8,128)(2,1)}, u32[]{:S(2)}, u32[]{:S(2)}) collective-permute-start(bf16[256,1024]{1,0:T(8,128)(2,1)} %refs_1_.13), channel_id=1, source_target_pairs={{0,4},{4,0},{8,12},{12,8},{16,20},{20,16},{24,28},{28,24},{1,5},{5... | collective-permute-start | bytes 1572872 | tf_op jit(solution)/shard_map/ppermute | solution.py:449
  5.2 14.9 %collective-permute-start = (bf16[256,1024]{1,0:T(8,128)(2,1)}, bf16[256,1024]{1,0:T(8,128)(2,1)S(1)}, u32[]{:S(2)}, u32[]{:S(2)}) collective-permute-start(bf16[256,1024]{1,0:T(8,128)(2,1)} %refs_1_.13), channel_id=1, source_target_pairs={{0,1},{1,0},{2,3},{3,2},{4,5},{5,4},{6,7},{7,6},{8,9},{9,8},{10,11... | collective-permute-start | bytes 1572872 | tf_op jit(solution)/shard_map/ppermute | solution.py:449
  6.0 14.1 %copy-start.2 = (bf16[256,4096]{1,0:T(8,128)(2,1)S(1)}, bf16[256,4096]{1,0:T(8,128)(2,1)}, u32[]{:S(2)}) copy-start(bf16[256,4096]{1,0:T(8,128)(2,1)} %refs_7_.3) | copy-start | bytes 6291460
  6.0 14.1 %copy-start.3 = (bf16[256,1024]{1,0:T(8,128)(2,1)S(1)}, bf16[256,1024]{1,0:T(8,128)(2,1)}, u32[]{:S(2)}) copy-start(bf16[256,1024]{1,0:T(8,128)(2,1)} %refs_1_.13) | copy-start | bytes 1572868
  15.8 1.0 copy-start.4
  16.8 3.3 %collective-permute-start.2 = (bf16[256,1024]{1,0:T(8,128)(2,1)S(1)}, bf16[256,1024]{1,0:T(8,128)(2,1)S(1)}, u32[]{:S(2)}, u32[]{:S(2)}) collective-permute-start(bf16[256,1024]{1,0:T(8,128)(2,1)S(1)} %gate.2.refs_3_), channel_id=1, source_target_pairs={{0,1},{1,0},{2,3},{3,2},{4,5},{5,4},{6,7},{7,6},{8,9},{9,8},{10,11... | collective-permute-start | bytes 1572872 | tf_op jit(solution)/shard_map/ppermute | solution.py:449
  16.8 14.6 %collective-permute-start.6 = (bf16[256,1024]{1,0:T(8,128)(2,1)}, bf16[256,1024]{1,0:T(8,128)(2,1)S(1)}, u32[]{:S(2)}, u32[]{:S(2)}) collective-permute-start(bf16[256,1024]{1,0:T(8,128)(2,1)} %cut.1.refs_1_), channel_id=1, source_target_pairs={{0,4},{4,0},{8,12},{12,8},{16,20},{20,16},{24,28},{28,24},{1,5},{5... | collective-permute-start | bytes 1572872 | tf_op jit(solution)/shard_map/ppermute | solution.py:449
  18.6 14.3 %collective-permute-start.5 = (bf16[256,1024]{1,0:T(8,128)(2,1)}, bf16[256,1024]{1,0:T(8,128)(2,1)S(1)}, u32[]{:S(2)}, u32[]{:S(2)}) collective-permute-start(bf16[256,1024]{1,0:T(8,128)(2,1)} %collective-permute-done.3.refs_5_), channel_id=1, source_target_pairs={{0,2},{1,3},{2,0},{3,1},{4,6},{5,7},{6,4},{7,5},{8,10},{9,11},{10,... | collective-permute-start | bytes 1572872 | tf_op jit(solution)/shard_map/ppermute | solution.py:449
  20.1 14.8 %collective-permute-start.4 = (bf16[256,1024]{1,0:T(8,128)(2,1)}, bf16[256,1024]{1,0:T(8,128)(2,1)S(1)}, u32[]{:S(2)}, u32[]{:S(2)}) collective-permute-start(bf16[256,1024]{1,0:T(8,128)(2,1)} %collective-permute-done.3.refs_5_), channel_id=1, source_target_pairs={{0,1},{1,0},{2,3},{3,2},{4,5},{5,4},{6,7},{7,6},{8,9},{9,8},{10,11... | collective-permute-start | bytes 1572872 | tf_op jit(solution)/shard_map/ppermute | solution.py:449
  20.1 3.4 %copy-start = (bf16[32,1024,128]{2,1,0:T(8,128)(2,1)S(1)}, bf16[32,1024,128]{2,1,0:T(8,128)(2,1)}, u32[]{:S(2)}) copy-start(bf16[32,1024,128]{2,1,0:T(8,128)(2,1)} %refs_9_.9) | copy-start | bytes 25165828
  23.5 11.4 %copy-start.1 = (bf16[32,1024,128]{2,1,0:T(8,128)(2,1)S(1)}, bf16[32,1024,128]{2,1,0:T(8,128)(2,1)}, u32[]{:S(2)}) copy-start(bf16[32,1024,128]{2,1,0:T(8,128)(2,1)} %refs_9_.9) | copy-start | bytes 25165828
  32.9 2.0 %collective-permute-start.7 = (bf16[256,1024]{1,0:T(8,128)(2,1)S(1)}, bf16[256,1024]{1,0:T(8,128)(2,1)S(1)}, u32[]{:S(2)}, u32[]{:S(2)}) collective-permute-start(bf16[256,1024]{1,0:T(8,128)(2,1)S(1)} %gate.3.refs_7_), channel_id=1, source_target_pairs={{0,1},{1,0},{2,3},{3,2},{4,5},{5,4},{6,7},{7,6},{8,9},{9,8},{10,11... | collective-permute-start | bytes 1572872 | tf_op jit(solution)/shard_map/ppermute | solution.py:449
  32.9 16.1 %collective-permute-start.8 = (bf16[256,1024]{1,0:T(8,128)(2,1)S(1)}, bf16[256,1024]{1,0:T(8,128)(2,1)S(1)}, u32[]{:S(2)}, u32[]{:S(2)}) collective-permute-start(bf16[256,1024]{1,0:T(8,128)(2,1)S(1)} %get-tuple-element.34), channel_id=1, source_target_pairs={{0,4},{4,0},{8,12},{12,8},{16,20},{20,16},{24,28},{28,24},{1,5},{5... | collective-permute-start | bytes 1572872 | tf_op jit(solution)/shard_map/ppermute | solution.py:449
  33.2 36.5 %collective-permute-start.11 = (bf16[256,2048]{1,0:T(8,128)(2,1)S(1)}, bf16[256,2048]{1,0:T(8,128)(2,1)S(1)}, u32[]{:S(2)}, u32[]{:S(2)}) collective-permute-start(bf16[256,2048]{1,0:T(8,128)(2,1)S(1)} %get-tuple-element.39), channel_id=1, source_target_pairs={{0,4},{4,0},{8,12},{12,8},{16,20},{20,16},{24,28},{28,24},{1,5},{5... | collective-permute-start | bytes 3145736 | tf_op jit(solution)/shard_map/ppermute | solution.py:449
  39.7 24.3 %collective-permute-start.13 = (bf16[3,8,128,128]{3,2,1,0:T(8,128)(2,1)S(1)}, bf16[3,8,128,128]{3,2,1,0:T(8,128)(2,1)S(1)}, u32[]{:S(2)}, u32[]{:S(2)}) collective-permute-start(bf16[3,8,128,128]{3,2,1,0:T(8,128)(2,1)S(1)} %get-tuple-element.41.refs_0_.refs_2_), channel_id=1, source_target_pairs={{0,8},{4,12},{24,16},{28,20},{1,9},{5,13},{25,17},{29,21},{2,10},{... | collective-permute-start | bytes 2359304 | tf_op jit(solution)/shard_map/ppermute | solution.py:449
  53.7 23.8 %collective-permute-start.12 = (bf16[3,8,128,128]{3,2,1,0:T(8,128)(2,1)S(1)}, bf16[3,8,128,128]{3,2,1,0:T(8,128)(2,1)S(1)}, u32[]{:S(2)}, u32[]{:S(2)}) collective-permute-start(bf16[3,8,128,128]{3,2,1,0:T(8,128)(2,1)S(1)} %get-tuple-element.40.refs_0_.refs_4_), channel_id=1, source_target_pairs={{0,8},{4,12},{24,16},{28,20},{1,9},{5,13},{25,17},{29,21},{2,10},{... | collective-permute-start | bytes 2359304 | tf_op jit(solution)/shard_map/ppermute | solution.py:449
  64.0 14.3 %collective-permute-start.14 = (bf16[2,8,128,128]{3,2,1,0:T(8,128)(2,1)S(1)}, bf16[2,8,128,128]{3,2,1,0:T(8,128)(2,1)S(1)}, u32[]{:S(2)}, u32[]{:S(2)}) collective-permute-start(bf16[2,8,128,128]{3,2,1,0:T(8,128)(2,1)S(1)} %relay.6.refs_12_), channel_id=1, source_target_pairs={{8,16},{12,20},{16,8},{20,12},{9,17},{13,21},{17,9},{21,13},{10,18... | collective-permute-start | bytes 1572872 | tf_op jit(solution)/shard_map/ppermute | solution.py:449
  64.7 24.8 %collective-permute-start.10 = (bf16[1,256,1024]{2,1,0:T(8,128)(2,1)S(1)}, bf16[1,256,1024]{2,1,0:T(8,128)(2,1)S(1)}, u32[]{:S(2)}, u32[]{:S(2)}) collective-permute-start(bf16[1,256,1024]{2,1,0:T(8,128)(2,1)S(1)} %get-tuple-element.38), channel_id=1, source_target_pairs={{0,1},{1,0},{2,3},{3,2},{4,5},{5,4},{6,7},{7,6},{8,9},{9,8},{10,11... | collective-permute-start | bytes 1572872 | tf_op jit(solution)/shard_map/ppermute | solution.py:449
  64.8 24.7 %collective-permute-start.9 = (bf16[1,256,1024]{2,1,0:T(8,128)(2,1)S(1)}, bf16[1,256,1024]{2,1,0:T(8,128)(2,1)S(1)}, u32[]{:S(2)}, u32[]{:S(2)}) collective-permute-start(bf16[1,256,1024]{2,1,0:T(8,128)(2,1)S(1)} %get-tuple-element.37), channel_id=1, source_target_pairs={{0,1},{1,0},{2,3},{3,2},{4,5},{5,4},{6,7},{7,6},{8,9},{9,8},{10,11... | collective-permute-start | bytes 1572872 | tf_op jit(solution)/shard_map/ppermute | solution.py:449
  74.0 17.3 %collective-permute-start.16 = (bf16[3,6,128,128]{3,2,1,0:T(8,128)(2,1)S(1)}, bf16[3,6,128,128]{3,2,1,0:T(8,128)(2,1)S(1)}, u32[]{:S(2)}, u32[]{:S(2)}) collective-permute-start(bf16[3,6,128,128]{3,2,1,0:T(8,128)(2,1)S(1)} %get-tuple-element.44.refs_0_.refs_4_), channel_id=1, source_target_pairs={{0,8},{4,12},{24,16},{28,20},{1,9},{5,13},{25,17},{29,21},{2,10},{... | collective-permute-start | bytes 1769480 | tf_op jit(solution)/shard_map/ppermute | solution.py:449
  77.7 13.6 %collective-permute-start.17 = (bf16[2,8,128,128]{3,2,1,0:T(8,128)(2,1)S(1)}, bf16[2,8,128,128]{3,2,1,0:T(8,128)(2,1)S(1)}, u32[]{:S(2)}, u32[]{:S(2)}) collective-permute-start(bf16[2,8,128,128]{3,2,1,0:T(8,128)(2,1)S(1)} %relay.7.refs_12_), channel_id=1, source_target_pairs={{8,16},{12,20},{16,8},{20,12},{9,17},{13,21},{17,9},{21,13},{10,18... | collective-permute-start | bytes 1572872 | tf_op jit(solution)/shard_map/ppermute | solution.py:449
  82.7 21.7 %collective-permute-start.19 = (bf16[3,6,128,128]{3,2,1,0:T(8,128)(2,1)S(1)}, bf16[3,6,128,128]{3,2,1,0:T(8,128)(2,1)S(1)}, u32[]{:S(2)}, u32[]{:S(2)}) collective-permute-start(bf16[3,6,128,128]{3,2,1,0:T(8,128)(2,1)S(1)} %get-tuple-element.46.refs_0_.refs_2_.refs_6_), channel_id=1, source_target_pairs={{0,8},{4,12},{24,16},{28,20},{1,9},{5,13},{25,17},{29,21},{2,10},{... | collective-permute-start | bytes 1769480 | tf_op jit(solution)/shard_map/ppermute | solution.py:449
  89.7 14.8 %collective-permute-start.15 = (bf16[1,256,1024]{2,1,0:T(8,128)(2,1)S(1)}, bf16[1,256,1024]{2,1,0:T(8,128)(2,1)S(1)}, u32[]{:S(2)}, u32[]{:S(2)}) collective-permute-start(bf16[1,256,1024]{2,1,0:T(8,128)(2,1)S(1)} %relay.8.refs_6_), channel_id=1, source_target_pairs={{0,2},{1,3},{2,0},{3,1},{4,6},{5,7},{6,4},{7,5},{8,10},{9,11},{10,... | collective-permute-start | bytes 1572872 | tf_op jit(solution)/shard_map/ppermute | solution.py:449
  91.5 13.0 %collective-permute-start.18 = (bf16[2,6,128,128]{3,2,1,0:T(8,128)(2,1)S(1)}, bf16[2,6,128,128]{3,2,1,0:T(8,128)(2,1)S(1)}, u32[]{:S(2)}, u32[]{:S(2)}) collective-permute-start(bf16[2,6,128,128]{3,2,1,0:T(8,128)(2,1)S(1)} %get-tuple-element.45.refs_12_), channel_id=1, source_target_pairs={{8,16},{12,20},{16,8},{20,12},{9,17},{13,21},{17,9},{21,13},{10,18... | collective-permute-start | bytes 1179656 | tf_op jit(solution)/shard_map/ppermute | solution.py:449
  92.1 20.0 %collective-permute-start.24 = (bf16[1,16,128,128]{3,2,1,0:T(8,128)(2,1)S(1)}, bf16[1,16,128,128]{3,2,1,0:T(8,128)(2,1)S(1)}, u32[]{:S(2)}, u32[]{:S(2)}) collective-permute-start(bf16[1,16,128,128]{3,2,1,0:T(8,128)(2,1)S(1)} %get-tuple-element.52), channel_id=1, source_target_pairs={{8,0},{12,4},{16,24},{20,28},{9,1},{13,5},{17,25},{21,29},{10,2},{... | collective-permute-start | bytes 1572872 | tf_op jit(solution)/shard_map/ppermute | solution.py:449
  96.4 14.6 %collective-permute-start.23 = (bf16[3,4,128,128]{3,2,1,0:T(8,128)(2,1)S(1)}, bf16[3,4,128,128]{3,2,1,0:T(8,128)(2,1)S(1)}, u32[]{:S(2)}, u32[]{:S(2)}) collective-permute-start(bf16[3,4,128,128]{3,2,1,0:T(8,128)(2,1)S(1)} %get-tuple-element.47.refs_7_.refs_0_.refs_2_), channel_id=1, source_target_pairs={{0,8},{4,12},{24,16},{28,20},{1,9},{5,13},{25,17},{29,21},{2,10},{... | collective-permute-start | bytes 1179656 | tf_op jit(solution)/shard_map/ppermute | solution.py:449
  104.6 23.1 %collective-permute-start.20 = (bf16[1,16,128,128]{3,2,1,0:T(8,128)(2,1)S(1)}, bf16[1,16,128,128]{3,2,1,0:T(8,128)(2,1)S(1)}, u32[]{:S(2)}, u32[]{:S(2)}) collective-permute-start(bf16[1,16,128,128]{3,2,1,0:T(8,128)(2,1)S(1)} %get-tuple-element.49), channel_id=1, source_target_pairs={{8,0},{12,4},{16,24},{20,28},{9,1},{13,5},{17,25},{21,29},{10,2},{... | collective-permute-start | bytes 1572872 | tf_op jit(solution)/shard_map/ppermute | solution.py:449
  105.9 18.2 %collective-permute-start.21 = (bf16[1,6,128,128]{3,2,1,0:T(8,128)(2,1)S(1)}, bf16[1,6,128,128]{3,2,1,0:T(8,128)(2,1)S(1)}, u32[]{:S(2)}, u32[]{:S(2)}) collective-permute-start(bf16[1,6,128,128]{3,2,1,0:T(8,128)(2,1)S(1)} %get-tuple-element.50.refs_4_), channel_id=1, source_target_pairs={{8,16},{12,20},{16,8},{20,12},{9,17},{13,21},{17,9},{21,13},{10,18... | collective-permute-start | bytes 589832 | tf_op jit(solution)/shard_map/ppermute | solution.py:449
  106.6 17.6 %collective-permute-start.22 = (bf16[1,6,128,128]{3,2,1,0:T(8,128)(2,1)S(1)}, bf16[1,6,128,128]{3,2,1,0:T(8,128)(2,1)S(1)}, u32[]{:S(2)}, u32[]{:S(2)}) collective-permute-start(bf16[1,6,128,128]{3,2,1,0:T(8,128)(2,1)S(1)} %get-tuple-element.51), channel_id=1, source_target_pairs={{8,24},{12,28},{16,0},{20,4},{9,25},{13,29},{17,1},{21,5},{10,26},... | collective-permute-start | bytes 589832 | tf_op jit(solution)/shard_map/ppermute | solution.py:449
  112.2 4.3 %collective-permute-start.25 = (bf16[1,4,128,128]{3,2,1,0:T(8,128)(2,1)S(1)}, bf16[1,4,128,128]{3,2,1,0:T(8,128)(2,1)S(1)}, u32[]{:S(2)}, u32[]{:S(2)}) collective-permute-start(bf16[1,4,128,128]{3,2,1,0:T(8,128)(2,1)S(1)} %get-tuple-element.53.refs_8_), channel_id=1, source_target_pairs={{8,16},{12,20},{16,8},{20,12},{9,17},{13,21},{17,9},{21,13},{10,18... | collective-permute-start | bytes 393224 | tf_op jit(solution)/shard_map/ppermute | solution.py:449
  112.9 11.3 %collective-permute-start.26 = (bf16[1,4,128,128]{3,2,1,0:T(8,128)(2,1)S(1)}, bf16[1,4,128,128]{3,2,1,0:T(8,128)(2,1)S(1)}, u32[]{:S(2)}, u32[]{:S(2)}) collective-permute-start(bf16[1,4,128,128]{3,2,1,0:T(8,128)(2,1)S(1)} %get-tuple-element.54), channel_id=1, source_target_pairs={{8,24},{12,28},{16,0},{20,4},{9,25},{13,29},{17,1},{21,5},{10,26},... | collective-permute-start | bytes 393224 | tf_op jit(solution)/shard_map/ppermute | solution.py:449

commit v5 on v4

--- a/solution.py
+++ b/solution.py
@@ -13,9 +13,6 @@
 ANY = pl.BlockSpec(memory_space=pl.ANY)
 PARAMS = pltpu.CompilerParams(
     dimension_semantics=("arbitrary",), vmem_limit_bytes=28 * 1024 * 1024
-)
-ALL = pltpu.CompilerParams(
-    dimension_semantics=("arbitrary",), vmem_limit_bytes=60 * 1024 * 1024
 )
 FEW = pltpu.CompilerParams(vmem_limit_bytes=1024 * 1024)
 STEP = 4
@@ -365,7 +362,7 @@
         in_specs=[spec],
         out_specs=spec,
         out_shape=jax.ShapeDtypeStruct((x.shape[0], width), x.dtype),
-        compiler_params=ALL,
+        compiler_params=PARAMS,
         name="cut",
     )(x)
 

time: 130 us -> 128 us (0.985)
  Pallas kernels: 46.2 us -> 41.1 us
  waiting for transfers between devices: 30.9 us -> 33 us
    pallas_call x5, Pallas kernels: 21.1 us -> 18 us  [grads(): pl.pallas_call(functools.partial(grads_kernel, len(mine), first, columns,...]
    ppermute x27, waiting for transfers between devices: 30.9 us -> 33 us  [permute(): return lambda x: lax.ppermute(x, axis, links)]
    pallas_call x1, Pallas kernels: 2.02 us -> 0.03 us  [cut(): pl.pallas_call(cut_kernel, grid=(1,), in_specs=[spec], out_specs=spec, ou...]
  transfers between devices with their start and end apart: 27 -> 27, of which waited for: 8 -> 9; matrix products, arithmetic and copies ran while one was open for 2% -> 2% of each run, Pallas kernels for 35% -> 31%
where the time goes in v5:
time: 128 us; the launch traced here: 127 us
  starting transfers between devices  45.1 us (35%)
  Pallas kernels  41.1 us (32%)
  waiting for transfers between devices  33 us (26%)
  local copies, waits for them, and re-layouts  5.85 us (5%)
    ppermute x27, starting transfers between devices, permute(): return lambda x: lax.ppermute(x, axis, links)  45.1 us
    ppermute x27, waiting for transfers between devices, permute(): return lambda x: lax.ppermute(x, axis, links)  33 us
    pallas_call x5, Pallas kernels, grads(): pl.pallas_call(functools.partial(grads_kernel, len(mine), first, columns,...  18 us
    pallas_call x2, Pallas kernels, forward(): pl.pallas_call(functools.partial(forward_kernel, len(feats), first, colum...  11.7 us
    pallas_call x1, Pallas kernels, dinput(): pl.pallas_call(functools.partial(dinput_kernel, len(deltas), fold, groups...  8.03 us
    unnamed x11, local copies, waits for them, and re-layouts  5.76 us
  transfers between devices with their start and end apart: 27, of which 9 were waited for; matrix products, arithmetic and copies ran while one was open for 2% of the time, Pallas kernels for 31%

profile of v5, /device:TPU:0, one launch (start us, length us, event | category | flops | bytes accessed | tf_op | source)
XLA Modules:
  0.0 127.0 jit_solution(4149300107066729385)
XLA Ops:
  0.6 3.0 %collective-permute-start.1 = (bf16[256,1024]{1,0:T(8,128)(2,1)}, bf16[256,1024]{1,0:T(8,128)(2,1)S(1)}, u32[]{:S(2)}, u32[]{:S(2)}) collective-permute-start(bf16[256,1024]{1,0:T(8,128)(2,1)} %refs_1_.13), channel_id=1, source_target_pairs={{0,2},{1,3},{2,0},{3,1},{4,6},{5,7},{6,4},{7,5},{8,10},{9,11},{10,... | collective-permute-start | bytes 1572872 | tf_op jit(solution)/shard_map/ppermute | solution.py:446
  3.6 1.5 %collective-permute-start.3 = (bf16[256,1024]{1,0:T(8,128)(2,1)}, bf16[256,1024]{1,0:T(8,128)(2,1)S(1)}, u32[]{:S(2)}, u32[]{:S(2)}) collective-permute-start(bf16[256,1024]{1,0:T(8,128)(2,1)} %refs_1_.13), channel_id=1, source_target_pairs={{0,4},{4,0},{8,12},{12,8},{16,20},{20,16},{24,28},{28,24},{1,5},{5... | collective-permute-start | bytes 1572872 | tf_op jit(solution)/shard_map/ppermute | solution.py:446
  6.0 1.6 %copy-done.2 = bf16[256,4096]{1,0:T(8,128)(2,1)S(1)} copy-done((bf16[256,4096]{1,0:T(8,128)(2,1)S(1)}, bf16[256,4096]{1,0:T(8,128)(2,1)}, u32[]{:S(2)}) %copy-start.2) | copy-done | bytes 2097176
  7.7 8.1 %collective-permute-done.1.refs_0_ = bf16[256,1024]{1,0:T(8,128)(2,1)S(1)} collective-permute-done((bf16[256,1024]{1,0:T(8,128)(2,1)}, bf16[256,1024]{1,0:T(8,128)(2,1)S(1)}, u32[]{:S(2)}, u32[]{:S(2)}) %collective-permute-start.1) | collective-permute-done | bytes 524320 | tf_op jit(solution)/shard_map/ppermute | solution.py:446
  15.8 1.8 %collective-permute-start.6 = (bf16[256,1024]{1,0:T(8,128)(2,1)S(1)}, bf16[256,1024]{1,0:T(8,128)(2,1)S(1)}, u32[]{:S(2)}, u32[]{:S(2)}) collective-permute-start(bf16[256,1024]{1,0:T(8,128)(2,1)S(1)} %cut.1.refs_1_), channel_id=1, source_target_pairs={{0,4},{4,0},{8,12},{12,8},{16,20},{20,16},{24,28},{28,24},{1,5},{5... | collective-permute-start | bytes 1572872 | tf_op jit(solution)/shard_map/ppermute | solution.py:446
  17.5 1.5 %collective-permute-start.5 = (bf16[256,1024]{1,0:T(8,128)(2,1)S(1)}, bf16[256,1024]{1,0:T(8,128)(2,1)S(1)}, u32[]{:S(2)}, u32[]{:S(2)}) collective-permute-start(bf16[256,1024]{1,0:T(8,128)(2,1)S(1)} %collective-permute-done.3.refs_5_), channel_id=1, source_target_pairs={{0,2},{1,3},{2,0},{3,1},{4,6},{5,7},{6,4},{7,5},{8,10},{9,11},{10,... | collective-permute-start | bytes 1572872 | tf_op jit(solution)/shard_map/ppermute | solution.py:446
  19.1 3.4 %copy-done = bf16[32,1024,128]{2,1,0:T(8,128)(2,1)S(1)} copy-done((bf16[32,1024,128]{2,1,0:T(8,128)(2,1)S(1)}, bf16[32,1024,128]{2,1,0:T(8,128)(2,1)}, u32[]{:S(2)}) %copy-start) | copy-done | bytes 8388632
  22.4 6.0 %forward.2 = (bf16[256,4096]{1,0:T(8,128)(2,1)}, bf16[256,2048]{1,0:T(8,128)(2,1)S(1)}, bf16[256,1024]{1,0:T(8,128)(2,1)S(1)}, bf16[256,2048]{1,0:T(8,128)(2,1)S(1)}) custom-call(s32[1024]{0:T(1024)S(1)} %reshape.15.refs_2_.refs_0_, bf16[256,1024]{1,0:T(8,128)(2,1)S(1)} %copy-done.4, bf16[256,1024]{1,0:T(8,128)(2,1)S(1)} %collective-permute-done.refs_2_, ...), custom_call_target="tpu_custom_call" | custom-call | tf_op jit(solution)/shard_map/forward/pallas_call | solution.py:153
  28.5 1.7 %collective-permute-done.6.refs_2_.refs_11_ = bf16[256,1024]{1,0:T(8,128)(2,1)S(1)} collective-permute-done((bf16[256,1024]{1,0:T(8,128)(2,1)S(1)}, bf16[256,1024]{1,0:T(8,128)(2,1)S(1)}, u32[]{:S(2)}, u32[]{:S(2)}) %collective-permute-start.6) | collective-permute-done | bytes 524320 | tf_op jit(solution)/shard_map/ppermute | solution.py:446
  30.1 1.5 %collective-permute-done.5.refs_0_ = bf16[256,1024]{1,0:T(8,128)(2,1)S(1)} collective-permute-done((bf16[256,1024]{1,0:T(8,128)(2,1)S(1)}, bf16[256,1024]{1,0:T(8,128)(2,1)S(1)}, u32[]{:S(2)}, u32[]{:S(2)}) %collective-permute-start.5) | collective-permute-done | bytes 524320 | tf_op jit(solution)/shard_map/ppermute | solution.py:446
  31.9 1.7 %collective-permute-start.11 = (bf16[256,2048]{1,0:T(8,128)(2,1)S(1)}, bf16[256,2048]{1,0:T(8,128)(2,1)S(1)}, u32[]{:S(2)}, u32[]{:S(2)}) collective-permute-start(bf16[256,2048]{1,0:T(8,128)(2,1)S(1)} %get-tuple-element.39), channel_id=1, source_target_pairs={{0,4},{4,0},{8,12},{12,8},{16,20},{20,16},{24,28},{28,24},{1,5},{5... | collective-permute-start | bytes 3145736 | tf_op jit(solution)/shard_map/ppermute | solution.py:446
  33.6 4.2 %grads.5 = (bf16[8,128,128]{2,1,0:T(8,128)(2,1)S(1)}, bf16[3,8,128,128]{3,2,1,0:T(8,128)(2,1)S(1)}) custom-call(s32[1024]{0:T(1024)S(1)} %reshape.15.refs_2_.refs_0_, bf16[256,1024]{1,0:T(8,128)(2,1)S(1)} %copy-done.4, bf16[256,1024]{1,0:T(8,128)(2,1)S(1)} %collective-permute-done.refs_2_, bf16[256,1024]{1,0:T(8,128)(2,1)S(1)} %gate.2.refs_3_, ...), custom_call_target="tpu_custom_call" | custom-call | tf_op jit(solution)/shard_map/grads/pallas_call | solution.py:231
  37.8 3.5 %collective-permute-start.13 = (bf16[3,8,128,128]{3,2,1,0:T(8,128)(2,1)S(1)}, bf16[3,8,128,128]{3,2,1,0:T(8,128)(2,1)S(1)}, u32[]{:S(2)}, u32[]{:S(2)}) collective-permute-start(bf16[3,8,128,128]{3,2,1,0:T(8,128)(2,1)S(1)} %get-tuple-element.41.refs_0_.refs_2_), channel_id=1, source_target_pairs={{0,8},{4,12},{24,16},{28,20},{1,9},{5,13},{25,17},{29,21},{2,10},{... | collective-permute-start | bytes 2359304 | tf_op jit(solution)/shard_map/ppermute | solution.py:446
  41.4 5.7 %forward.3 = (bf16[256,4096]{1,0:T(8,128)(2,1)}, bf16[256,2048]{1,0:T(8,128)(2,1)S(1)}) custom-call(s32[1024]{0:T(1024)S(1)} %reshape.15.refs_2_.refs_0_, bf16[256,1024]{1,0:T(8,128)(2,1)S(1)} %copy-done.4, bf16[256,1024]{1,0:T(8,128)(2,1)S(1)} %collective-permute-done.refs_2_, bf16[256,1024]{1,0:T(8,128)(2,1)S(1)} %gate.2.refs_3_, ...), custom_call_target="tpu_custom_call", output_to_operand_aliasing={{0}: (8, {})} | custom-call | tf_op jit(solution)/shard_map/forward/pallas_call | solution.py:153
  47.1 4.1 %grads.6 = (bf16[8,128,128]{2,1,0:T(8,128)(2,1)S(1)}, bf16[3,8,128,128]{3,2,1,0:T(8,128)(2,1)S(1)}) custom-call(s32[1024]{0:T(1024)S(1)} %reshape.15.refs_2_.refs_0_, bf16[256,1024]{1,0:T(8,128)(2,1)S(1)} %copy-done.4, bf16[256,1024]{1,0:T(8,128)(2,1)S(1)} %collective-permute-done.refs_2_, bf16[256,1024]{1,0:T(8,128)(2,1)S(1)} %gate.2.refs_3_, ...), custom_call_target="tpu_custom_call" | custom-call | tf_op jit(solution)/shard_map/grads/pallas_call | solution.py:231
  51.3 2.7 %collective-permute-start.12 = (bf16[3,8,128,128]{3,2,1,0:T(8,128)(2,1)S(1)}, bf16[3,8,128,128]{3,2,1,0:T(8,128)(2,1)S(1)}, u32[]{:S(2)}, u32[]{:S(2)}) collective-permute-start(bf16[3,8,128,128]{3,2,1,0:T(8,128)(2,1)S(1)} %get-tuple-element.40.refs_0_.refs_4_), channel_id=1, source_target_pairs={{0,8},{4,12},{24,16},{28,20},{1,9},{5,13},{25,17},{29,21},{2,10},{... | collective-permute-start | bytes 2359304 | tf_op jit(solution)/shard_map/ppermute | solution.py:446
  54.0 8.0 %dinput.1 = (bf16[2,256,1024]{2,1,0:T(8,128)(2,1)S(1)}, bf16[1,256,1024]{2,1,0:T(8,128)(2,1)S(1)}, bf16[1,256,1024]{2,1,0:T(8,128)(2,1)S(1)}) custom-call(s32[1024]{0:T(1024)S(1)} %reshape.15.refs_2_.refs_0_, bf16[256,2048]{1,0:T(8,128)(2,1)S(1)} %get-tuple-element.30.refs_1_.refs_10_, bf16[256,2048]{1,0:T(8,128)(2,1)S(1)} %get-tuple-element.33.refs_12_.refs_2_.refs_10_, ...), custom_call_target="tpu_custom_call" | custom-call | tf_op jit(solution)/shard_map/dinput/pallas_call | solution.py:290
  63.4 5.0 %collective-permute-done.11.refs_11_ = bf16[256,2048]{1,0:T(8,128)(2,1)S(1)} collective-permute-done((bf16[256,2048]{1,0:T(8,128)(2,1)S(1)}, bf16[256,2048]{1,0:T(8,128)(2,1)S(1)}, u32[]{:S(2)}, u32[]{:S(2)}) %collective-permute-start.11) | collective-permute-done | bytes 1048608 | tf_op jit(solution)/shard_map/ppermute | solution.py:446
  68.4 3.7 %grads.7 = (bf16[6,128,128]{2,1,0:T(8,128)(2,1)S(1)}, bf16[3,6,128,128]{3,2,1,0:T(8,128)(2,1)S(1)}) custom-call(s32[1024]{0:T(1024)S(1)} %reshape.15.refs_2_.refs_0_, bf16[256,1024]{1,0:T(8,128)(2,1)S(1)} %copy-done.4, bf16[256,1024]{1,0:T(8,128)(2,1)S(1)} %collective-permute-done.refs_2_, bf16[256,1024]{1,0:T(8,128)(2,1)S(1)} %gate.2.refs_3_, ...), custom_call_target="tpu_custom_call" | custom-call | tf_op jit(solution)/shard_map/grads/pallas_call | solution.py:231
  72.1 3.5 %collective-permute-start.16 = (bf16[3,6,128,128]{3,2,1,0:T(8,128)(2,1)S(1)}, bf16[3,6,128,128]{3,2,1,0:T(8,128)(2,1)S(1)}, u32[]{:S(2)}, u32[]{:S(2)}) collective-permute-start(bf16[3,6,128,128]{3,2,1,0:T(8,128)(2,1)S(1)} %get-tuple-element.44.refs_0_.refs_4_), channel_id=1, source_target_pairs={{0,8},{4,12},{24,16},{28,20},{1,9},{5,13},{25,17},{29,21},{2,10},{... | collective-permute-start | bytes 1769480 | tf_op jit(solution)/shard_map/ppermute | solution.py:446
  76.5 3.7 %grads.8 = (bf16[6,128,128]{2,1,0:T(8,128)(2,1)S(1)}, bf16[3,6,128,128]{3,2,1,0:T(8,128)(2,1)S(1)}) custom-call(s32[1024]{0:T(1024)S(1)} %reshape.15.refs_2_.refs_0_, bf16[256,1024]{1,0:T(8,128)(2,1)S(1)} %copy-done.4, bf16[256,1024]{1,0:T(8,128)(2,1)S(1)} %collective-permute-done.refs_2_, bf16[256,1024]{1,0:T(8,128)(2,1)S(1)} %gate.2.refs_3_, ...), custom_call_target="tpu_custom_call" | custom-call | tf_op jit(solution)/shard_map/grads/pallas_call | solution.py:231
  80.2 6.8 %collective-permute-start.19 = (bf16[3,6,128,128]{3,2,1,0:T(8,128)(2,1)S(1)}, bf16[3,6,128,128]{3,2,1,0:T(8,128)(2,1)S(1)}, u32[]{:S(2)}, u32[]{:S(2)}) collective-permute-start(bf16[3,6,128,128]{3,2,1,0:T(8,128)(2,1)S(1)} %get-tuple-element.46.refs_0_.refs_2_.refs_6_), channel_id=1, source_target_pairs={{0,8},{4,12},{24,16},{28,20},{1,9},{5,13},{25,17},{29,21},{2,10},{... | collective-permute-start | bytes 1769480 | tf_op jit(solution)/shard_map/ppermute | solution.py:446
  87.2 1.5 %collective-permute-start.15 = (bf16[1,256,1024]{2,1,0:T(8,128)(2,1)S(1)}, bf16[1,256,1024]{2,1,0:T(8,128)(2,1)S(1)}, u32[]{:S(2)}, u32[]{:S(2)}) collective-permute-start(bf16[1,256,1024]{2,1,0:T(8,128)(2,1)S(1)} %relay.8.refs_6_), channel_id=1, source_target_pairs={{0,2},{1,3},{2,0},{3,1},{4,6},{5,7},{6,4},{7,5},{8,10},{9,11},{10,... | collective-permute-start | bytes 1572872 | tf_op jit(solution)/shard_map/ppermute | solution.py:446
  90.2 1.3 %collective-permute-start.24 = (bf16[1,16,128,128]{3,2,1,0:T(8,128)(2,1)S(1)}, bf16[1,16,128,128]{3,2,1,0:T(8,128)(2,1)S(1)}, u32[]{:S(2)}, u32[]{:S(2)}) collective-permute-start(bf16[1,16,128,128]{3,2,1,0:T(8,128)(2,1)S(1)} %get-tuple-element.52), channel_id=1, source_target_pairs={{8,0},{12,4},{16,24},{20,28},{9,1},{13,5},{17,25},{21,29},{10,2},{... | collective-permute-start | bytes 1572872 | tf_op jit(solution)/shard_map/ppermute | solution.py:446
  91.5 2.3 %grads.9 = (bf16[4,128,128]{2,1,0:T(8,128)(2,1)S(1)}, bf16[3,4,128,128]{3,2,1,0:T(8,128)(2,1)S(1)}) custom-call(s32[1024]{0:T(1024)S(1)} %reshape.15.refs_2_.refs_0_, bf16[256,1024]{1,0:T(8,128)(2,1)S(1)} %copy-done.4, bf16[256,1024]{1,0:T(8,128)(2,1)S(1)} %collective-permute-done.refs_2_, bf16[256,1024]{1,0:T(8,128)(2,1)S(1)} %gate.2.refs_3_, ...), custom_call_target="tpu_custom_call" | custom-call | tf_op jit(solution)/shard_map/grads/pallas_call | solution.py:231
  93.8 8.0 %collective-permute-start.23 = (bf16[3,4,128,128]{3,2,1,0:T(8,128)(2,1)S(1)}, bf16[3,4,128,128]{3,2,1,0:T(8,128)(2,1)S(1)}, u32[]{:S(2)}, u32[]{:S(2)}) collective-permute-start(bf16[3,4,128,128]{3,2,1,0:T(8,128)(2,1)S(1)} %get-tuple-element.47.refs_7_.refs_0_.refs_2_), channel_id=1, source_target_pairs={{0,8},{4,12},{24,16},{28,20},{1,9},{5,13},{25,17},{29,21},{2,10},{... | collective-permute-start | bytes 1179656 | tf_op jit(solution)/shard_map/ppermute | solution.py:446
  102.0 1.3 %collective-permute-start.20 = (bf16[1,16,128,128]{3,2,1,0:T(8,128)(2,1)S(1)}, bf16[1,16,128,128]{3,2,1,0:T(8,128)(2,1)S(1)}, u32[]{:S(2)}, u32[]{:S(2)}) collective-permute-start(bf16[1,16,128,128]{3,2,1,0:T(8,128)(2,1)S(1)} %get-tuple-element.49), channel_id=1, source_target_pairs={{8,0},{12,4},{16,24},{20,28},{9,1},{13,5},{17,25},{21,29},{10,2},{... | collective-permute-start | bytes 1572872 | tf_op jit(solution)/shard_map/ppermute | solution.py:446
  104.0 1.3 %collective-permute-start.22 = (bf16[1,6,128,128]{3,2,1,0:T(8,128)(2,1)S(1)}, bf16[1,6,128,128]{3,2,1,0:T(8,128)(2,1)S(1)}, u32[]{:S(2)}, u32[]{:S(2)}) collective-permute-start(bf16[1,6,128,128]{3,2,1,0:T(8,128)(2,1)S(1)} %get-tuple-element.51), channel_id=1, source_target_pairs={{8,24},{12,28},{16,0},{20,4},{9,25},{13,29},{17,1},{21,5},{10,26},... | collective-permute-start | bytes 589832 | tf_op jit(solution)/shard_map/ppermute | solution.py:446
  105.3 3.8 %collective-permute-done.23.refs_1_.refs_3_.refs_10_ = bf16[3,4,128,128]{3,2,1,0:T(8,128)(2,1)S(1)} collective-permute-done((bf16[3,4,128,128]{3,2,1,0:T(8,128)(2,1)S(1)}, bf16[3,4,128,128]{3,2,1,0:T(8,128)(2,1)S(1)}, u32[]{:S(2)}, u32[]{:S(2)}) %collective-permute-start.23) | collective-permute-done | bytes 393248 | tf_op jit(solution)/shard_map/ppermute | solution.py:446
  109.1 3.3 %collective-permute-done.24.refs_5_.refs_3_.refs_7_ = bf16[1,16,128,128]{3,2,1,0:T(8,128)(2,1)S(1)} collective-permute-done((bf16[1,16,128,128]{3,2,1,0:T(8,128)(2,1)S(1)}, bf16[1,16,128,128]{3,2,1,0:T(8,128)(2,1)S(1)}, u32[]{:S(2)}, u32[]{:S(2)}) %collective-permute-start.24) | collective-permute-done | bytes 524320 | tf_op jit(solution)/shard_map/ppermute | solution.py:446
  116.8 4.8 %collective-permute-done.26.refs_12_ = bf16[1,4,128,128]{3,2,1,0:T(8,128)(2,1)S(1)} collective-permute-done((bf16[1,4,128,128]{3,2,1,0:T(8,128)(2,1)S(1)}, bf16[1,4,128,128]{3,2,1,0:T(8,128)(2,1)S(1)}, u32[]{:S(2)}, u32[]{:S(2)}) %collective-permute-start.26) | collective-permute-done | bytes 131104 | tf_op jit(solution)/shard_map/ppermute | solution.py:446
  121.6 4.2 %collective-permute-done.20.refs_3_.refs_8_.refs_13_ = bf16[1,16,128,128]{3,2,1,0:T(8,128)(2,1)S(1)} collective-permute-done((bf16[1,16,128,128]{3,2,1,0:T(8,128)(2,1)S(1)}, bf16[1,16,128,128]{3,2,1,0:T(8,128)(2,1)S(1)}, u32[]{:S(2)}, u32[]{:S(2)}) %collective-permute-start.20) | collective-permute-done | bytes 524320 | tf_op jit(solution)/shard_map/ppermute | solution.py:446
  (54 shorter events, 11.5 us)
Async XLA Ops:
  0.6 15.1 %collective-permute-start.1 = (bf16[256,1024]{1,0:T(8,128)(2,1)}, bf16[256,1024]{1,0:T(8,128)(2,1)S(1)}, u32[]{:S(2)}, u32[]{:S(2)}) collective-permute-start(bf16[256,1024]{1,0:T(8,128)(2,1)} %refs_1_.13), channel_id=1, source_target_pairs={{0,2},{1,3},{2,0},{3,1},{4,6},{5,7},{6,4},{7,5},{8,10},{9,11},{10,... | collective-permute-start | bytes 1572872 | tf_op jit(solution)/shard_map/ppermute | solution.py:446
  3.6 13.9 %collective-permute-start.3 = (bf16[256,1024]{1,0:T(8,128)(2,1)}, bf16[256,1024]{1,0:T(8,128)(2,1)S(1)}, u32[]{:S(2)}, u32[]{:S(2)}) collective-permute-start(bf16[256,1024]{1,0:T(8,128)(2,1)} %refs_1_.13), channel_id=1, source_target_pairs={{0,4},{4,0},{8,12},{12,8},{16,20},{20,16},{24,28},{28,24},{1,5},{5... | collective-permute-start | bytes 1572872 | tf_op jit(solution)/shard_map/ppermute | solution.py:446
  5.2 13.9 %collective-permute-start = (bf16[256,1024]{1,0:T(8,128)(2,1)}, bf16[256,1024]{1,0:T(8,128)(2,1)S(1)}, u32[]{:S(2)}, u32[]{:S(2)}) collective-permute-start(bf16[256,1024]{1,0:T(8,128)(2,1)} %refs_1_.13), channel_id=1, source_target_pairs={{0,1},{1,0},{2,3},{3,2},{4,5},{5,4},{6,7},{7,6},{8,9},{9,8},{10,11... | collective-permute-start | bytes 1572872 | tf_op jit(solution)/shard_map/ppermute | solution.py:446
  6.0 1.6 %copy-start.2 = (bf16[256,4096]{1,0:T(8,128)(2,1)S(1)}, bf16[256,4096]{1,0:T(8,128)(2,1)}, u32[]{:S(2)}) copy-start(bf16[256,4096]{1,0:T(8,128)(2,1)} %refs_7_.3) | copy-start | bytes 6291460
  7.6 11.4 %copy-start.4 = (bf16[256,1024]{1,0:T(8,128)(2,1)S(1)}, bf16[256,1024]{1,0:T(8,128)(2,1)}, u32[]{:S(2)}) copy-start(bf16[256,1024]{1,0:T(8,128)(2,1)} %refs_1_.13) | copy-start | bytes 1572868
  15.8 3.3 %collective-permute-start.2 = (bf16[256,1024]{1,0:T(8,128)(2,1)S(1)}, bf16[256,1024]{1,0:T(8,128)(2,1)S(1)}, u32[]{:S(2)}, u32[]{:S(2)}) collective-permute-start(bf16[256,1024]{1,0:T(8,128)(2,1)S(1)} %gate.2.refs_3_), channel_id=1, source_target_pairs={{0,1},{1,0},{2,3},{3,2},{4,5},{5,4},{6,7},{7,6},{8,9},{9,8},{10,11... | collective-permute-start | bytes 1572872 | tf_op jit(solution)/shard_map/ppermute | solution.py:446
  15.8 14.4 %collective-permute-start.6 = (bf16[256,1024]{1,0:T(8,128)(2,1)S(1)}, bf16[256,1024]{1,0:T(8,128)(2,1)S(1)}, u32[]{:S(2)}, u32[]{:S(2)}) collective-permute-start(bf16[256,1024]{1,0:T(8,128)(2,1)S(1)} %cut.1.refs_1_), channel_id=1, source_target_pairs={{0,4},{4,0},{8,12},{12,8},{16,20},{20,16},{24,28},{28,24},{1,5},{5... | collective-permute-start | bytes 1572872 | tf_op jit(solution)/shard_map/ppermute | solution.py:446
  17.5 14.1 %collective-permute-start.5 = (bf16[256,1024]{1,0:T(8,128)(2,1)S(1)}, bf16[256,1024]{1,0:T(8,128)(2,1)S(1)}, u32[]{:S(2)}, u32[]{:S(2)}) collective-permute-start(bf16[256,1024]{1,0:T(8,128)(2,1)S(1)} %collective-permute-done.3.refs_5_), channel_id=1, source_target_pairs={{0,2},{1,3},{2,0},{3,1},{4,6},{5,7},{6,4},{7,5},{8,10},{9,11},{10,... | collective-permute-start | bytes 1572872 | tf_op jit(solution)/shard_map/ppermute | solution.py:446
  19.0 14.6 %collective-permute-start.4 = (bf16[256,1024]{1,0:T(8,128)(2,1)S(1)}, bf16[256,1024]{1,0:T(8,128)(2,1)S(1)}, u32[]{:S(2)}, u32[]{:S(2)}) collective-permute-start(bf16[256,1024]{1,0:T(8,128)(2,1)S(1)} %collective-permute-done.3.refs_5_), channel_id=1, source_target_pairs={{0,1},{1,0},{2,3},{3,2},{4,5},{5,4},{6,7},{7,6},{8,9},{9,8},{10,11... | collective-permute-start | bytes 1572872 | tf_op jit(solution)/shard_map/ppermute | solution.py:446
  19.1 3.4 %copy-start = (bf16[32,1024,128]{2,1,0:T(8,128)(2,1)S(1)}, bf16[32,1024,128]{2,1,0:T(8,128)(2,1)}, u32[]{:S(2)}) copy-start(bf16[32,1024,128]{2,1,0:T(8,128)(2,1)} %refs_9_.9) | copy-start | bytes 25165828
  22.4 11.2 %copy-start.1 = (bf16[32,1024,128]{2,1,0:T(8,128)(2,1)S(1)}, bf16[32,1024,128]{2,1,0:T(8,128)(2,1)}, u32[]{:S(2)}) copy-start(bf16[32,1024,128]{2,1,0:T(8,128)(2,1)} %refs_9_.9) | copy-start | bytes 25165828
  31.6 2.0 %collective-permute-start.7 = (bf16[256,1024]{1,0:T(8,128)(2,1)S(1)}, bf16[256,1024]{1,0:T(8,128)(2,1)S(1)}, u32[]{:S(2)}, u32[]{:S(2)}) collective-permute-start(bf16[256,1024]{1,0:T(8,128)(2,1)S(1)} %gate.3.refs_7_), channel_id=1, source_target_pairs={{0,1},{1,0},{2,3},{3,2},{4,5},{5,4},{6,7},{7,6},{8,9},{9,8},{10,11... | collective-permute-start | bytes 1572872 | tf_op jit(solution)/shard_map/ppermute | solution.py:446
  31.6 15.5 %collective-permute-start.8 = (bf16[256,1024]{1,0:T(8,128)(2,1)S(1)}, bf16[256,1024]{1,0:T(8,128)(2,1)S(1)}, u32[]{:S(2)}, u32[]{:S(2)}) collective-permute-start(bf16[256,1024]{1,0:T(8,128)(2,1)S(1)} %get-tuple-element.34), channel_id=1, source_target_pairs={{0,4},{4,0},{8,12},{12,8},{16,20},{20,16},{24,28},{28,24},{1,5},{5... | collective-permute-start | bytes 1572872 | tf_op jit(solution)/shard_map/ppermute | solution.py:446
  31.9 9.4 %copy-start.3 = (bf16[256,4096]{1,0:T(8,128)(2,1)S(1)}, bf16[256,4096]{1,0:T(8,128)(2,1)}, u32[]{:S(2)}) copy-start(bf16[256,4096]{1,0:T(8,128)(2,1)} %refs_7_.3) | copy-start | bytes 6291460
  31.9 36.5 %collective-permute-start.11 = (bf16[256,2048]{1,0:T(8,128)(2,1)S(1)}, bf16[256,2048]{1,0:T(8,128)(2,1)S(1)}, u32[]{:S(2)}, u32[]{:S(2)}) collective-permute-start(bf16[256,2048]{1,0:T(8,128)(2,1)S(1)} %get-tuple-element.39), channel_id=1, source_target_pairs={{0,4},{4,0},{8,12},{12,8},{16,20},{20,16},{24,28},{28,24},{1,5},{5... | collective-permute-start | bytes 3145736 | tf_op jit(solution)/shard_map/ppermute | solution.py:446
  37.8 24.2 %collective-permute-start.13 = (bf16[3,8,128,128]{3,2,1,0:T(8,128)(2,1)S(1)}, bf16[3,8,128,128]{3,2,1,0:T(8,128)(2,1)S(1)}, u32[]{:S(2)}, u32[]{:S(2)}) collective-permute-start(bf16[3,8,128,128]{3,2,1,0:T(8,128)(2,1)S(1)} %get-tuple-element.41.refs_0_.refs_2_), channel_id=1, source_target_pairs={{0,8},{4,12},{24,16},{28,20},{1,9},{5,13},{25,17},{29,21},{2,10},{... | collective-permute-start | bytes 2359304 | tf_op jit(solution)/shard_map/ppermute | solution.py:446
  51.3 24.3 %collective-permute-start.12 = (bf16[3,8,128,128]{3,2,1,0:T(8,128)(2,1)S(1)}, bf16[3,8,128,128]{3,2,1,0:T(8,128)(2,1)S(1)}, u32[]{:S(2)}, u32[]{:S(2)}) collective-permute-start(bf16[3,8,128,128]{3,2,1,0:T(8,128)(2,1)S(1)} %get-tuple-element.40.refs_0_.refs_4_), channel_id=1, source_target_pairs={{0,8},{4,12},{24,16},{28,20},{1,9},{5,13},{25,17},{29,21},{2,10},{... | collective-permute-start | bytes 2359304 | tf_op jit(solution)/shard_map/ppermute | solution.py:446
  62.2 14.3 %collective-permute-start.14 = (bf16[2,8,128,128]{3,2,1,0:T(8,128)(2,1)S(1)}, bf16[2,8,128,128]{3,2,1,0:T(8,128)(2,1)S(1)}, u32[]{:S(2)}, u32[]{:S(2)}) collective-permute-start(bf16[2,8,128,128]{3,2,1,0:T(8,128)(2,1)S(1)} %relay.6.refs_12_), channel_id=1, source_target_pairs={{8,16},{12,20},{16,8},{20,12},{9,17},{13,21},{17,9},{21,13},{10,18... | collective-permute-start | bytes 1572872 | tf_op jit(solution)/shard_map/ppermute | solution.py:446
  62.9 24.2 %collective-permute-start.10 = (bf16[1,256,1024]{2,1,0:T(8,128)(2,1)S(1)}, bf16[1,256,1024]{2,1,0:T(8,128)(2,1)S(1)}, u32[]{:S(2)}, u32[]{:S(2)}) collective-permute-start(bf16[1,256,1024]{2,1,0:T(8,128)(2,1)S(1)} %get-tuple-element.38), channel_id=1, source_target_pairs={{0,1},{1,0},{2,3},{3,2},{4,5},{5,4},{6,7},{7,6},{8,9},{9,8},{10,11... | collective-permute-start | bytes 1572872 | tf_op jit(solution)/shard_map/ppermute | solution.py:446
  62.9 24.1 %collective-permute-start.9 = (bf16[1,256,1024]{2,1,0:T(8,128)(2,1)S(1)}, bf16[1,256,1024]{2,1,0:T(8,128)(2,1)S(1)}, u32[]{:S(2)}, u32[]{:S(2)}) collective-permute-start(bf16[1,256,1024]{2,1,0:T(8,128)(2,1)S(1)} %get-tuple-element.37), channel_id=1, source_target_pairs={{0,1},{1,0},{2,3},{3,2},{4,5},{5,4},{6,7},{7,6},{8,9},{9,8},{10,11... | collective-permute-start | bytes 1572872 | tf_op jit(solution)/shard_map/ppermute | solution.py:446
  72.1 17.2 %collective-permute-start.16 = (bf16[3,6,128,128]{3,2,1,0:T(8,128)(2,1)S(1)}, bf16[3,6,128,128]{3,2,1,0:T(8,128)(2,1)S(1)}, u32[]{:S(2)}, u32[]{:S(2)}) collective-permute-start(bf16[3,6,128,128]{3,2,1,0:T(8,128)(2,1)S(1)} %get-tuple-element.44.refs_0_.refs_4_), channel_id=1, source_target_pairs={{0,8},{4,12},{24,16},{28,20},{1,9},{5,13},{25,17},{29,21},{2,10},{... | collective-permute-start | bytes 1769480 | tf_op jit(solution)/shard_map/ppermute | solution.py:446
  75.8 13.0 %collective-permute-start.17 = (bf16[2,8,128,128]{3,2,1,0:T(8,128)(2,1)S(1)}, bf16[2,8,128,128]{3,2,1,0:T(8,128)(2,1)S(1)}, u32[]{:S(2)}, u32[]{:S(2)}) collective-permute-start(bf16[2,8,128,128]{3,2,1,0:T(8,128)(2,1)S(1)} %relay.7.refs_12_), channel_id=1, source_target_pairs={{8,16},{12,20},{16,8},{20,12},{9,17},{13,21},{17,9},{21,13},{10,18... | collective-permute-start | bytes 1572872 | tf_op jit(solution)/shard_map/ppermute | solution.py:446
  80.2 21.7 %collective-permute-start.19 = (bf16[3,6,128,128]{3,2,1,0:T(8,128)(2,1)S(1)}, bf16[3,6,128,128]{3,2,1,0:T(8,128)(2,1)S(1)}, u32[]{:S(2)}, u32[]{:S(2)}) collective-permute-start(bf16[3,6,128,128]{3,2,1,0:T(8,128)(2,1)S(1)} %get-tuple-element.46.refs_0_.refs_2_.refs_6_), channel_id=1, source_target_pairs={{0,8},{4,12},{24,16},{28,20},{1,9},{5,13},{25,17},{29,21},{2,10},{... | collective-permute-start | bytes 1769480 | tf_op jit(solution)/shard_map/ppermute | solution.py:446
  87.2 14.7 %collective-permute-start.15 = (bf16[1,256,1024]{2,1,0:T(8,128)(2,1)S(1)}, bf16[1,256,1024]{2,1,0:T(8,128)(2,1)S(1)}, u32[]{:S(2)}, u32[]{:S(2)}) collective-permute-start(bf16[1,256,1024]{2,1,0:T(8,128)(2,1)S(1)} %relay.8.refs_6_), channel_id=1, source_target_pairs={{0,2},{1,3},{2,0},{3,1},{4,6},{5,7},{6,4},{7,5},{8,10},{9,11},{10,... | collective-permute-start | bytes 1572872 | tf_op jit(solution)/shard_map/ppermute | solution.py:446
  89.5 12.3 %collective-permute-start.18 = (bf16[2,6,128,128]{3,2,1,0:T(8,128)(2,1)S(1)}, bf16[2,6,128,128]{3,2,1,0:T(8,128)(2,1)S(1)}, u32[]{:S(2)}, u32[]{:S(2)}) collective-permute-start(bf16[2,6,128,128]{3,2,1,0:T(8,128)(2,1)S(1)} %get-tuple-element.45.refs_12_), channel_id=1, source_target_pairs={{8,16},{12,20},{16,8},{20,12},{9,17},{13,21},{17,9},{21,13},{10,18... | collective-permute-start | bytes 1179656 | tf_op jit(solution)/shard_map/ppermute | solution.py:446
  90.2 22.2 %collective-permute-start.24 = (bf16[1,16,128,128]{3,2,1,0:T(8,128)(2,1)S(1)}, bf16[1,16,128,128]{3,2,1,0:T(8,128)(2,1)S(1)}, u32[]{:S(2)}, u32[]{:S(2)}) collective-permute-start(bf16[1,16,128,128]{3,2,1,0:T(8,128)(2,1)S(1)} %get-tuple-element.52), channel_id=1, source_target_pairs={{8,0},{12,4},{16,24},{20,28},{9,1},{13,5},{17,25},{21,29},{10,2},{... | collective-permute-start | bytes 1572872 | tf_op jit(solution)/shard_map/ppermute | solution.py:446
  93.8 15.3 %collective-permute-start.23 = (bf16[3,4,128,128]{3,2,1,0:T(8,128)(2,1)S(1)}, bf16[3,4,128,128]{3,2,1,0:T(8,128)(2,1)S(1)}, u32[]{:S(2)}, u32[]{:S(2)}) collective-permute-start(bf16[3,4,128,128]{3,2,1,0:T(8,128)(2,1)S(1)} %get-tuple-element.47.refs_7_.refs_0_.refs_2_), channel_id=1, source_target_pairs={{0,8},{4,12},{24,16},{28,20},{1,9},{5,13},{25,17},{29,21},{2,10},{... | collective-permute-start | bytes 1179656 | tf_op jit(solution)/shard_map/ppermute | solution.py:446
  102.0 23.8 %collective-permute-start.20 = (bf16[1,16,128,128]{3,2,1,0:T(8,128)(2,1)S(1)}, bf16[1,16,128,128]{3,2,1,0:T(8,128)(2,1)S(1)}, u32[]{:S(2)}, u32[]{:S(2)}) collective-permute-start(bf16[1,16,128,128]{3,2,1,0:T(8,128)(2,1)S(1)} %get-tuple-element.49), channel_id=1, source_target_pairs={{8,0},{12,4},{16,24},{20,28},{9,1},{13,5},{17,25},{21,29},{10,2},{... | collective-permute-start | bytes 1572872 | tf_op jit(solution)/shard_map/ppermute | solution.py:446
  103.3 18.3 %collective-permute-start.21 = (bf16[1,6,128,128]{3,2,1,0:T(8,128)(2,1)S(1)}, bf16[1,6,128,128]{3,2,1,0:T(8,128)(2,1)S(1)}, u32[]{:S(2)}, u32[]{:S(2)}) collective-permute-start(bf16[1,6,128,128]{3,2,1,0:T(8,128)(2,1)S(1)} %get-tuple-element.50.refs_4_), channel_id=1, source_target_pairs={{8,16},{12,20},{16,8},{20,12},{9,17},{13,21},{17,9},{21,13},{10,18... | collective-permute-start | bytes 589832 | tf_op jit(solution)/shard_map/ppermute | solution.py:446
  104.0 17.6 %collective-permute-start.22 = (bf16[1,6,128,128]{3,2,1,0:T(8,128)(2,1)S(1)}, bf16[1,6,128,128]{3,2,1,0:T(8,128)(2,1)S(1)}, u32[]{:S(2)}, u32[]{:S(2)}) collective-permute-start(bf16[1,6,128,128]{3,2,1,0:T(8,128)(2,1)S(1)} %get-tuple-element.51), channel_id=1, source_target_pairs={{8,24},{12,28},{16,0},{20,4},{9,25},{13,29},{17,1},{21,5},{10,26},... | collective-permute-start | bytes 589832 | tf_op jit(solution)/shard_map/ppermute | solution.py:446
  112.5 4.3 %collective-permute-start.25 = (bf16[1,4,128,128]{3,2,1,0:T(8,128)(2,1)S(1)}, bf16[1,4,128,128]{3,2,1,0:T(8,128)(2,1)S(1)}, u32[]{:S(2)}, u32[]{:S(2)}) collective-permute-start(bf16[1,4,128,128]{3,2,1,0:T(8,128)(2,1)S(1)} %get-tuple-element.53.refs_8_), channel_id=1, source_target_pairs={{8,16},{12,20},{16,8},{20,12},{9,17},{13,21},{17,9},{21,13},{10,18... | collective-permute-start | bytes 393224 | tf_op jit(solution)/shard_map/ppermute | solution.py:446
  113.2 8.4 %collective-permute-start.26 = (bf16[1,4,128,128]{3,2,1,0:T(8,128)(2,1)S(1)}, bf16[1,4,128,128]{3,2,1,0:T(8,128)(2,1)S(1)}, u32[]{:S(2)}, u32[]{:S(2)}) collective-permute-start(bf16[1,4,128,128]{3,2,1,0:T(8,128)(2,1)S(1)} %get-tuple-element.54), channel_id=1, source_target_pairs={{8,24},{12,28},{16,0},{20,4},{9,25},{13,29},{17,1},{21,5},{10,26},... | collective-permute-start | bytes 393224 | tf_op jit(solution)/shard_map/ppermute | solution.py:446
